TPU v7x, 32 devices: a whole 2x2x4 slice. The times are simulated.
32 devices in a mesh: batch: 8 (over y, x, core), head: 4 (over z).
Axes of the slice: x: 2, y: 2, z: 4, core: 2. Of those that a mesh axis runs over, the one named last changes fastest.
Arguments:
- tokens: bfloat16 [8, 1024, 2048], P('batch', 'head'), may hold values from -6 to 6
- z_weight: bfloat16 [2048, 4096], P(None, 'head'), may hold values from -0.125 to 0.125
- x_weight: bfloat16 [2048, 4096], P(None, 'head'), may hold values from -0.125 to 0.125
- bc_weight: bfloat16 [2048, 256], replicated, may hold values from -0.125 to 0.125
- dt_weight: bfloat16 [2048, 64], P(None, 'head'), may hold values from -0.125 to 0.125
- conv_weight: float32 [4, 4096], P(None, 'head'), may hold values from -3 to 3
- conv_bias: float32 [4096], P('head'), may hold values from -3 to 3
- dt_bias: float32 [64], P('head'), may hold values from -4 to -1
- a_log: float32 [64], P('head'), may hold values from -3 to 1
- skip: float32 [4096], P('head'), may hold values from 0.5 to 1.5
- norm_gain: float32 [4096], P('head'), may hold values from 0.25 to 1.75
- pre_gain: float32 [2048], replicated, may hold values from 0.25 to 1.75
- out_weight: bfloat16 [4096, 2048], P('head'), may hold values from -0.1875 to 0.1875
- cotangent: bfloat16 [4, 8, 1024, 2048], P(None, 'batch', 'head'), may hold values from -6 to 6
Outputs:
- outputs: bfloat16 [4, 8, 1024, 2048], P(None, 'batch', 'head')
- tokens_grad: bfloat16 [8, 1024, 2048], P('batch', 'head')
- z_weight_grad: float32 [2048, 4096], P(None, 'head')
- x_weight_grad: float32 [2048, 4096], P(None, 'head')
- state_proj_weight_gradient: float32 [2048, 256], replicated
- dt_weight_grad: float32 [2048, 64], P(None, 'head')
- conv_weight_grad: float32 [4, 4096], P(None, 'head')
- conv_bias_grad: float32 [4096], P('head')
- dt_bias_grad: float32 [64], P('head')
- a_log_grad: float32 [64], P('head')
- skip_grad: float32 [4096], P('head')
- norm_gain_grad: float32 [4096], P('head')
- pre_gain_grad: float32 [2048], replicated
- out_weight_grad: float32 [4096, 2048], P('head')
All inputs are finite; a program needn't handle non-finite values.
Results may differ from a plain program's by a relative error of at most 0.015.
Values may be sent and summed in bfloat16 or wider, within the bound.
A program may use at most 256 MiB of HBM per device.

v0:
```python
import jax
import jax.numpy as jnp
from jax import lax
from jax.sharding import PartitionSpec as P

SPAN = 128


EPSILON = 1e-05
HIGHEST = lax.Precision.HIGHEST


def scan_blocks(act_in, incoming_deltas, decay_rate, b_proj, c_proj, block_len):
    length, head_count, head_size = act_in.shape
    blocks_num = length // block_len
    act_blocks = act_in.reshape(blocks_num, block_len, head_count, head_size)
    deltas = incoming_deltas.reshape(blocks_num, block_len, head_count).transpose(0, 2, 1)
    b_blocks = b_proj.reshape(blocks_num, block_len, -1)
    c_blocks = c_proj.reshape(blocks_num, block_len, -1)
    log_decay = jnp.cumsum(deltas * decay_rate[None, :, None], axis=2)
    log_diff = log_decay[..., :, None] - log_decay[..., None, :]
    causal = jnp.tril(jnp.ones((block_len, block_len), dtype=bool))
    decay_mat = jnp.exp(jnp.where(causal, log_diff, -jnp.inf))
    inner_prod = jnp.einsum("ctn,csn->cts", c_blocks, b_blocks, precision=HIGHEST)
    weights = decay_mat * inner_prod[:, None] * deltas[:, :, None, :]
    within = jnp.einsum("chts,cshp->cthp", weights, act_blocks, precision=HIGHEST)
    tail_scale = jnp.exp(log_decay[..., -1:] - log_decay) * deltas
    scaled = act_blocks * tail_scale.transpose(0, 2, 1)[..., None]
    local_states = jnp.einsum("cshp,csn->chpn", scaled, b_blocks, precision=HIGHEST)
    totals_decay = jnp.exp(log_decay[..., -1])

    def advance(state_now, inputs):
        new_state, factor = inputs
        return (factor[:, None, None] * state_now + new_state, state_now)

    start_state = jnp.zeros((head_count, head_size, b_proj.shape[-1]), act_in.dtype)
    _, before = lax.scan(advance, start_state, (local_states, totals_decay))
    across = jnp.einsum("ctn,chpn->cthp", c_blocks, before, precision=HIGHEST)
    across = across * jnp.exp(log_decay).transpose(0, 2, 1)[..., None]
    return (within + across).reshape(length, head_count, head_size)


def mixer(gate_proj, inner_proj, bc_proj, step_raw, w_conv, b_conv, b_step, log_rate, skip_gain):
    length, channels = inner_proj.shape
    kernel_len = w_conv.shape[0]
    head_count = step_raw.shape[1]
    state_size = bc_proj.shape[1] // 2
    padded = jnp.pad(inner_proj, ((kernel_len - 1, 0), (0, 0)))
    conv_out = b_conv + sum(
        (w_conv[offset] * padded[offset : offset + length] for offset in range(kernel_len))
    )
    active = jax.nn.silu(conv_out)
    step_size = jax.nn.softplus(step_raw + b_step)
    decay_rate = -jnp.exp(log_rate)
    scanned = scan_blocks(
        active.reshape(length, head_count, channels // head_count),
        step_size,
        decay_rate,
        bc_proj[:, :state_size],
        bc_proj[:, state_size:],
        SPAN,
    )
    scanned = scanned.reshape(length, channels) + skip_gain * active
    return scanned * jax.nn.silu(gate_proj)


def local_mix(
    gate_proj, inner_proj, bc_proj, step_raw, w_conv, b_conv, b_step, log_rate, skip_gain
):
    mapped = jax.vmap(mixer, in_axes=(0, 0, 0, 0, None, None, None, None, None))
    return mapped(
        gate_proj, inner_proj, bc_proj, step_raw, w_conv, b_conv, b_step, log_rate, skip_gain
    )


def per_device(
    tokens,
    z_weight,
    x_weight,
    bc_weight,
    dt_weight,
    conv_weight,
    conv_bias,
    dt_bias,
    a_log,
    skip,
    norm_gain,
    pre_gain,
    out_weight,
    cotangent,
):
    head_group = lax.axis_size("head")
    seq_count, own_len, model_dim = tokens.shape
    local_dim = z_weight.shape[1]
    tokens_f = tokens.astype(jnp.float32)
    recip_in = lax.rsqrt(jnp.mean(tokens_f * tokens_f, axis=-1, keepdims=True) + EPSILON)
    normed_own = (tokens_f * recip_in * pre_gain).astype(jnp.bfloat16)
    gathered = lax.all_gather(normed_own, "head", axis=1, tiled=True)
    full_len = gathered.shape[1]
    flat_rows = gathered.reshape(seq_count * full_len, model_dim)
    gate_proj = jnp.dot(flat_rows, z_weight, preferred_element_type=jnp.float32)
    inner_proj = jnp.dot(flat_rows, x_weight, preferred_element_type=jnp.float32)
    step_raw = jnp.dot(flat_rows, dt_weight, preferred_element_type=jnp.float32)
    bc_proj = jnp.dot(flat_rows, bc_weight, preferred_element_type=jnp.float32)

    def as_sequences(values):
        return values.reshape(seq_count, full_len, values.shape[-1])

    gated, pullback = jax.vjp(
        local_mix,
        as_sequences(gate_proj),
        as_sequences(inner_proj),
        as_sequences(bc_proj),
        as_sequences(step_raw),
        conv_weight,
        conv_bias,
        dt_bias,
        a_log,
        skip,
    )
    width_cols = [local_dim * 2**nested_widths // 8 for nested_widths in range(4)]
    squares = jnp.stack(
        [jnp.sum(gated[..., :prefix_cols] ** 2, axis=-1) for prefix_cols in width_cols]
    )
    totals = lax.psum(squares, "head")
    recips = [
        lax.rsqrt(totals[nested_widths] / (width_cols[nested_widths] * head_group) + EPSILON)[
            ..., None
        ]
        for nested_widths in range(4)
    ]
    normalized_rows = [
        (
            gated[..., : width_cols[nested_widths]]
            * recips[nested_widths]
            * norm_gain[: width_cols[nested_widths]]
        ).astype(jnp.bfloat16)
        for nested_widths in range(4)
    ]
    partial_terms = jnp.stack(
        [
            jnp.einsum(
                "ira,at->irt",
                normalized_rows[nested_widths],
                out_weight[: width_cols[nested_widths]],
                preferred_element_type=jnp.float32,
            )
            for nested_widths in range(4)
        ]
    )
    branch = lax.psum_scatter(
        partial_terms.astype(jnp.bfloat16), "head", scatter_dimension=2, tiled=True
    ).astype(jnp.float32)
    outputs = (tokens_f[None] + branch).astype(jnp.bfloat16)
    cotangent_everything = lax.all_gather(cotangent, "head", axis=2, tiled=True)
    out_grad = jnp.zeros((local_dim, model_dim), jnp.float32)
    d_normed = []
    product_terms = []
    for nested_widths in range(4):
        prefix_cols = width_cols[nested_widths]
        d_norm = jnp.einsum(
            "gum,rm->gur",
            cotangent_everything[nested_widths],
            out_weight[:prefix_cols],
            preferred_element_type=jnp.float32,
        )
        out_grad = out_grad.at[:prefix_cols].add(
            jnp.einsum(
                "jnt,jnh->th",
                normalized_rows[nested_widths],
                cotangent_everything[nested_widths],
                preferred_element_type=jnp.float32,
            )
        )
        d_normed.append(d_norm)
        product_terms.append(
            jnp.sum(gated[..., :prefix_cols] * norm_gain[:prefix_cols] * d_norm, axis=-1)
        )
    dot_totals = lax.psum(jnp.stack(product_terms), "head")
    d_gated = jnp.zeros_like(gated)
    gain_grad = jnp.zeros((local_dim,), jnp.float32)
    for nested_widths in range(4):
        prefix_cols = width_cols[nested_widths]
        prefix = gated[..., :prefix_cols]
        recip = recips[nested_widths]
        d_gated = d_gated.at[..., :prefix_cols].add(
            recip * norm_gain[:prefix_cols] * d_normed[nested_widths]
            - prefix * recip**3 * dot_totals[nested_widths][..., None] / (prefix_cols * head_group)
        )
        gain_grad = gain_grad.at[:prefix_cols].add(
            jnp.sum(prefix * recip * d_normed[nested_widths], axis=(0, 1))
        )
    (
        d_gate3,
        d_inner3,
        d_bc3,
        d_step3,
        conv_w_grad,
        conv_b_grad,
        dt_bias_grad,
        a_log_grad,
        skip_grad,
    ) = pullback(d_gated)
    d_gate = d_gate3.reshape(-1, local_dim).astype(jnp.bfloat16)
    d_inner = d_inner3.reshape(-1, local_dim).astype(jnp.bfloat16)
    d_step = d_step3.reshape(-1, d_step3.shape[-1]).astype(jnp.bfloat16)
    d_bc = d_bc3.reshape(-1, d_bc3.shape[-1])
    d_rows = jnp.einsum("rc,dc->rd", d_gate, z_weight, preferred_element_type=jnp.float32)
    d_rows = d_rows + jnp.einsum("rc,dc->rd", d_inner, x_weight, preferred_element_type=jnp.float32)
    d_rows = d_rows + jnp.einsum("rc,dc->rd", d_step, dt_weight, preferred_element_type=jnp.float32)
    d_rows = d_rows + jnp.einsum(
        "rc,dc->rd", d_bc, bc_weight.astype(jnp.float32), precision=HIGHEST
    )
    z_grad = jnp.einsum("rd,rc->dc", flat_rows, d_gate, preferred_element_type=jnp.float32)
    x_grad = jnp.einsum("rd,rc->dc", flat_rows, d_inner, preferred_element_type=jnp.float32)
    dt_grad = jnp.einsum("rd,rc->dc", flat_rows, d_step, preferred_element_type=jnp.float32)
    bc_grad = jnp.einsum("rd,rc->dc", flat_rows.astype(jnp.float32), d_bc, precision=HIGHEST)
    d_own = lax.psum_scatter(
        d_rows.reshape(seq_count, full_len, model_dim).astype(jnp.bfloat16),
        "head",
        scatter_dimension=1,
        tiled=True,
    ).astype(jnp.float32)
    inner_sum = jnp.mean(tokens_f * pre_gain * d_own, axis=-1, keepdims=True)
    tokens_grad = jnp.sum(cotangent.astype(jnp.float32), axis=0) + pre_gain * recip_in * d_own
    tokens_grad = (tokens_grad - tokens_f * recip_in**3 * inner_sum).astype(jnp.bfloat16)
    prenorm_gradient = jnp.sum(tokens_f * recip_in * d_own, axis=(0, 1))
    bc_grad, prenorm_gradient = (
        lax.psum(bc_grad.astype(jnp.bfloat16), "head").astype(jnp.float32),
        lax.psum(prenorm_gradient.astype(jnp.bfloat16), "head").astype(jnp.float32),
    )
    reduced = (
        lax.psum_scatter(z_grad, "batch", scatter_dimension=0, tiled=True),
        lax.psum_scatter(x_grad, "batch", scatter_dimension=0, tiled=True),
        lax.psum_scatter(dt_grad, "batch", scatter_dimension=0, tiled=True),
        lax.psum_scatter(bc_grad, "batch", scatter_dimension=0, tiled=True),
        lax.psum_scatter(out_grad, "batch", scatter_dimension=0, tiled=True),
        lax.psum_scatter(prenorm_gradient, "batch", scatter_dimension=0, tiled=True),
        lax.psum_scatter(conv_w_grad.T, "batch", scatter_dimension=0, tiled=True),
        lax.psum_scatter(conv_b_grad, "batch", scatter_dimension=0, tiled=True),
        lax.psum_scatter(skip_grad, "batch", scatter_dimension=0, tiled=True),
        lax.psum_scatter(gain_grad, "batch", scatter_dimension=0, tiled=True),
    )
    joined = (
        lax.all_gather(reduced[0].astype(jnp.bfloat16), "batch", axis=0, tiled=True).astype(
            jnp.float32
        ),
        lax.all_gather(reduced[1].astype(jnp.bfloat16), "batch", axis=0, tiled=True).astype(
            jnp.float32
        ),
        lax.all_gather(reduced[2].astype(jnp.bfloat16), "batch", axis=0, tiled=True).astype(
            jnp.float32
        ),
        lax.all_gather(reduced[3].astype(jnp.bfloat16), "batch", axis=0, tiled=True).astype(
            jnp.float32
        ),
        lax.all_gather(reduced[4].astype(jnp.bfloat16), "batch", axis=0, tiled=True).astype(
            jnp.float32
        ),
        lax.all_gather(reduced[5].astype(jnp.bfloat16), "batch", axis=0, tiled=True).astype(
            jnp.float32
        ),
        lax.all_gather(reduced[6].astype(jnp.bfloat16), "batch", axis=0, tiled=True).astype(
            jnp.float32
        ),
        lax.all_gather(reduced[7].astype(jnp.bfloat16), "batch", axis=0, tiled=True).astype(
            jnp.float32
        ),
        lax.all_gather(reduced[8].astype(jnp.bfloat16), "batch", axis=0, tiled=True).astype(
            jnp.float32
        ),
        lax.all_gather(reduced[9].astype(jnp.bfloat16), "batch", axis=0, tiled=True).astype(
            jnp.float32
        ),
    )
    dt_bias_grad, a_log_grad = lax.psum((dt_bias_grad, a_log_grad), "batch")
    return (
        outputs,
        tokens_grad,
        joined[0],
        joined[1],
        joined[3],
        joined[2],
        joined[6].T,
        joined[7],
        dt_bias_grad,
        a_log_grad,
        joined[8],
        joined[9],
        joined[5],
        joined[4],
    )


def solution(mesh):
    placed = (
        P("batch", "head", None),
        P(None, "head"),
        P(None, "head"),
        P(),
        P(None, "head"),
        P(None, "head"),
        P("head"),
        P("head"),
        P("head"),
        P("head"),
        P("head"),
        P(),
        P("head", None),
        P(None, "batch", "head", None),
    )
    return jax.shard_map(
        per_device,
        mesh=mesh,
        in_specs=placed,
        out_specs=(
            P(None, "batch", "head", None),
            P("batch", "head", None),
            P(None, "head"),
            P(None, "head"),
            P(),
            P(None, "head"),
            P(None, "head"),
            P("head"),
            P("head"),
            P("head"),
            P("head"),
            P("head"),
            P(),
            P("head", None),
        ),
        check_vma=False,
    )
```

profile of v0, /device:TPU:0, one launch (start us, length us, event | category | flops | bytes accessed | tf_op | source)
XLA Modules:
  0.0 1453.6 jit_solution(13073609465849552262)
XLA Ops:
  13.6 82.6 %all-gather.11.cloned.1.call-done = bf16[1,1024,2048]{2,1,0:T(8,128)(2,1)} async-done(((bf16[1,256,2048]{2,1,0:T(8,128)(2,1)}), bf16[1,1024,2048]{2,1,0:T(8,128)(2,1)}) %all-gather.11.cloned.1.call-update) | async-done | bytes 4194320 | tf_op jit(solution)/shard_map/all_gather | solution.py:98
  137.1 20.1 %while.49 = (s32[]{:T(128)}, f32[1,16,64,128]{3,2,1,0:T(8,128)S(1)}, f32[8,1,16,64,128]{4,3,2,1,0:T(8,128)}, f32[8,1,16,1,1]{2,4,3,1,0:T(1,128)}, f32[8,1,16]{2,...) while((s32[]{:T(128)}, f32[1,16,64,128]{3,2,1,0:T(8,128)S(1)}, ...), condition=%wide.region_3.4_spmd.clone, body=%wide.region_2.3_spmd.clone.sunk | while | flops 524291 | bytes 2623336 | solution.py:37
  163.0 17.6 %bitcast_add_fusion.3 = f32[1,8,128,16,64]{2,4,3,1,0:T(8,128)S(1)} fusion(f32[8,128,16,64]{1,3,2,0:T(8,128)S(1)} %fusion.29, f32[8,128,16]{1,2,0:T(8,128)S(1)} %get-tuple-element.518, f32[8,16,128]{2,1,0:T(8,128)S(1)} %bitcast.489, f32[8,128,128]{2,1,0:T(8,128)S(1)} %copy-done.32, f32[8,16,128]{2,1,0:T(8,128)S(1)} %bitcast.466, ...), kind=kOutput, calls=%fused_computation.45 | convolution fusion | flops 1621098496 | bytes 13320192 | tf_op jit(solution)/shard_map/jvp(vmap(chts,cshp->cthp))/dot_general | solution.py:26
  185.8 11.0 copy.79
  196.8 13.1 multiply_reduce_fusion.8
  212.1 22.0 %psum.42 = f32[4,1,1024]{2,1,0:T(1,128)S(1)} all-reduce(f32[4,1,1024]{2,1,0:T(1,128)S(1)} %pad_maximum_fusion.1), channel_id=1, replica_groups=mesh['batch'=8,'head'=4] {'head'}, use_global_device_ids=true, to_apply=%region_8.9 | all-reduce | flops 4096 | bytes 32768 | tf_op jit(solution)/shard_map/psum | solution.py:125
  234.2 149.4 %all-gather.13.cloned.1.call-done = bf16[4,1,1024,2048]{3,2,1,0:T(8,128)(2,1)} async-done(((bf16[4,1,256,2048]{3,2,1,0:T(8,128)(2,1)}), bf16[4,1,1024,2048]{3,2,1,0:T(8,128)(2,1)}) %all-gather.13.cloned.1.call-update) | async-done | bytes 16777232 | tf_op jit(solution)/shard_map/all_gather | solution.py:155
  383.7 12.1 fusion.26
  407.1 15.6 %psum.43 = f32[4,1,1024]{2,1,0:T(1,128)S(1)} all-reduce(f32[4,1,1024]{2,1,0:T(1,128)S(1)} %pad_maximum_fusion.2), channel_id=1, replica_groups=mesh['batch'=8,'head'=4] {'head'}, use_global_device_ids=true, to_apply=%region_15.16 | all-reduce | flops 4096 | bytes 32768 | tf_op jit(solution)/shard_map/psum | solution.py:179
  446.1 11.0 copy.83
  480.2 19.6 %fusion.10 = (f32[8,16,128]{2,1,0:T(8,128)S(1)}, f32[8,16,128]{2,1,0:T(8,128)S(1)}, f32[8,16,128]{2,1,0:T(8,128)S(1)}, f32[8,128,128]{2,1,0:T(8,128)S(1)}) fusion(f32[8,16,128]{2,1,0:T(8,128)S(1)} %bitcast.490, f32[8,128,128]{2,1,0:T(8,128)S(1)} %copy-done.33, f32[8,16,128]{2,1,0:T(8,128)S(1)} %bitcast.467, pred[128,128]{1,0:T(8,128)(4,1)S(1)} %copy-done.57, ...), kind=kOutput, calls=%fused_computation.27 | convolution fusion | flops 1637695488 | bytes 9781248 | tf_op jit(solution)/shard_map/transpose(jvp(vmap(chts,cshp->cthp)))/dot_general | solution.py:26
  504.8 23.8 %while.50 = (s32[]{:T(128)}, f32[1,16,64,128]{3,2,1,0:T(8,128)S(1)}, f32[8,1,16,64,128]{4,3,2,1,0:T(8,128)}, f32[8,1,16]{2,1,0:T(1,128)S(1)}, f32[8,1,16,64,128]...) while((s32[]{:T(128)}, ...), condition=%wide.region_18.19_spmd.clone, body=%wide.region_16.18_spmd.clone.sunk | while | flops 786420 | bytes 3147148 | solution.py:37
  528.6 10.8 fusion.134
  558.3 37.5 %all-reduce.23.cloned.1.call-done = bf16[2048,256]{1,0:T(8,128)(2,1)} async-done(((bf16[2048,256]{1,0:T(8,128)(2,1)}), bf16[2048,256]{1,0:T(8,128)(2,1)}) %all-reduce.23.cloned.1.call-update) | async-done | bytes 1048592 | tf_op jit(solution)/shard_map/psum | solution.py:229
  604.6 10.8 convolution_add_fusion
  615.5 10.9 copy.87
  650.1 11.1 copy.86
  661.3 12.4 multiply_reduce_fusion.5
  695.7 10.8 fusion.38
  728.6 11.1 fusion.210
  740.2 10.8 fusion.105
  786.8 73.1 %reduce-scatter.15.cloned.1.call-done = f32[256,1024]{1,0:T(8,128)} async-done(((f32[2048,1024]{1,0:T(8,128)}), f32[256,1024]{1,0:T(8,128)}) %reduce-scatter.15.cloned.1.call-update) | async-done | bytes 1048592 | tf_op jit(solution)/shard_map/reduce_scatter | solution.py:233
  870.2 27.6 %reduce-scatter.25.cloned.1.call-done = f32[128,4]{1,0:T(8,128)} async-done(((f32[1024,4]{1,0:T(8,128)}), f32[128,4]{1,0:T(8,128)}) %reduce-scatter.25.cloned.1.call-update) | async-done | bytes 2064
  908.2 26.9 %reduce-scatter.21.cloned.1.call-done = f32[256,16]{0,1:T(8,128)} async-done(((f32[2048,16]{0,1:T(8,128)}), f32[256,16]{0,1:T(8,128)}) %reduce-scatter.21.cloned.1.call-update) | async-done | bytes 16400 | tf_op jit(solution)/shard_map/reduce_scatter | solution.py:235
  945.5 14.9 %all-gather.19.cloned.1.call-done = bf16[2048,256]{1,0:T(8,128)(2,1)} async-done(((bf16[256,256]{1,0:T(8,128)(2,1)}), bf16[2048,256]{1,0:T(8,128)(2,1)}) %all-gather.19.cloned.1.call-update) | async-done | bytes 1048592 | tf_op jit(solution)/shard_map/all_gather | solution.py:254
  963.1 77.0 %reduce-scatter.13.cloned.1.call-done = bf16[1,256,2048]{2,1,0:T(8,128)(2,1)} async-done(((bf16[1,1024,2048]{2,1,0:T(8,128)(2,1)}), bf16[1,256,2048]{2,1,0:T(8,128)(2,1)}) %reduce-scatter.13.cloned.1.call-update) | async-done | bytes 1048592 | tf_op jit(solution)/shard_map/reduce_scatter | solution.py:218
  1042.3 11.1 psum.47
  1053.4 23.0 %all-reduce.20 = (bf16[1024]{0:T(1024)(128)(2,1)S(1)}, f32[16]{0:T(128)}, f32[16]{0:T(128)}, bf16[1024]{0:T(1024)(128)(2,1)S(1)}, bf16[1024]{0:T(1024)(128)(2,1)S(1)}, /*index=5*/bf16[2048]{0:T(1024)(128)(2,1)S(1)}) all-reduce(f32[1024]{0:T(1024)S(1)} %get-tuple-element.460, ...), channel_id=9, replica_groups=mesh['batch'=8,'head'=4] {'batch'}, use_global_device_ids=true, to_apply=%region_40.41.clone | all-reduce | flops 5152 | bytes 26880
  1116.1 207.2 %reduce-scatter.11.cloned.1.call-done = bf16[4,1,256,2048]{3,2,1,0:T(8,128)(2,1)} async-done(((bf16[4,1,1024,2048]{3,2,1,0:T(8,128)(2,1)}), bf16[4,1,256,2048]{3,2,1,0:T(8,128)(2,1)}) %reduce-scatter.11.cloned.1.call-update) | async-done | bytes 4194320 | tf_op jit(solution)/shard_map/reduce_scatter | solution.py:151
  1329.5 33.1 %all-gather.21.cloned.1.call-done = bf16[1024,2048]{1,0:T(8,128)(2,1)} async-done(((bf16[128,2048]{1,0:T(8,128)(2,1)}), bf16[1024,2048]{1,0:T(8,128)(2,1)}) %all-gather.21.cloned.1.call-update) | async-done | bytes 4194320 | tf_op jit(solution)/shard_map/all_gather | solution.py:257
  1369.3 31.8 %all-gather.17.cloned.1.call-done = bf16[2048,1024]{1,0:T(8,128)(2,1)} async-done(((bf16[256,1024]{1,0:T(8,128)(2,1)}), bf16[2048,1024]{1,0:T(8,128)(2,1)}) %all-gather.17.cloned.1.call-update) | async-done | bytes 4194320 | tf_op jit(solution)/shard_map/all_gather | solution.py:248
  1407.8 32.4 %all-gather.15.cloned.1.call-done = bf16[2048,1024]{1,0:T(8,128)(2,1)} async-done(((bf16[256,1024]{1,0:T(8,128)(2,1)}), bf16[2048,1024]{1,0:T(8,128)(2,1)}) %all-gather.15.cloned.1.call-update) | async-done | bytes 4194320 | tf_op jit(solution)/shard_map/all_gather | solution.py:245
  (378 shorter events, 398.1 us)
Async XLA Ops:
  7.2 118.0 %copy-start = (bf16[2048,256]{1,0:T(8,128)(2,1)S(1)}, bf16[2048,256]{1,0:T(8,128)(2,1)}, u32[]{:S(2)}) copy-start(bf16[2048,256]{1,0:T(8,128)(2,1)} %param.51) | copy-start | bytes 3145732
  7.2 89.0 %copy-start.35 = (bf16[2048,16]{0,1:T(8,128)(2,1)S(1)}, bf16[2048,16]{0,1:T(8,128)(2,1)}, u32[]{:S(2)}) copy-start(bf16[2048,16]{0,1:T(8,128)(2,1)} %param.52) | copy-start | bytes 196612
  7.2 89.0 %copy-start.67 = (f32[16]{0:T(128)S(1)}, f32[16]{0:T(128)}, u32[]{:S(2)}) copy-start(f32[16]{0:T(128)} %param.55) | copy-start | bytes 196
  7.2 89.0 %all-gather.11.cloned.1.call-start = ((), (), s32[]{:S(2)}) async-start(), calls=%async_computation.8 | async-start | bytes 5242880 | tf_op jit(solution)/shard_map/all_gather | solution.py:98
  12.6 371.1 %all-gather.13.cloned.1.call-start = ((), (), s32[]{:S(2)}) async-start(), calls=%async_computation.10 | async-start | bytes 20971520 | tf_op jit(solution)/shard_map/all_gather | solution.py:155
  13.3 582.5 %all-reduce.23.cloned.1.call-start = ((), (), s32[]{:S(2)}) async-start(), calls=%async_computation.16 | async-start | bytes 2097152 | tf_op jit(solution)/shard_map/psum | solution.py:229
  13.4 409.3 %copy-start.61 = (f32[128]{0:T(128)}, f32[128]{0:T(128)S(1)}, u32[]{:S(2)}) copy-start(f32[128]{0:T(128)S(1)} %slice.336) | copy-start | bytes 1540
  13.5 149.4 %copy-start.56 = (pred[128,128]{1,0:T(8,128)(4,1)}, pred[128,128]{1,0:T(8,128)(4,1)S(1)}, u32[]{:S(2)}) copy-start(pred[128,128]{1,0:T(8,128)(4,1)S(1)} %iota_compare_fusion) | copy-start | bytes 49156
  13.5 86.8 %copy-start.68 = (f32[16]{0:T(128)}, f32[16]{0:T(128)S(1)}, u32[]{:S(2)}) copy-start(f32[16]{0:T(128)S(1)} %exponential_negate_fusion) | copy-start | bytes 196
  13.6 97.9 %copy-start.45 = (f32[1,1024]{1,0:T(1,128)}, f32[1,1024]{1,0:T(1,128)S(1)}, u32[]{:S(2)}) copy-start(f32[1,1024]{1,0:T(1,128)S(1)} %get-tuple-element.528) | copy-start | bytes 12292
  13.6 97.9 %copy-start.47 = (f32[1,1024]{1,0:T(1,128)}, f32[1,1024]{1,0:T(1,128)S(1)}, u32[]{:S(2)}) copy-start(f32[1,1024]{1,0:T(1,128)S(1)} %get-tuple-element.529) | copy-start | bytes 12292
  13.6 97.9 %copy-start.49 = (f32[1,1024]{1,0:T(1,128)}, f32[1,1024]{1,0:T(1,128)S(1)}, u32[]{:S(2)}) copy-start(f32[1,1024]{1,0:T(1,128)S(1)} %get-tuple-element.530) | copy-start | bytes 12292
  13.6 97.9 %copy-start.51 = (f32[1,1024]{1,0:T(1,128)}, f32[1,1024]{1,0:T(1,128)S(1)}, u32[]{:S(2)}) copy-start(f32[1,1024]{1,0:T(1,128)S(1)} %get-tuple-element.531) | copy-start | bytes 12292
  100.2 62.7 %copy-start.42 = (f32[1,8,128,16]{2,3,1,0:T(8,128)}, f32[1,8,128,16]{2,3,1,0:T(8,128)S(1)}, u32[]{:S(2)}) copy-start(f32[1,8,128,16]{2,3,1,0:T(8,128)S(1)} %copy.147) | copy-start | bytes 196612
  545.4 194.3 %reduce-scatter.19.cloned.1.call-start = ((), (), s32[]{:S(2)}) async-start(), calls=%async_computation.17 | async-start | bytes 1179648 | tf_op jit(solution)/shard_map/reduce_scatter | solution.py:236
  595.8 186.6 %reduce-scatter.23.cloned.1.call-start = ((), (), s32[]{:S(2)}) async-start(), calls=%async_computation.20 | async-start | bytes 9437184 | tf_op jit(solution)/shard_map/reduce_scatter | solution.py:237
  615.5 169.2 %reduce-scatter.17.cloned.1.call-start = ((), (), s32[]{:S(2)}) async-start(), calls=%async_computation.14 | async-start | bytes 9437184 | tf_op jit(solution)/shard_map/reduce_scatter | solution.py:234
  695.4 164.6 %reduce-scatter.15.cloned.1.call-start = ((), (), s32[]{:S(2)}) async-start(), calls=%async_computation.12 | async-start | bytes 9437184 | tf_op jit(solution)/shard_map/reduce_scatter | solution.py:233
  706.5 191.3 %reduce-scatter.25.cloned.1.call-start = ((), (), s32[]{:S(2)}) async-start(), calls=%async_computation.22 | async-start | bytes 589824
  724.2 210.9 %reduce-scatter.21.cloned.1.call-start = ((), (), s32[]{:S(2)}) async-start(), calls=%async_computation.19 | async-start | bytes 147456 | tf_op jit(solution)/shard_map/reduce_scatter | solution.py:235
  728.6 231.8 %all-gather.19.cloned.1.call-start = ((), (), s32[]{:S(2)}) async-start(), calls=%async_computation.18 | async-start | bytes 1179648 | tf_op jit(solution)/shard_map/all_gather | solution.py:254
  739.7 300.3 %reduce-scatter.13.cloned.1.call-start = ((), (), s32[]{:S(2)}) async-start(), calls=%async_computation.11 | async-start | bytes 5242880 | tf_op jit(solution)/shard_map/reduce_scatter | solution.py:218
  762.0 561.3 %reduce-scatter.11.cloned.1.call-start = ((), (), s32[]{:S(2)}) async-start(), calls=%async_computation.9 | async-start | bytes 20971520 | tf_op jit(solution)/shard_map/reduce_scatter | solution.py:151
  782.3 79.8 %copy-start.75 = (u32[32]{0:T(128)S(1)}, u32[32]{0:T(128)}, u32[]{:S(2)}) copy-start(u32[32]{0:T(128)} %constant.457) | copy-start | bytes 388
  782.4 580.3 %all-gather.21.cloned.1.call-start = ((), (), s32[]{:S(2)}) async-start(), calls=%async_computation.21 | async-start | bytes 4718592 | tf_op jit(solution)/shard_map/all_gather | solution.py:257
  784.6 616.6 %all-gather.17.cloned.1.call-start = ((), (), s32[]{:S(2)}) async-start(), calls=%async_computation.15 | async-start | bytes 4718592 | tf_op jit(solution)/shard_map/all_gather | solution.py:248
  786.8 81.8 %copy-start.10 = (bf16[1,256,2048]{2,1,0:T(8,128)(2,1)S(1)}, bf16[1,256,2048]{2,1,0:T(8,128)(2,1)}, u32[]{:S(2)}) copy-start(bf16[1,256,2048]{2,1,0:T(8,128)(2,1)} %param.48) | copy-start | bytes 3145732
  786.8 653.4 %all-gather.15.cloned.1.call-start = ((), (), s32[]{:S(2)}) async-start(), calls=%async_computation.13 | async-start | bytes 4718592 | tf_op jit(solution)/shard_map/all_gather | solution.py:245
  868.6 171.5 %copy-start.41 = (f32[2048]{0:T(1024)S(1)}, f32[2048]{0:T(1024)}, u32[]{:S(2)}) copy-start(f32[2048]{0:T(1024)} %param.59) | copy-start | bytes 24580
  868.6 171.5 %copy-start.59 = (f32[256]{0:T(256)S(1)}, f32[256]{0:T(256)}, u32[]{:S(2)}) copy-start(f32[256]{0:T(256)} %copy-done.58) | copy-start | bytes 3076
  868.6 184.8 %copy-start.54 = (f32[1024]{0:T(1024)S(1)}, f32[1024]{0:T(1024)}, u32[]{:S(2)}) copy-start(f32[1024]{0:T(1024)} %get-tuple-element.498) | copy-start | bytes 12292
  868.6 243.9 %copy-start.65 = (f32[256]{0:T(256)S(1)}, f32[256]{0:T(256)}, u32[]{:S(2)}) copy-start(f32[256]{0:T(256)} %get-tuple-element.532) | copy-start | bytes 3076
  (59 other events, 443.0 us)
Sparse Core Ops, SparseCore 0:
  12.7 83.4 all-gather.10
  97.8 285.8 all-gather.12
  545.5 50.2 all-reduce.22
  599.2 35.4 reduce-scatter.18
  638.3 71.2 reduce-scatter.22
  712.9 71.3 reduce-scatter.16
  788.7 71.2 reduce-scatter.14
  863.6 34.1 reduce-scatter.24
  901.7 33.3 reduce-scatter.20
  936.8 23.5 all-gather.18
  963.2 76.7 reduce-scatter.12
  1042.4 280.8 reduce-scatter.10
  1325.2 37.4 all-gather.20
  1364.4 36.7 all-gather.16
  1403.4 36.7 all-gather.14
where the time goes:
time: 1470 us; the launch traced here: 1450 us
  waiting for transfers between devices  795 us (54%)
  matrix products  250 us (17%)
  other arithmetic  160 us (11%)
  blocking collectives  123 us (8%)
  local copies, waits for them, and re-layouts  108 us (7%)
  between operations  16.7 us (1%)
    reduce_scatter x1, waiting for transfers between devices, per_device(): lax.psum_scatter(partial_terms.astype(jnp.bfloat16), 'head', scatter_dime...  207 us
    all_gather x1, waiting for transfers between devices, per_device(): cotangent_everything = lax.all_gather(cotangent, 'head', axis=2, tiled=True)  149 us
    all_gather x1, waiting for transfers between devices, per_device(): gathered = lax.all_gather(normed_own, 'head', axis=1, tiled=True)  82.6 us
    reduce_scatter x1, waiting for transfers between devices, per_device(): lax.psum_scatter(d_rows.reshape(seq_count, full_len, model_dim).astype(jn...  77 us
    reduce_scatter x1, waiting for transfers between devices, per_device(): lax.psum_scatter(z_grad, 'batch', scatter_dimension=0, tiled=True)  73.1 us
    dot_general x3, matrix products, scan_blocks(): jnp.einsum('chts,cshp->cthp', weights, act_blocks, precision=HIGHEST)  47.2 us
    psum x1, waiting for transfers between devices, per_device(): lax.psum(bc_grad.astype(jnp.bfloat16), 'head').astype(jnp.float32)  37.5 us
    all_gather x1, waiting for transfers between devices, per_device(): lax.all_gather(reduced[4].astype(jnp.bfloat16), 'batch', axis=0, tiled=True)  33.1 us
  transfers between devices with their start and end apart: 15, of which 12 were waited for; matrix products, arithmetic and copies ran while one was open for 25% of the time, Pallas kernels for 0%

commit v1 on v0

v1 whole, which is shorter than its diff:
```python
import functools
import itertools

import jax
import jax.numpy as jnp
from jax import lax
from jax.experimental import pallas as pl
from jax.experimental.pallas import tpu as pltpu
from jax.sharding import PartitionSpec as P

SPAN = 128
ROWS = 256
EPSILON = 1e-05
BF16 = jnp.bfloat16
F32 = jnp.float32
HIGHEST = lax.Precision.HIGHEST
VMEM_BYTES = 60 * 1024 * 1024


def mm(a, b):
    return lax.dot_general(a, b, (((1,), (0,)), ((), ())), preferred_element_type=F32)


def mm_nt(a, b):
    return lax.dot_general(a, b, (((1,), (1,)), ((), ())), preferred_element_type=F32)


def mm_tn(a, b):
    return lax.dot_general(a, b, (((0,), (0,)), ((), ())), preferred_element_type=F32)


def mm_exact(a, b):
    return lax.dot_general(
        a, b, (((1,), (0,)), ((), ())), preferred_element_type=F32, precision=HIGHEST
    )


def lower_mask(shape):
    return lax.broadcasted_iota(jnp.int32, shape, 0) >= lax.broadcasted_iota(jnp.int32, shape, 1)


def softplus(v):
    return jnp.maximum(v, 0.0) + jnp.log1p(jnp.exp(-jnp.abs(v)))


def sigmoid(v):
    return 1.0 / (1.0 + jnp.exp(-v))


def pair_columns(values, pair, left):
    shape = (SPAN, 128)
    one = jnp.broadcast_to(values[:, 2 * pair : 2 * pair + 1], shape)
    two = jnp.broadcast_to(values[:, 2 * pair + 1 : 2 * pair + 2], shape)
    return one, two, jnp.where(left, one, two)


def forward_kernel(
    x_ref, zw_ref, xw_ref, bcw_ref, dtw_ref, convw_ref, convb_ref, dtb_ref, alog_ref, skip_ref,
    gated_ref, gate_ref, scan_ref, conv_ref, inner_ref, bc_ref, step_ref, prev_ref,
    state, ext, tails,
):
    rows_num, channels = gate_ref.shape
    n = state.shape[0]

    @pl.when(pl.program_id(0) == 0)
    def _():
        state[...] = jnp.zeros_like(state)
        ext[0:8, :] = jnp.zeros((8, channels), F32)

    x = x_ref[...]
    gate_ref[...] = mm(x, zw_ref[...])
    ext[8:, :] = mm(x, xw_ref[...])
    bc_ref[...] = mm(x, bcw_ref[...])
    step_ref[...] = mm(x, dtw_ref[...])
    conv = convb_ref[...] + sum(
        convw_ref[k : k + 1, :] * ext[5 + k : 5 + k + rows_num, :] for k in range(4)
    )
    conv_ref[...] = conv
    inner_ref[...] = ext[8:, :]
    ext[0:8, :] = ext[rows_num : rows_num + 8, :]
    rate = -jnp.exp(alog_ref[...])
    lower = lower_mask((SPAN, SPAN))
    lower_f = lower.astype(F32)
    left = lax.broadcasted_iota(jnp.int32, (SPAN, 128), 1) < 64

    def block(at, carry):
        rows = pl.ds(pl.multiple_of(at * SPAN, SPAN), SPAN)
        delta = softplus(step_ref[rows, :] + dtb_ref[...])
        cum = mm_exact(lower_f, delta * rate)
        cum_t = cum.T
        b_val = bc_ref[rows, :n].astype(BF16)
        c_val = bc_ref[rows, n:].astype(BF16)
        inner = jnp.where(lower, mm_nt(c_val, b_val), 0.0)
        before = state[...].astype(BF16)
        prev_ref[at] = before
        across = mm(c_val, before)
        for pair in range(channels // 128):
            cols = slice(pair * 128, pair * 128 + 128)
            c0, c1, ce = pair_columns(cum, pair, left)
            _, _, de = pair_columns(delta, pair, left)
            tot = ce[SPAN - 1 : SPAN, :]
            conv_p = conv_ref[rows, cols]
            act = conv_p * sigmoid(conv_p)
            u = act * de
            tails[:, cols] = (u * jnp.exp(tot - ce)).astype(BF16)
            u0 = jnp.where(left, u, 0.0).astype(BF16)
            u1 = jnp.where(left, 0.0, u).astype(BF16)
            p0 = (jnp.exp(jnp.minimum(c0 - cum_t[2 * pair : 2 * pair + 1, :], 0.0)) * inner).astype(BF16)
            p1 = (jnp.exp(jnp.minimum(c1 - cum_t[2 * pair + 1 : 2 * pair + 2, :], 0.0)) * inner).astype(BF16)
            within = mm(jnp.concatenate([p0, p1], axis=1), jnp.concatenate([u0, u1], axis=0))
            y = within + across[:, cols] * jnp.exp(ce) + skip_ref[:, cols] * act
            scan_ref[rows, cols] = y
            gate = gate_ref[rows, cols]
            gated_ref[rows, cols] = (y * gate * sigmoid(gate)).astype(BF16)
            state[:, cols] = state[:, cols] * jnp.exp(tot)
        state[...] += mm(bc_ref[rows, :n].T.astype(BF16), tails[...])
        return carry

    lax.fori_loop(0, rows_num // SPAN, block, 0)


def forward_call(x, zw, xw, bcw, dtw, convw, convb, dtb, alog, skip):
    length, model = x.shape
    channels = zw.shape[1]
    n = bcw.shape[1] // 2
    steps = length // ROWS
    fixed = lambda a: pl.BlockSpec(a.shape, lambda i: (0,) * a.ndim)
    rows = lambda w: pl.BlockSpec((ROWS, w), lambda i: (i, 0))
    sub = ROWS // SPAN
    shapes = (
        (channels, BF16), (channels, F32), (channels, F32), (channels, F32), (channels, F32),
        (2 * n, F32), (dtw.shape[1], F32),
    )
    return pl.pallas_call(
        forward_kernel,
        grid=(steps,),
        in_specs=[rows(model)] + [fixed(a) for a in (zw, xw, bcw, dtw, convw, convb, dtb, alog, skip)],
        out_specs=[rows(w) for w, _ in shapes]
        + [pl.BlockSpec((sub, n, channels), lambda i: (i, 0, 0))],
        out_shape=[jax.ShapeDtypeStruct((length, w), t) for w, t in shapes]
        + [jax.ShapeDtypeStruct((length // SPAN, n, channels), BF16)],
        scratch_shapes=[
            pltpu.VMEM((n, channels), F32),
            pltpu.VMEM((ROWS + 8, channels), F32),
            pltpu.VMEM((SPAN, channels), BF16),
        ],
        compiler_params=pltpu.CompilerParams(vmem_limit_bytes=VMEM_BYTES),
        cost_estimate=pl.CostEstimate(
            flops=4 * length * model * channels, bytes_accessed=32 * 2**20, transcendentals=length * channels * 8
        ),
        name="scan_forward",
    )(x, zw, xw, bcw, dtw, convw, convb, dtb, alog, skip)


def backward_kernel(
    dg_ref, gate_ref, scan_ref, conv_ref, inner_ref, bc_ref, step_ref, prev_ref,
    convw_ref, dtb_ref, alog_ref, skip_ref, hot_ref,
    dgate_ref, dinner_ref, dbc_ref, dstep_ref, vec_ref, head_ref,
    lam, dconv, dyc_s, vt_s, q_s, v_s, w_s, da_s, etot_s,
):
    rows_num, channels = gate_ref.shape
    n = lam.shape[0]
    heads = hot_ref.shape[0]

    @pl.when(pl.program_id(0) == 0)
    def _():
        lam[...] = jnp.zeros_like(lam)
        dconv[rows_num:, :] = jnp.zeros((8, channels), F32)
        vec_ref[...] = jnp.zeros_like(vec_ref)
        head_ref[...] = jnp.zeros_like(head_ref)

    rate = -jnp.exp(alog_ref[...])
    lower = lower_mask((SPAN, SPAN))
    lower_f = lower.astype(F32)
    lower_b = lower.astype(BF16)
    row_at = lax.broadcasted_iota(jnp.int32, (SPAN, SPAN), 0)
    col_at = lax.broadcasted_iota(jnp.int32, (SPAN, SPAN), 1)
    upper = row_at <= col_at
    strict = row_at < col_at
    strict_f = strict.astype(F32)
    left = lax.broadcasted_iota(jnp.int32, (SPAN, 128), 1) < 64

    def block(back, carry):
        at = rows_num // SPAN - 1 - back
        rows = pl.ds(pl.multiple_of(at * SPAN, SPAN), SPAN)
        raw = step_ref[rows, :] + dtb_ref[...]
        delta = softplus(raw)
        cum = mm_exact(lower_f, delta * rate)
        cum_t = cum.T
        delta_t = delta.T
        slope_t = sigmoid(raw).T
        rate_t = jnp.broadcast_to(rate, (SPAN, 128)).T
        b_val = bc_ref[rows, :n].astype(BF16)
        c_val = bc_ref[rows, n:].astype(BF16)
        inner = jnp.where(upper, mm_nt(b_val, c_val), 0.0)
        before = prev_ref[at]
        lam_b = lam[...].astype(BF16)
        across = mm(c_val, before)
        dtail = mm(b_val, lam_b)
        d_inner_prod = jnp.zeros((SPAN, SPAN), F32)
        for pair in range(channels // 128):
            cols = slice(pair * 128, pair * 128 + 128)
            c0, c1, ce = pair_columns(cum, pair, left)
            _, _, de = pair_columns(delta, pair, left)
            tot = ce[SPAN - 1 : SPAN, :]
            e_cum = jnp.exp(ce)
            e_tail = jnp.exp(tot - ce)
            dg = dg_ref[rows, cols].astype(F32)
            gate = gate_ref[rows, cols]
            sg = sigmoid(gate)
            sl = gate * sg
            dgate_ref[rows, cols] = (dg * scan_ref[rows, cols] * (sg + sl * (1.0 - sg))).astype(BF16)
            dy = dg * sl
            conv_p = conv_ref[rows, cols]
            sc = sigmoid(conv_p)
            act = conv_p * sc
            vec_ref[5:6, cols] += jnp.sum(dy * act, axis=0, keepdims=True)
            u = act * de
            u_b = u.astype(BF16)
            dy0 = jnp.where(left, dy, 0.0).astype(BF16)
            dy1 = jnp.where(left, 0.0, dy).astype(BF16)
            dy01 = jnp.concatenate([dy0, dy1], axis=0)
            m0 = jnp.exp(jnp.minimum(cum_t[2 * pair : 2 * pair + 1, :] - c0, 0.0))
            m1 = jnp.exp(jnp.minimum(cum_t[2 * pair + 1 : 2 * pair + 2, :] - c1, 0.0))
            p0 = m0 * inner
            p1 = m1 * inner
            du = mm(jnp.concatenate([p0.astype(BF16), p1.astype(BF16)], axis=1), dy01)
            dp = mm_nt(u_b, dy01)
            dp0, dp1 = dp[:, :SPAN], dp[:, SPAN:]
            d_inner_prod += dp0 * m0 + dp1 * m1
            e01 = jnp.concatenate([(dp0 * p0).astype(BF16), (dp1 * p1).astype(BF16)], axis=0)
            spans = mm(e01, lower_b)
            da_s[2 * pair : 2 * pair + 1, :] = jnp.sum(
                jnp.where(strict, spans[:SPAN], 0.0), axis=0, keepdims=True
            )
            da_s[2 * pair + 1 : 2 * pair + 2, :] = jnp.sum(
                jnp.where(strict, spans[SPAN:], 0.0), axis=0, keepdims=True
            )
            dut = dtail[:, cols] * e_tail
            du = du + dut
            dye = dy * e_cum
            dyc_s[:, cols] = dye.astype(BF16)
            vt_s[:, cols] = (u * e_tail).astype(BF16)
            q_s[:, cols] = (dye * across[:, cols]).astype(BF16)
            v_s[:, cols] = (u * dut).astype(BF16)
            w_s[:, cols] = (act * du).astype(BF16)
            etot_s[:, cols] = jnp.exp(tot)
            d_act = de * du + skip_ref[:, cols] * dy
            dconv[rows, cols] = d_act * (sc * (1.0 + conv_p * (1.0 - sc)))
        hot = hot_ref[...]
        over = jnp.sum(lam[...] * before.astype(F32), axis=0, keepdims=True) * etot_s[...]
        over = jnp.broadcast_to(over, (128, channels))
        over = lax.dot_general(
            hot.astype(F32), over, (((1,), (1,)), ((), ())), preferred_element_type=F32, precision=HIGHEST
        )
        da = (
            da_s[...]
            + mm_exact(mm_nt(hot, q_s[...]), lower_f)
            + mm_exact(mm_nt(hot, v_s[...]), strict_f)
            + over
        )
        d_step = mm_nt(hot, w_s[...]) + rate_t[:heads] * da
        d_raw = d_step * slope_t[:heads]
        head_ref[0:heads, :] += d_raw
        head_ref[heads : 2 * heads, :] += delta_t[:heads] * da * rate_t[:heads]
        dstep_ref[:, rows] = d_raw
        dg_b = jnp.where(upper, d_inner_prod, 0.0)
        dbc_ref[rows, :n] = mm(dg_b.astype(BF16), c_val) + mm_nt(vt_s[...], lam_b)
        dbc_ref[rows, n:] = mm(dg_b.T.astype(BF16), b_val) + mm_nt(dyc_s[...], before)
        lam[...] = lam[...] * etot_s[...] + mm(bc_ref[rows, n:].T.astype(BF16), dyc_s[...])
        return carry

    lax.fori_loop(0, rows_num // SPAN, block, 0)
    inner_v = inner_ref[...]
    d_in = jnp.zeros((rows_num, channels), F32)
    for k in range(4):
        shifted = dconv[3 - k : 3 - k + rows_num, :]
        d_in += convw_ref[k : k + 1, :] * shifted
        vec_ref[k : k + 1, :] += jnp.sum(inner_v * shifted, axis=0, keepdims=True)
    vec_ref[4:5, :] += jnp.sum(dconv[0:rows_num, :], axis=0, keepdims=True)
    dinner_ref[...] = d_in.astype(BF16)
    dconv[rows_num:, :] = dconv[0:8, :]


def backward_call(dg, gate, scan, conv, inner, bc, step, prev, convw, dtb, alog, skip, hot):
    length, channels = gate.shape
    n = bc.shape[1] // 2
    heads = hot.shape[0]
    steps = length // ROWS
    fixed = lambda a: pl.BlockSpec(a.shape, lambda i: (0,) * a.ndim)
    rows = lambda w: pl.BlockSpec((ROWS, w), lambda i: (steps - 1 - i, 0))
    sub = ROWS // SPAN
    return pl.pallas_call(
        backward_kernel,
        grid=(steps,),
        in_specs=[rows(a.shape[1]) for a in (dg, gate, scan, conv, inner, bc, step)]
        + [pl.BlockSpec((sub, n, channels), lambda i: (steps - 1 - i, 0, 0))]
        + [fixed(a) for a in (convw, dtb, alog, skip, hot)],
        out_specs=[
            rows(channels), rows(channels), rows(2 * n),
            pl.BlockSpec((heads, ROWS), lambda i: (0, steps - 1 - i)),
            pl.BlockSpec((8, channels), lambda i: (0, 0)),
            pl.BlockSpec((2 * heads, SPAN), lambda i: (0, 0)),
        ],
        out_shape=[
            jax.ShapeDtypeStruct((length, channels), BF16),
            jax.ShapeDtypeStruct((length, channels), BF16),
            jax.ShapeDtypeStruct((length, 2 * n), F32),
            jax.ShapeDtypeStruct((heads, length), F32),
            jax.ShapeDtypeStruct((8, channels), F32),
            jax.ShapeDtypeStruct((2 * heads, SPAN), F32),
        ],
        scratch_shapes=[
            pltpu.VMEM((n, channels), F32),
            pltpu.VMEM((ROWS + 8, channels), F32),
        ]
        + [pltpu.VMEM((SPAN, channels), BF16)] * 5
        + [pltpu.VMEM((heads, SPAN), F32), pltpu.VMEM((1, channels), F32)],
        compiler_params=pltpu.CompilerParams(vmem_limit_bytes=VMEM_BYTES),
        cost_estimate=pl.CostEstimate(
            flops=2**31, bytes_accessed=30 * 2**20, transcendentals=length * channels * 16
        ),
        name="scan_backward",
    )(dg, gate, scan, conv, inner, bc, step, prev, convw, dtb, alog, skip, hot)


def segments(channels):
    ends = [channels * 2**w // 8 for w in range(4)]
    return list(zip([0] + ends[:-1], ends))


def middle_kernel(g_ref, w_ref, gain_ref, tok_ref, cot_ref, out_ref, dg_ref, dy_ref, gg_ref, ggrad_ref):
    groups, rows_num, channels = g_ref.shape
    model = tok_ref.shape[1]
    segs = segments(channels)
    sums = [jnp.zeros((rows_num, 1), F32) for _ in segs]
    for j in range(groups):
        g = g_ref[j].astype(F32)
        gg_ref[j] = (g * gain_ref[j]).astype(BF16)
        for w, (lo, hi) in enumerate(segs):
            sums[w] += jnp.sum(g[:, lo:hi] * g[:, lo:hi], axis=1, keepdims=True)
    recips = []
    total = jnp.zeros((rows_num, 1), F32)
    for w, (lo, hi) in enumerate(segs):
        total = total + sums[w]
        recips.append(lax.rsqrt(total / (hi * groups) + EPSILON))
    tile = 512

    def forward(at, dots):
        cols = pl.ds(pl.multiple_of(at * tile, tile), tile)
        acc = jnp.zeros((rows_num, tile), F32)
        tok = tok_ref[:, cols].astype(F32)
        new = []
        for w, (lo, hi) in enumerate(segs):
            acc += mm(
                jnp.concatenate([gg_ref[j, :, lo:hi] for j in range(groups)], axis=1),
                jnp.concatenate([w_ref[j, lo:hi, cols] for j in range(groups)], axis=0),
            )
            out_ref[w, :, cols] = (tok + recips[w] * acc).astype(BF16)
            new.append(dots[w] + jnp.sum(cot_ref[w, :, cols].astype(F32) * acc, axis=1, keepdims=True))
        combined = jnp.zeros((rows_num, tile), F32)
        for w in reversed(range(4)):
            combined += recips[w] * cot_ref[w, :, cols].astype(F32)
            dy_ref[w, :, cols] = combined.astype(BF16)
        return tuple(new)

    dots = lax.fori_loop(
        0, model // tile, forward, tuple(jnp.zeros((rows_num, 1), F32) for _ in segs)
    )
    scales = [None] * 4
    scale = jnp.zeros((rows_num, 1), F32)
    for w in reversed(range(4)):
        scale = scale + recips[w] ** 3 * dots[w] / (segs[w][1] * groups)
        scales[w] = scale

    def back(j, carry):
        for w, (lo, hi) in enumerate(segs):
            dn = mm_nt(dy_ref[w], w_ref[j, lo:hi, :])
            g = g_ref[j, :, lo:hi].astype(F32)
            ggrad_ref[j, :, lo:hi] = jnp.sum(g * dn, axis=0, keepdims=True)
            dg_ref[j, :, lo:hi] = (gain_ref[j, :, lo:hi] * dn - g * scales[w]).astype(BF16)
        return carry

    lax.fori_loop(0, groups, back, 0)


def middle_call(g, w_all, gain, tok, cot):
    groups, rows_num, channels = g.shape
    model = tok.shape[1]
    return pl.pallas_call(
        middle_kernel,
        out_shape=[
            jax.ShapeDtypeStruct((4, rows_num, model), BF16),
            jax.ShapeDtypeStruct(g.shape, BF16),
            jax.ShapeDtypeStruct((4, rows_num, model), BF16),
            jax.ShapeDtypeStruct(g.shape, BF16),
            jax.ShapeDtypeStruct((groups, 1, channels), F32),
        ],
        compiler_params=pltpu.CompilerParams(vmem_limit_bytes=VMEM_BYTES),
        cost_estimate=pl.CostEstimate(
            flops=4 * groups * rows_num * channels * model, bytes_accessed=36 * 2**20, transcendentals=0
        ),
        name="nested_norm",
    )(g, w_all, gain, tok, cot)


def partner(axis, bit):
    me = lax.axis_index(axis)
    return me + (1 - 2 * ((me // 2**bit) % 2)) * 2**bit


def bits_of(axis, count):
    me = lax.axis_index(axis)
    return [(me // 2**b) % 2 for b in range(count)]


def log2(value):
    return value.bit_length() - 1


def place(count, fixed):
    return tuple(fixed[b] if b in fixed else slice(None) for b in reversed(range(count)))


class Links:
    def __init__(self, send, recv):
        self.send, self.recv, self.used = send, recv, 0

    def copy(self, src, dst, axis, to):
        at = self.used
        self.used += 1
        return pltpu.make_async_remote_copy(
            src_ref=src, dst_ref=dst, send_sem=self.send.at[at], recv_sem=self.recv.at[at],
            device_id={axis: to}, device_id_type=pl.DeviceIdType.MESH,
        )


def meet(peers):
    barrier = pltpu.get_barrier_semaphore()
    for axis, to in peers:
        pl.semaphore_signal(barrier, inc=1, device_id={axis: to}, device_id_type=pl.DeviceIdType.MESH)
    pl.semaphore_wait(barrier, len(peers))


def add_block(buf, index, slot, at):
    rows = slot.shape[-2]
    step = min(rows, 32)
    index = index + (slice(None),) * (len(buf.shape) - len(index))
    free = [i for i, v in enumerate(index[:-2]) if isinstance(v, slice)]
    full = list(index[:-2])
    for i, v in zip(free, at):
        full[i] = v
    full = tuple(full)

    def piece(r, carry):
        rs = pl.ds(pl.multiple_of(r * step, step), step)
        total = buf[full + (rs, index[-1])].astype(F32) + slot[tuple(at) + (rs, slice(None))].astype(F32)
        buf[full + (rs, index[-1])] = total.astype(buf.dtype)
        return carry

    lax.fori_loop(0, rows // step, piece, 0)


def scatter(links, buf, slots, order, lead=()):
    count = len(order)
    mine = bits_of("batch", count)
    fixed = {}
    for i, b in enumerate(order):
        keep = {**fixed, b: mine[b]}
        copy = links.copy(buf.at[place(count, {**fixed, b: 1 - mine[b]})], slots[i], "batch", partner("batch", b))
        copy.start()
        yield
        copy.wait()
        dims = slots[i].shape[:-2]
        for at in itertools.product(*(range(d) for d in dims)):
            add_block(buf, place(count, keep), slots[i], at)
        fixed = keep


def gather(links, buf, order):
    count = len(order)
    fixed = dict(enumerate(bits_of("batch", count)))
    for b in order:
        at = buf.at[place(count, fixed)]
        copy = links.copy(at, at, "batch", partner("batch", b))
        copy.start()
        yield
        copy.wait()
        fixed = {k: v for k, v in fixed.items() if k != b}


def doubling(links, buf, slots, axis, bits):
    for i, b in enumerate(bits):
        copy = links.copy(buf, slots[i], axis, partner(axis, b))
        copy.start()
        yield
        copy.wait()
        buf[...] = (buf[...].astype(F32) + slots[i][...].astype(F32)).astype(buf.dtype)


def chain(*parts):
    for part in parts:
        yield from part


def run_streams(streams):
    live = list(streams)
    while live:
        live = [s for s in live if next(s, live) is not live]


def halving_slots(count, block, dtype):
    return [pltpu.VMEM((2,) * (count - 1 - i) + tuple(block), dtype) for i in range(count)]


def weights_kernel(w_ref, gain_ref, all_ref, gains_ref, local, send, recv):
    groups = all_ref.shape[0]
    count = len(all_ref.shape) - 3
    part, model = all_ref.shape[-2:]
    half = model // 2
    group_bits = log2(groups)
    me = lax.axis_index("head")
    mine = bits_of("batch", count)
    others = [me + sum((1 - 2 * ((me // 2**b) % 2)) * 2**b for b in range(group_bits) if k & 2**b) for k in range(1, groups)]
    links = Links(send, recv)
    meet([("head", z) for z in others] + [("batch", partner("batch", b)) for b in range(count)])
    own = place(count, dict(enumerate(mine)))
    own_copy = pltpu.make_async_copy(w_ref, all_ref.at[me], local.at[0])
    own_copy.start()
    gain_copy = pltpu.make_async_copy(gain_ref, gains_ref.at[me], local.at[1])
    gain_copy.start()
    gain_sends = []
    for z in others:
        gain_sends.append(links.copy(gain_ref, gains_ref.at[me], "head", z))
        gain_sends[-1].start()
    up = list(range(1, count))

    def stream(z, cols, order):
        copy = links.copy(
            w_ref.at[own + (slice(None), cols)], all_ref.at[(me,) + own + (slice(None), cols)], "head", z
        )
        copy.start()
        yield
        copy.wait()
        fixed = dict(enumerate(mine))
        for b in order:
            at = all_ref.at[(z,) + place(count, fixed) + (slice(None), cols)]
            step = links.copy(at, at, "batch", partner("batch", b))
            step.start()
            yield
            step.wait()
            fixed = {k: v for k, v in fixed.items() if k != b}

    streams = []
    for z in others:
        streams.append(stream(z, pl.ds(0, half), up + [0]))
        streams.append(stream(z, pl.ds(half, half), up[::-1] + [0]))
    run_streams(streams)
    for c in gain_sends:
        c.wait()
    own_copy.wait()
    gain_copy.wait()


def weights_call(out_weight, norm_gain, groups, batches):
    channels, model = out_weight.shape
    count = log2(batches)
    part = channels // batches
    copies = (groups - 1) * (1 + 2 * (1 + count))
    hbm = pl.BlockSpec(memory_space=pl.ANY)
    w_all, gains = pl.pallas_call(
        weights_kernel,
        in_specs=[hbm, hbm],
        out_specs=[hbm, hbm],
        out_shape=[
            jax.ShapeDtypeStruct((groups,) + (2,) * count + (part, model), BF16),
            jax.ShapeDtypeStruct((groups, 8, channels), F32),
        ],
        scratch_shapes=[
            pltpu.SemaphoreType.DMA((2,)), pltpu.SemaphoreType.DMA((copies,)), pltpu.SemaphoreType.DMA((copies,)),
        ],
        compiler_params=pltpu.CompilerParams(
            collective_id=1, has_side_effects=True, vmem_limit_bytes=VMEM_BYTES
        ),
        cost_estimate=pl.CostEstimate(flops=0, bytes_accessed=300 * 2**20, transcendentals=0),
        name="gather_weights",
    )(out_weight.reshape((2,) * count + (part, model)), jnp.broadcast_to(norm_gain[None], (8, channels)))
    return w_all.reshape(groups, channels, model), gains[:, :1]


def outgrad_scatter_kernel(count, gg_ref, dy_ref, out_ref, *refs):
    buf, send, recv = refs[0], refs[-2], refs[-1]
    streams_num = 4
    slots = [refs[1 + s * count : 1 + (s + 1) * count] for s in range(streams_num)]
    groups, _, channels = gg_ref.shape
    part, cols = buf.shape[-2:]
    model = dy_ref.shape[2]
    links = Links(send, recv)
    meet([("batch", partner("batch", b)) for b in range(count)])
    up = list(range(1, count))

    def stream(s):
        g0, c0 = (s // 2) * (groups // 2), (s % 2) * cols
        for j in range(groups // 2):
            for w, (lo, hi) in enumerate(segments(channels)):
                term = mm_tn(gg_ref[g0 + j, :, lo:hi], dy_ref[w, :, c0 : c0 + cols]).astype(BF16)
                for p in range(lo // part, hi // part):
                    index = tuple((p >> b) & 1 for b in reversed(range(count)))
                    buf[(s,) + index + (j,)] = term[p * part - lo : (p + 1) * part - lo]
        order = [0] + (up if s % 2 == 0 else up[::-1])
        yield from scatter(links, buf.at[s], slots[s], order)
        mine = place(count, dict(enumerate(bits_of("batch", count))))
        for j in range(groups // 2):
            out_ref[g0 + j, :, c0 : c0 + cols] = buf[(s,) + mine + (j,)]

    run_streams([stream(s) for s in range(streams_num)])


def outgrad_scatter_call(gg, dy, batches):
    groups, _, channels = gg.shape
    model = dy.shape[2]
    count = log2(batches)
    part = channels // batches
    block = (groups // 2, part, model // 2)
    vmem = pl.BlockSpec(memory_space=pltpu.VMEM)
    return pl.pallas_call(
        functools.partial(outgrad_scatter_kernel, count),
        in_specs=[vmem, vmem],
        out_specs=vmem,
        out_shape=jax.ShapeDtypeStruct((groups, part, model), BF16),
        scratch_shapes=[pltpu.VMEM((4,) + (2,) * count + block, BF16)]
        + [s for _ in range(4) for s in halving_slots(count, block, BF16)]
        + [pltpu.SemaphoreType.DMA((4 * count,)), pltpu.SemaphoreType.DMA((4 * count,))],
        compiler_params=pltpu.CompilerParams(
            collective_id=2, has_side_effects=True, vmem_limit_bytes=VMEM_BYTES
        ),
        cost_estimate=pl.CostEstimate(
            flops=2 * groups * gg.shape[1] * channels * model, bytes_accessed=200 * 2**20, transcendentals=0
        ),
        name="out_weight_grad",
    )(gg, dy)


def tail_kernel(
    count, group_bits,
    z_ref, x_ref, o_ref, bc_ref, small_ref,
    zo_ref, xo_ref, oo_ref, bco_ref, smallo_ref, *refs
):
    zx, zx_full, obuf, bcbuf, bc_full, small = refs[:6]
    refs = refs[6:]
    zx_slots = [refs[s * count : (s + 1) * count] for s in range(4)]
    refs = refs[4 * count :]
    bc_slots, refs = refs[:count], refs[count:]
    bc_head, refs = refs[:group_bits], refs[group_bits:]
    small_slots, refs = refs[:count], refs[count:]
    small_head, refs = refs[:group_bits], refs[group_bits:]
    local, send, recv = refs
    cols = zx.shape[-1]
    ocols = obuf.shape[-1]
    shared = small_head[0].shape[0]
    links = Links(send, recv)
    mine = place(count, dict(enumerate(bits_of("batch", count))))
    loads = []
    for s in range(4):
        src = (z_ref, x_ref)[s // 2]
        index = (slice(None),) * (count + 1) + (pl.ds((s % 2) * cols, cols),)
        loads.append(pltpu.make_async_copy(src.at[index], zx.at[s], local.at[s]))
    loads.append(pltpu.make_async_copy(bc_ref, bcbuf, local.at[4]))
    loads.append(pltpu.make_async_copy(small_ref, small, local.at[5]))
    for s in range(2):
        loads.append(
            pltpu.make_async_copy(o_ref.at[:, pl.ds(s * ocols, ocols)], obuf.at[(s,) + mine], local.at[6 + s])
        )
    for load in loads:
        load.start()
    meet(
        [("batch", partner("batch", b)) for b in range(count)]
        + [("head", partner("head", b)) for b in range(group_bits)]
    )
    up = list(range(1, count))
    orders = [up, up[::-1]]
    stores = []

    def store(src, dst, at):
        stores.append(pltpu.make_async_copy(src, dst, local.at[at]))
        stores[-1].start()

    def grads(s):
        loads[s].wait()
        yield from scatter(links, zx.at[s], zx_slots[s], [0] + orders[s // 2])
        zx_full[(s,) + mine] = zx[(s,) + mine]
        yield from gather(links, zx_full.at[s], orders[s // 2][::-1] + [0])
        index = (slice(None),) * (count + 1) + (pl.ds((s % 2) * cols, cols),)
        store(zx_full.at[s], (zo_ref, xo_ref)[s // 2].at[index], 8 + s)

    def state(order):
        loads[4].wait()
        yield from scatter(links, bcbuf, bc_slots, [0] + order)
        yield from doubling(links, bcbuf.at[mine], bc_head, "head", range(group_bits))
        bc_full[mine] = bcbuf[mine]
        yield from gather(links, bc_full, order[::-1] + [0])
        store(bc_full, bco_ref, 12)

    def vectors():
        loads[5].wait()
        yield from doubling(links, small, small_slots, "batch", range(count))
        yield from doubling(links, small.at[pl.ds(0, shared)], small_head, "head", range(group_bits))
        smallo_ref[...] = small[...]

    def outs(s):
        loads[6 + s].wait()
        yield from gather(links, obuf.at[s], orders[s] + [0])
        index = (slice(None),) * (count + 1) + (pl.ds(s * ocols, ocols),)
        store(obuf.at[s], oo_ref.at[index], 13 + s)

    run_streams([grads(0), grads(2), grads(1), grads(3), vectors(), state(orders[0]), outs(0), outs(1)])
    for item in stores:
        item.wait()


def tail_call(z_grad, x_grad, out_own, bc_grad, small, shared, groups, batches):
    model, channels = z_grad.shape
    count = log2(batches)
    group_bits = log2(groups)
    rows = model // batches
    part, width = out_own.shape
    n2 = bc_grad.shape[1]
    lead = (2,) * count
    hbm = pl.BlockSpec(memory_space=pl.ANY)
    vmem = pl.BlockSpec(memory_space=pltpu.VMEM)
    block = (rows, channels // 2)
    copies = 4 * 2 * count + 2 * count + group_bits + count + group_bits + 2 * count
    zo, xo, oo, bco, smallo = pl.pallas_call(
        functools.partial(tail_kernel, count, group_bits),
        in_specs=[hbm] * 5,
        out_specs=[hbm] * 4 + [vmem],
        out_shape=[
            jax.ShapeDtypeStruct(lead + (rows, channels), BF16),
            jax.ShapeDtypeStruct(lead + (rows, channels), BF16),
            jax.ShapeDtypeStruct(lead + (part, width), BF16),
            jax.ShapeDtypeStruct(lead + (rows, n2), BF16),
            jax.ShapeDtypeStruct(small.shape, F32),
        ],
        scratch_shapes=[
            pltpu.VMEM((4,) + lead + block, BF16),
            pltpu.VMEM((4,) + lead + block, BF16),
            pltpu.VMEM((2,) + lead + (part, width // 2), BF16),
            pltpu.VMEM(lead + (rows, n2), BF16),
            pltpu.VMEM(lead + (rows, n2), BF16),
            pltpu.VMEM(small.shape, F32),
        ]
        + [s for _ in range(4) for s in halving_slots(count, block, BF16)]
        + halving_slots(count, (rows, n2), BF16)
        + [pltpu.VMEM((rows, n2), BF16)] * group_bits
        + [pltpu.VMEM(small.shape, F32)] * count
        + [pltpu.VMEM((shared, small.shape[1]), F32)] * group_bits
        + [
            pltpu.SemaphoreType.DMA((15,)), pltpu.SemaphoreType.DMA((copies,)), pltpu.SemaphoreType.DMA((copies,)),
        ],
        compiler_params=pltpu.CompilerParams(
            collective_id=3, has_side_effects=True, vmem_limit_bytes=VMEM_BYTES
        ),
        cost_estimate=pl.CostEstimate(flops=0, bytes_accessed=300 * 2**20, transcendentals=0),
        name="sum_grads",
    )(
        z_grad.reshape(lead + (rows, channels)), x_grad.reshape(lead + (rows, channels)), out_own,
        bc_grad.reshape(lead + (rows, n2)), small,
    )
    return (
        zo.reshape(model, channels), xo.reshape(model, channels), oo.reshape(part * batches, width),
        bco.reshape(model, n2), smallo,
    )


def per_device(
    tokens, z_weight, x_weight, bc_weight, dt_weight, conv_weight, conv_bias, dt_bias,
    a_log, skip, norm_gain, pre_gain, out_weight, cotangent,
):
    groups = lax.axis_size("head")
    batches = lax.axis_size("batch")
    head_at = lax.axis_index("head")
    _, own_len, model = tokens.shape
    tokens = tokens[0]
    cot = cotangent[:, 0]
    channels = z_weight.shape[1]
    heads = dt_weight.shape[1]
    tokens_f = tokens.astype(F32)
    recip_in = lax.rsqrt(jnp.mean(tokens_f * tokens_f, axis=-1, keepdims=True) + EPSILON)
    normed = (tokens_f * recip_in * pre_gain).astype(BF16)
    x = lax.all_gather(normed, "head", axis=0, tiled=True)
    w_all, gain_all = weights_call(out_weight, norm_gain, groups, batches)
    x, w_all = lax.optimization_barrier((x, w_all))

    pad = lambda v: jnp.pad(v, ((0, 0), (0, 128 - heads)))
    dtb = pad(dt_bias[None])
    alog = pad(a_log[None])
    skip_r = skip[None]
    gated, gate, scan, conv, inner, bc, step, prev = forward_call(
        x, z_weight, x_weight, bc_weight, pad(dt_weight), conv_weight, conv_bias[None], dtb, alog, skip_r
    )
    gated = lax.all_to_all(gated.reshape(groups, own_len, channels), "head", 0, 0, tiled=True)
    outputs, d_gated, dy, gg, gain_grad = middle_call(gated, w_all, gain_all, tokens, cot)
    d_gated = lax.all_to_all(d_gated, "head", 0, 0, tiled=True).reshape(groups * own_len, channels)
    out_part = outgrad_scatter_call(gg, dy, batches)
    d_gated, out_part = lax.optimization_barrier((d_gated, out_part))
    out_part = lax.psum_scatter(out_part.reshape(-1, model), "head", scatter_dimension=0, tiled=True)
    hot = (jnp.arange(channels)[None] // (channels // heads) == jnp.arange(heads)[:, None]).astype(BF16)
    d_gate, d_inner, d_bc, d_step, vec, per_head = backward_call(
        d_gated, gate, scan, conv, inner, bc, step, prev, conv_weight, dtb, alog, skip_r, hot
    )
    d_step = d_step.astype(BF16)
    d_bc = d_bc.astype(BF16)
    d_rows = (
        mm_nt(d_gate, z_weight)
        + mm_nt(d_inner, x_weight)
        + lax.dot_general(d_step, dt_weight, (((0,), (1,)), ((), ())), preferred_element_type=F32)
        + mm_nt(d_bc, bc_weight)
    )
    d_rows = d_rows.astype(BF16)
    d_own = lax.psum_scatter(d_rows, "head", scatter_dimension=0, tiled=True).astype(F32)
    z_grad = mm_tn(x, d_gate).astype(BF16)
    x_grad = mm_tn(x, d_inner).astype(BF16)
    dt_grad = lax.dot_general(x, d_step, (((0,), (1,)), ((), ())), preferred_element_type=F32)
    bc_grad = mm_tn(x, d_bc).astype(BF16)
    pre_grad = jnp.sum(x.astype(F32) * d_rows.astype(F32), axis=0) / pre_gain

    width = 1024
    all_part = jnp.concatenate([jnp.zeros((groups, channels), F32) + gain_grad[:, 0], pre_grad.reshape(-1, width)])
    shared = -(-all_part.shape[0] // 8) * 8
    own_part = jnp.concatenate([vec[:6].reshape(-1), jnp.sum(per_head, axis=1), dt_grad.reshape(-1)])
    own_rows = -(-own_part.shape[0] // (8 * width)) * 8
    small = jnp.concatenate([
        jnp.pad(all_part, ((0, shared - all_part.shape[0]), (0, 0))),
        jnp.pad(own_part, (0, own_rows * width - own_part.shape[0])).reshape(own_rows, width),
    ])
    z_grad, x_grad, out_grad, bc_grad, small = tail_call(
        z_grad, x_grad, out_part, bc_grad, small, shared, groups, batches
    )
    z_grad, x_grad, out_grad, bc_grad = (v.astype(F32) for v in (z_grad, x_grad, out_grad, bc_grad))
    gain_grad = lax.dynamic_slice_in_dim(small, head_at, 1, 0)[0]
    pre_grad = small[groups : groups + model // width].reshape(-1)
    own = small[shared:].reshape(-1)

    inner_sum = jnp.mean(tokens_f * pre_gain * d_own, axis=-1, keepdims=True)
    tokens_grad = jnp.sum(cot.astype(F32), axis=0) + pre_gain * recip_in * d_own
    tokens_grad = (tokens_grad - tokens_f * recip_in**3 * inner_sum).astype(BF16)
    c = channels
    return (
        outputs[:, None],
        tokens_grad[None],
        z_grad,
        x_grad,
        bc_grad,
        own[6 * c + 2 * heads : 6 * c + 2 * heads + model * heads].reshape(model, heads),
        own[: 4 * c].reshape(4, c),
        own[4 * c : 5 * c],
        own[6 * c : 6 * c + heads],
        own[6 * c + heads : 6 * c + 2 * heads],
        own[5 * c : 6 * c],
        gain_grad,
        pre_grad,
        out_grad,
    )


def solution(mesh):
    head_cols = P(None, "head")
    rows4 = P(None, "batch", "head", None)
    return jax.shard_map(
        per_device,
        mesh=mesh,
        in_specs=(
            P("batch", "head", None), head_cols, head_cols, P(), head_cols, head_cols, P("head"),
            P("head"), P("head"), P("head"), P("head"), P(), P("head", None), rows4,
        ),
        out_specs=(
            rows4, P("batch", "head", None), head_cols, head_cols, P(), head_cols, head_cols,
            P("head"), P("head"), P("head"), P("head"), P("head"), P(), P("head", None),
        ),
        check_vma=False,
    )
```

time: 1470 us -> 612 us (0.42)
  waiting for transfers between devices: 795 us -> 47.3 us
  Pallas kernels: 0 us -> 426 us
  matrix products: 250 us -> 47.1 us
  other arithmetic: 160 us -> 34.7 us
  blocking collectives: 123 us -> 0 us
  local copies, waits for them, and re-layouts: 108 us -> 16.5 us
  starting transfers between devices: 1.4 us -> 18 us
    pallas_call x0 -> x6, Pallas kernels: none -> 426 us  [the longest x1 135 us: weights_call(): pl.pallas_call(weights_kernel, in_specs=[hbm, hbm], out_specs=[hbm, hbm],...]
    reduce_scatter x7 -> x2, waiting for transfers between devices: 384 us -> 0.01 us  [the longest x1 0.01 us: per_device(): lax.psum_scatter(out_part.reshape(-1, model), 'head', scatter_dimension=0...]
    all_gather x6 -> x1, waiting for transfers between devices: 344 us -> 0.01 us  [per_device(): x = lax.all_gather(normed, 'head', axis=0, tiled=True)]
    dot_general x36 -> x8, matrix products: 250 us -> 47.1 us  [the longest x3 23.9 us: mm_nt(): lax.dot_general(a, b, (((1,), (1,)), ((), ())), preferred_element_type=F32)]
    all_gather x6 -> x0, blocking collectives: 51.2 us -> none  [the longest x1 9.16 us: per_device(): lax.all_gather(reduced[5].astype(jnp.bfloat16), 'batch', axis=0, tiled=True)]
    psum x3 -> x0, blocking collectives: 48.7 us -> none  [the longest x1 22 us: per_device(): totals = lax.psum(squares, 'head')]
    all_to_all x0 -> x2, waiting for transfers between devices: none -> 47.2 us  [the longest x1 47.2 us: per_device(): lax.all_to_all(gated.reshape(groups, own_len, channels), 'head', 0, 0, ti...]
    reduce_sum x19 -> x3, other arithmetic: 45 us -> 4.93 us  [the longest x1 3.17 us: per_device(): tokens_grad = jnp.sum(cot.astype(F32), axis=0) + pre_gain * recip_in * d_own]
  transfers between devices with their start and end apart: 15 -> 5, of which waited for: 12 -> 1; matrix products, arithmetic and copies ran while one was open for 25% -> 14% of each run, Pallas kernels for 0% -> 61%
where the time goes in v1:
time: 612 us; the launch traced here: 604 us
  Pallas kernels  426 us (70%)
  waiting for transfers between devices  47.3 us (8%)
  matrix products  47.1 us (8%)
  other arithmetic  34.7 us (6%)
  starting transfers between devices  18 us (3%)
  local copies, waits for them, and re-layouts  16.5 us (3%)
  between operations  14.6 us (2%)
    pallas_call x1, Pallas kernels, weights_call(): pl.pallas_call(weights_kernel, in_specs=[hbm, hbm], out_specs=[hbm, hbm],...  135 us
    pallas_call x1, Pallas kernels, tail_call(): pl.pallas_call(functools.partial(tail_kernel, count, group_bits), in_spec...  115 us
    pallas_call x1, Pallas kernels, outgrad_scatter_call(): pl.pallas_call(functools.partial(outgrad_scatter_kernel, count), in_specs...  84.2 us
    all_to_all x1, waiting for transfers between devices, per_device(): lax.all_to_all(gated.reshape(groups, own_len, channels), 'head', 0, 0, ti...  47.2 us
    pallas_call x1, Pallas kernels, backward_call(): pl.pallas_call(backward_kernel, grid=(steps,), in_specs=[rows(a.shape[1])...  35.4 us
    pallas_call x1, Pallas kernels, forward_call(): pl.pallas_call(forward_kernel, grid=(steps,), in_specs=[rows(model)] + [f...  31.3 us
    pallas_call x1, Pallas kernels, middle_call(): pl.pallas_call(middle_kernel, out_shape=[jax.ShapeDtypeStruct((4, rows_nu...  25.4 us
    dot_general x3, matrix products, mm_nt(): lax.dot_general(a, b, (((1,), (1,)), ((), ())), preferred_element_type=F32)  23.9 us
  transfers between devices with their start and end apart: 5, of which 1 were waited for; matrix products, arithmetic and copies ran while one was open for 14% of the time, Pallas kernels for 61%

profile of v1, /device:TPU:0, one launch (start us, length us, event | category | flops | bytes accessed | tf_op | source)
XLA Modules:
  0.0 604.5 jit_solution(8491582306740866860)
XLA Ops:
  7.3 1.5 fusion.4
  8.8 2.5 fusion.6
  13.3 134.7 %gather_weights.1 = (bf16[4,2,2,2,128,2048]{5,4,3,2,1,0:T(8,128)(2,1)}, f32[4,8,1024]{2,1,0:T(8,128)}) custom-call(bf16[2,2,2,128,2048]{4,3,2,1,0:T(8,128)(2,1)} %bitcast.65, f32[8,1024]{1,0:T(8,128)} %broadcast_in_dim.14.gain_ref), custom_call_target="tpu_custom_call" | custom-call | bytes 314572800 | tf_op jit(solution)/shard_map/gather_weights/pallas_call | solution.py:571
  148.9 31.3 %scan_forward.1 = (bf16[1024,1024]{1,0:T(8,128)(2,1)}, f32[1024,1024]{1,0:T(8,128)}, f32[1024,1024]{1,0:T(8,128)}, f32[1024,1024]{1,0:T(8,128)}, f32[1024,1024]{...) custom-call(bf16[1024,2048]{1,0:T(8,128)(2,1)} %all-gather.2.cloned.1.call-done.x_ref, ...), custom_call_target="tpu_custom_call" | custom-call | flops 8589934592 | bytes 33554432 | tf_op jit(solution)/shard_map/scan_forward/pallas_call | solution.py:134
  180.2 13.9 %all-to-all-start = ((bf16[4,256,1024]{2,1,0:T(8,128)(2,1)}), bf16[4,256,1024]{2,1,0:T(8,128)(2,1)S(1)}, u32[]{:S(2)}, u32[]{:S(2)}) async-start(bf16[4,256,1024]{2,1,0:T(8,128)(2,1)} %bitcast.70), calls=%async_computation | async-start | bytes 4194304 | tf_op jit(solution)/shard_map/all_to_all | solution.py:801
  194.1 1.5 slice.43.gain_ref
  195.6 47.2 %all-to-all-done.g_ref = bf16[4,256,1024]{2,1,0:T(8,128)(2,1)S(1)} async-done(((bf16[4,256,1024]{2,1,0:T(8,128)(2,1)}), bf16[4,256,1024]{2,1,0:T(8,128)(2,1)S(1)}, u32[]{:S(2)}, u32[]{:S(2)}) %all-to-all-start) | async-done | bytes 2097184 | tf_op jit(solution)/shard_map/all_to_all | solution.py:801
  242.8 1.3 copy-done.3
  244.2 25.4 %nested_norm.1 = (bf16[4,256,2048]{2,1,0:T(8,128)(2,1)}, bf16[4,256,1024]{2,1,0:T(8,128)(2,1)}, bf16[4,256,2048]{2,1,0:T(8,128)(2,1)}, bf16[4,256,1024]{2,1,0:T(8,128)(2,1)}, f32[4,1,1024]{2,1,0:T(1,128)}) custom-call(bf16[4,256,1024]{2,1,0:T(8,128)(2,1)} %copy-done.3, bf16[4,1024,2048]{2,1,0:T(8,128)(2,1)} %bitcast.79, f32[4,1,1024]{2,1,0:T(1,128)} %slice.43.gain_ref, ...), custom_call_target="tpu_custom_call" | custom-call | flops 8589934592 | bytes 37748736 | tf_op jit(solution)/shard_map/nested_norm/pallas_call | solution.py:390
  269.6 3.6 all-to-all-start.1
  273.4 84.2 %out_weight_grad.1 = bf16[4,128,2048]{2,1,0:T(8,128)(2,1)} custom-call(bf16[4,256,1024]{2,1,0:T(8,128)(2,1)} %get-tuple-element.51.gg_ref, bf16[4,256,2048]{2,1,0:T(8,128)(2,1)} %get-tuple-element.52.dy_ref), custom_call_target="tpu_custom_call" | custom-call | flops 4294967296 | bytes 209715200 | tf_op jit(solution)/shard_map/out_weight_grad/pallas_call | solution.py:626
  358.9 35.4 %scan_backward.1 = (bf16[1024,1024]{1,0:T(8,128)(2,1)}, bf16[1024,1024]{1,0:T(8,128)(2,1)}, f32[1024,256]{1,0:T(8,128)}, f32[16,1024]{1,0:T(8,128)}, f32[8,1024]{1,0:T(8,128)}, /*index=5*/f32[32,128]{1,0:T(8,128)}) custom-call(bf16[1024,1024]{1,0:T(8,128)(2,1)} %bitcast.69, f32[1024,1024]{1,0:T(8,128)} %get-tuple-element.54.gate_ref, ...), custom_call_target="tpu_custom_call" | custom-call | flops 2147483648 | bytes 31457280 | tf_op jit(solution)/shard_map/scan_backward/pallas_call | solution.py:293
  394.3 2.3 fusion.14
  397.3 6.8 %fusion.20 = f32[1024,2048]{1,0:T(8,128)} fusion(bf16[1024,1024]{1,0:T(8,128)(2,1)S(1)} %copy-done.18, bf16[2048,1024]{1,0:T(8,128)(2,1)S(1)} %copy-done.12), kind=kOutput, calls=%fused_computation.52 | convolution fusion | flops 4294967296 | bytes 14680064 | tf_op jit(solution)/shard_map/dot_general | solution.py:25
  404.1 6.8 %fusion.21 = f32[1024,2048]{1,0:T(8,128)} fusion(bf16[1024,1024]{1,0:T(8,128)(2,1)S(1)} %copy-done.16, bf16[2048,1024]{1,0:T(8,128)(2,1)S(1)} %copy-done.13), kind=kOutput, calls=%fused_computation.53 | convolution fusion | flops 4294967296 | bytes 14680064 | tf_op jit(solution)/shard_map/dot_general | solution.py:25
  410.9 10.4 %multiply_reduce_fusion = (f32[2048]{0:T(1024)S(1)}, bf16[1024,2048]{1,0:T(8,128)(2,1)}) fusion(bf16[1024,2048]{1,0:T(8,128)(2,1)} %all-gather.2.cloned.1.call-done.x_ref, bf16[2048,256]{1,0:T(8,128)(2,1)S(1)} %copy-done.4, f32[1024,256]{1,0:T(8,128)} %get-tuple-element.64, f32[1024,2048]{1,0:T(8,128)S(1)} %fusion.14, f32[1024,2048]{1,0:T(8,128)} %fusion.20, ...), kind=kOutput, calls=%fused_computation | convolution fusion | flops 1090779136 | bytes 35659776 | tf_op jit(solution)/shard_map/dot_general | solution.py:25
  421.3 3.2 convert_reduce_fusion
  424.6 3.5 fusion.12
  429.4 5.0 convolution_convert_fusion.2
  434.4 6.2 %convolution_convert_fusion.1 = bf16[2048,1024]{1,0:T(8,128)(2,1)} fusion(bf16[1024,2048]{1,0:T(8,128)(2,1)S(1)} %copy-done, bf16[1024,1024]{1,0:T(8,128)(2,1)S(1)} %copy-done.19), kind=kOutput, calls=%fused_computation.7 | convolution fusion | flops 4297064448 | bytes 10485760 | tf_op jit(solution)/shard_map/dot_general | solution.py:29
  440.6 6.2 %convolution_convert_fusion = bf16[2048,1024]{1,0:T(8,128)(2,1)} fusion(bf16[1024,2048]{1,0:T(8,128)(2,1)S(1)} %copy-done, bf16[1024,1024]{1,0:T(8,128)(2,1)S(1)} %copy-done.17), kind=kOutput, calls=%fused_computation.6 | convolution fusion | flops 4297064448 | bytes 10485760 | tf_op jit(solution)/shard_map/dot_general | solution.py:29
  446.8 115.4 %sum_grads.1 = (bf16[2,2,2,256,1024]{4,3,2,1,0:T(8,128)(2,1)}, bf16[2,2,2,256,1024]{4,3,2,1,0:T(8,128)(2,1)}, bf16[2,2,2,128,2048]{4,3,2,1,0:T(8,128)(2,1)}, bf1...) custom-call(bf16[2,2,2,256,1024]{4,3,2,1,0:T(8,128)(2,1)} %bitcast.66, bf16[2,2,2,256,1024]{4,3,2,1,0:T(8,128)(2,1)} %bitcast.67, ...), custom_call_target="tpu_custom_call" | custom-call | bytes 314572800 | tf_op jit(solution)/shard_map/sum_grads/pallas_call | solution.py:733
  562.2 1.4 slice.48
  564.5 1.5 slice.46
  566.0 1.3 slice.56
  567.3 1.0 copy.34
  570.3 1.4 constant_dynamic-slice_fusion
  571.7 2.7 bitcast_convert_fusion.3
  574.4 6.7 %bitcast_convert_fusion = f32[1024,2048]{1,0:T(8,128)} fusion(bf16[2,2,2,128,2048]{4,3,2,1,0:T(8,128)(2,1)} %get-tuple-element.73), kind=kLoop, calls=%fused_computation.3 | loop fusion | flops 2097152 | bytes 12582912 | tf_op jit(solution)/shard_map/convert_element_type | solution.py:839
  581.1 11.8 %bitcast_convert_fusion.1 = (f32[2048,1024]{1,0:T(8,128)}, f32[2048,1024]{1,0:T(8,128)}) fusion(bf16[2,2,2,256,1024]{4,3,2,1,0:T(8,128)(2,1)} %get-tuple-element.70, bf16[2,2,2,256,1024]{4,3,2,1,0:T(8,128)(2,1)} %get-tuple-element.69), kind=kLoop, calls=%fused_computation.4 | loop fusion | flops 4194304 | bytes 25165824 | tf_op jit(solution)/shard_map/convert_element_type | solution.py:839
  592.9 1.6 fusion.3
  594.6 2.9 fusion.8
  (74 shorter events, 9.4 us)
Async XLA Ops:
  7.2 4.2 copy-start.14
  7.2 4.7 copy-start.15
  7.2 5.2 copy-start.6
  7.2 5.5 copy-start.11
  7.2 141.7 %all-gather.2.cloned.1.call-start = ((), (), s32[]{:S(2)}) async-start(), calls=%async_computation.4 | async-start | bytes 5242880 | tf_op jit(solution)/shard_map/all_gather | solution.py:790
  180.2 62.6 %all-to-all-start = ((bf16[4,256,1024]{2,1,0:T(8,128)(2,1)}), bf16[4,256,1024]{2,1,0:T(8,128)(2,1)S(1)}, u32[]{:S(2)}, u32[]{:S(2)}) async-start(bf16[4,256,1024]{2,1,0:T(8,128)(2,1)} %bitcast.70), calls=%async_computation | async-start | bytes 4194304 | tf_op jit(solution)/shard_map/all_to_all | solution.py:801
  242.8 1.3 copy-start.3
  269.6 88.0 %all-to-all-start.1 = ((bf16[4,256,1024]{2,1,0:T(8,128)(2,1)}), bf16[4,256,1024]{2,1,0:T(8,128)(2,1)S(1)}, u32[]{:S(2)}, u32[]{:S(2)}) async-start(bf16[4,256,1024]{2,1,0:T(8,128)(2,1)} %get-tuple-element.50), calls=%async_computation.1 | async-start | bytes 4194304 | tf_op jit(solution)/shard_map/all_to_all | solution.py:803
  273.2 173.7 %reduce-scatter.5.cloned.1.call-start = ((), (), s32[]{:S(2)}) async-start(), calls=%async_computation.6 | async-start | bytes 2621440 | tf_op jit(solution)/shard_map/reduce_scatter | solution.py:806
  357.6 1.3 copy-start.2
  357.6 235.3 %reduce-scatter.3.cloned.1.call-start = ((), (), s32[]{:S(2)}) async-start(), calls=%async_computation.5 | async-start | bytes 5242880 | tf_op jit(solution)/shard_map/reduce_scatter | solution.py:820
  394.3 2.3 copy-start.12
  394.3 2.9 copy-start.18
  397.3 6.8 %copy-start.13 = (bf16[2048,1024]{1,0:T(8,128)(2,1)S(1)}, bf16[2048,1024]{1,0:T(8,128)(2,1)}, u32[]{:S(2)}) copy-start(bf16[2048,1024]{1,0:T(8,128)(2,1)} %xw_ref.1) | copy-start | bytes 12582916
  397.3 6.8 %copy-start.16 = (bf16[1024,1024]{1,0:T(8,128)(2,1)S(1)}, bf16[1024,1024]{1,0:T(8,128)(2,1)}, u32[]{:S(2)}) copy-start(bf16[1024,1024]{1,0:T(8,128)(2,1)} %get-tuple-element.62) | copy-start | bytes 6291460
  404.1 6.8 %copy-start.4 = (bf16[2048,256]{1,0:T(8,128)(2,1)S(1)}, bf16[2048,256]{1,0:T(8,128)(2,1)}, u32[]{:S(2)}) copy-start(bf16[2048,256]{1,0:T(8,128)(2,1)} %bcw_ref.1) | copy-start | bytes 3145732
  421.3 3.2 copy-start.9
  421.3 3.3 copy-start.7
  421.3 3.3 copy-start.5
  424.5 3.9 copy-start.8
  424.5 3.9 copy-start.10
  429.4 5.0 copy-start
  429.4 5.0 copy-start.19
  434.4 6.2 %copy-start.17 = (bf16[1024,1024]{1,0:T(8,128)(2,1)S(1)}, bf16[1024,1024]{1,0:T(8,128)(2,1)}, u32[]{:S(2)}) copy-start(bf16[1024,1024]{1,0:T(8,128)(2,1)} %get-tuple-element.62) | copy-start | bytes 6291460
  581.1 11.9 %copy-start.1 = (bf16[1,256,2048]{2,1,0:T(8,128)(2,1)S(1)}, bf16[1,256,2048]{2,1,0:T(8,128)(2,1)}, u32[]{:S(2)}) copy-start(bf16[1,256,2048]{2,1,0:T(8,128)(2,1)} %param.14) | copy-start | bytes 3145732
Sparse Core Ops, SparseCore 0:
  11.5 123.5 all-gather.1
  357.8 44.3 reduce-scatter.4
  421.4 77.1 reduce-scatter.2

commit v2 on v1

--- a/solution.py
+++ b/solution.py
@@ -52,104 +52,6 @@
     one = jnp.broadcast_to(values[:, 2 * pair : 2 * pair + 1], shape)
     two = jnp.broadcast_to(values[:, 2 * pair + 1 : 2 * pair + 2], shape)
     return one, two, jnp.where(left, one, two)
-
-
-def forward_kernel(
-    x_ref, zw_ref, xw_ref, bcw_ref, dtw_ref, convw_ref, convb_ref, dtb_ref, alog_ref, skip_ref,
-    gated_ref, gate_ref, scan_ref, conv_ref, inner_ref, bc_ref, step_ref, prev_ref,
-    state, ext, tails,
-):
-    rows_num, channels = gate_ref.shape
-    n = state.shape[0]
-
-    @pl.when(pl.program_id(0) == 0)
-    def _():
-        state[...] = jnp.zeros_like(state)
-        ext[0:8, :] = jnp.zeros((8, channels), F32)
-
-    x = x_ref[...]
-    gate_ref[...] = mm(x, zw_ref[...])
-    ext[8:, :] = mm(x, xw_ref[...])
-    bc_ref[...] = mm(x, bcw_ref[...])
-    step_ref[...] = mm(x, dtw_ref[...])
-    conv = convb_ref[...] + sum(
-        convw_ref[k : k + 1, :] * ext[5 + k : 5 + k + rows_num, :] for k in range(4)
-    )
-    conv_ref[...] = conv
-    inner_ref[...] = ext[8:, :]
-    ext[0:8, :] = ext[rows_num : rows_num + 8, :]
-    rate = -jnp.exp(alog_ref[...])
-    lower = lower_mask((SPAN, SPAN))
-    lower_f = lower.astype(F32)
-    left = lax.broadcasted_iota(jnp.int32, (SPAN, 128), 1) < 64
-
-    def block(at, carry):
-        rows = pl.ds(pl.multiple_of(at * SPAN, SPAN), SPAN)
-        delta = softplus(step_ref[rows, :] + dtb_ref[...])
-        cum = mm_exact(lower_f, delta * rate)
-        cum_t = cum.T
-        b_val = bc_ref[rows, :n].astype(BF16)
-        c_val = bc_ref[rows, n:].astype(BF16)
-        inner = jnp.where(lower, mm_nt(c_val, b_val), 0.0)
-        before = state[...].astype(BF16)
-        prev_ref[at] = before
-        across = mm(c_val, before)
-        for pair in range(channels // 128):
-            cols = slice(pair * 128, pair * 128 + 128)
-            c0, c1, ce = pair_columns(cum, pair, left)
-            _, _, de = pair_columns(delta, pair, left)
-            tot = ce[SPAN - 1 : SPAN, :]
-            conv_p = conv_ref[rows, cols]
-            act = conv_p * sigmoid(conv_p)
-            u = act * de
-            tails[:, cols] = (u * jnp.exp(tot - ce)).astype(BF16)
-            u0 = jnp.where(left, u, 0.0).astype(BF16)
-            u1 = jnp.where(left, 0.0, u).astype(BF16)
-            p0 = (jnp.exp(jnp.minimum(c0 - cum_t[2 * pair : 2 * pair + 1, :], 0.0)) * inner).astype(BF16)
-            p1 = (jnp.exp(jnp.minimum(c1 - cum_t[2 * pair + 1 : 2 * pair + 2, :], 0.0)) * inner).astype(BF16)
-            within = mm(jnp.concatenate([p0, p1], axis=1), jnp.concatenate([u0, u1], axis=0))
-            y = within + across[:, cols] * jnp.exp(ce) + skip_ref[:, cols] * act
-            scan_ref[rows, cols] = y
-            gate = gate_ref[rows, cols]
-            gated_ref[rows, cols] = (y * gate * sigmoid(gate)).astype(BF16)
-            state[:, cols] = state[:, cols] * jnp.exp(tot)
-        state[...] += mm(bc_ref[rows, :n].T.astype(BF16), tails[...])
-        return carry
-
-    lax.fori_loop(0, rows_num // SPAN, block, 0)
-
-
-def forward_call(x, zw, xw, bcw, dtw, convw, convb, dtb, alog, skip):
-    length, model = x.shape
-    channels = zw.shape[1]
-    n = bcw.shape[1] // 2
-    steps = length // ROWS
-    fixed = lambda a: pl.BlockSpec(a.shape, lambda i: (0,) * a.ndim)
-    rows = lambda w: pl.BlockSpec((ROWS, w), lambda i: (i, 0))
-    sub = ROWS // SPAN
-    shapes = (
-        (channels, BF16), (channels, F32), (channels, F32), (channels, F32), (channels, F32),
-        (2 * n, F32), (dtw.shape[1], F32),
-    )
-    return pl.pallas_call(
-        forward_kernel,
-        grid=(steps,),
-        in_specs=[rows(model)] + [fixed(a) for a in (zw, xw, bcw, dtw, convw, convb, dtb, alog, skip)],
-        out_specs=[rows(w) for w, _ in shapes]
-        + [pl.BlockSpec((sub, n, channels), lambda i: (i, 0, 0))],
-        out_shape=[jax.ShapeDtypeStruct((length, w), t) for w, t in shapes]
-        + [jax.ShapeDtypeStruct((length // SPAN, n, channels), BF16)],
-        scratch_shapes=[
-            pltpu.VMEM((n, channels), F32),
-            pltpu.VMEM((ROWS + 8, channels), F32),
-            pltpu.VMEM((SPAN, channels), BF16),
-        ],
-        compiler_params=pltpu.CompilerParams(vmem_limit_bytes=VMEM_BYTES),
-        cost_estimate=pl.CostEstimate(
-            flops=4 * length * model * channels, bytes_accessed=32 * 2**20, transcendentals=length * channels * 8
-        ),
-        name="scan_forward",
-    )(x, zw, xw, bcw, dtw, convw, convb, dtb, alog, skip)
 
 
 def backward_kernel(
@@ -513,31 +415,90 @@
     return [pltpu.VMEM((2,) * (count - 1 - i) + tuple(block), dtype) for i in range(count)]
 
 
-def weights_kernel(w_ref, gain_ref, all_ref, gains_ref, local, send, recv):
-    groups = all_ref.shape[0]
-    count = len(all_ref.shape) - 3
-    part, model = all_ref.shape[-2:]
-    half = model // 2
-    group_bits = log2(groups)
+def front_kernel(
+    count, tok_ref, pre_ref, zw_hbm, xw_hbm, bcw_hbm, dtw_hbm, w_hbm, gain_hbm,
+    convw_ref, convb_ref, dtb_ref, alog_ref, skip_ref,
+    x_out, gate_out, scan_out, conv_out, inner_out, bc_out, step_out, prev_out, gated_out, all_ref, gains_ref,
+    xs, zw, xw, bcw, dtw, gate_s, scan_s, conv_s, inner_s, bc_s, step_s, prev_s, gated_s, state, tails,
+    load_sem, local_sem, store_sem, away_sem, here_sem, send, recv,
+):
+    rows_num, channels = gated_s.shape[1:]
+    groups = gated_s.shape[0]
+    length = groups * rows_num
+    n = state.shape[0]
+    model = tok_ref.shape[1]
+    chunks = 2
+    chunk = rows_num // chunks
     me = lax.axis_index("head")
+    hi, lo = me // 2, me % 2
+    near = partner("head", 0)
+    far = partner("head", 1)
+    others = [near, far, near + far - me]
+    links = Links(send, recv)
+
+    loads = [
+        pltpu.make_async_copy(src, dst, load_sem.at[i])
+        for i, (src, dst) in enumerate(((zw_hbm, zw), (xw_hbm, xw), (bcw_hbm, bcw), (dtw_hbm, dtw)))
+    ]
+    for load in loads:
+        load.start()
+    tok = tok_ref[...].astype(F32)
+    recip = lax.rsqrt(jnp.mean(tok * tok, axis=-1, keepdims=True) + EPSILON)
+    xs[hi, lo] = (tok * recip * pre_ref[...]).astype(BF16)
+    meet([("head", z) for z in others] + [("batch", partner("batch", b)) for b in range(count)])
+
+    own_rows = xs.at[hi, lo]
+    to_far = []
+    for c in range(chunks):
+        part = xs.at[hi, lo, pl.ds(c * chunk, chunk)]
+        to_far.append(links.copy(part, part, "head", far))
+        to_far[-1].start()
+    to_near = links.copy(own_rows, own_rows, "head", near)
+    to_near.start()
     mine = bits_of("batch", count)
-    others = [me + sum((1 - 2 * ((me // 2**b) % 2)) * 2**b for b in range(group_bits) if k & 2**b) for k in range(1, groups)]
-    links = Links(send, recv)
-    meet([("head", z) for z in others] + [("batch", partner("batch", b)) for b in range(count)])
     own = place(count, dict(enumerate(mine)))
-    own_copy = pltpu.make_async_copy(w_ref, all_ref.at[me], local.at[0])
-    own_copy.start()
-    gain_copy = pltpu.make_async_copy(gain_ref, gains_ref.at[me], local.at[1])
-    gain_copy.start()
-    gain_sends = []
-    for z in others:
-        gain_sends.append(links.copy(gain_ref, gains_ref.at[me], "head", z))
-        gain_sends[-1].start()
-    up = list(range(1, count))
-
-    def stream(z, cols, order):
+    keep = [pltpu.make_async_copy(w_hbm, all_ref.at[me], local_sem.at[0])]
+    keep.append(pltpu.make_async_copy(gain_hbm, gains_ref.at[me], local_sem.at[1]))
+    for item in keep:
+        item.start()
+    inner_s[0:8, :] = jnp.zeros((8, channels), F32)
+    state[...] = jnp.zeros_like(state)
+    for load in loads:
+        load.wait()
+
+    def project(at_hi, at_lo):
+        first = pl.multiple_of((2 * at_hi + at_lo) * rows_num, rows_num)
+        rows = pl.ds(first, rows_num)
+        inner_rows = pl.ds(pl.multiple_of(first + 8, 8), rows_num)
+        tile = 256
+
+        def columns(t, carry):
+            cols = pl.ds(pl.multiple_of(t * tile, tile), tile)
+            x = xs[at_hi, at_lo]
+            gate_s[rows, cols] = mm(x, zw[:, cols])
+            inner_s[inner_rows, cols] = mm(x, xw[:, cols])
+            return carry
+
+        lax.fori_loop(0, channels // tile, columns, 0)
+        x = xs[at_hi, at_lo]
+        bc_s[rows, :] = mm(x, bcw[...])
+        step_s[rows, :] = mm(x, dtw[...])
+
+    project(hi, lo)
+    to_near.wait()
+    project(hi, 1 - lo)
+    onward = []
+    for c in range(chunks):
+        to_far[c].wait()
+        part = xs.at[1 - hi, lo, pl.ds(c * chunk, chunk)]
+        onward.append(links.copy(part, part, "head", near))
+        onward[-1].start()
+
+    half = w_hbm.shape[-1] // 2
+
+    def pieces(z, cols, order):
         copy = links.copy(
-            w_ref.at[own + (slice(None), cols)], all_ref.at[(me,) + own + (slice(None), cols)], "head", z
+            w_hbm.at[own + (slice(None), cols)], all_ref.at[(me,) + own + (slice(None), cols)], "head", z
         )
         copy.start()
         yield
@@ -551,41 +512,181 @@
             step.wait()
             fixed = {k: v for k, v in fixed.items() if k != b}
 
+    up = list(range(1, count))
     streams = []
     for z in others:
-        streams.append(stream(z, pl.ds(0, half), up + [0]))
-        streams.append(stream(z, pl.ds(half, half), up[::-1] + [0]))
+        streams.append(pieces(z, pl.ds(0, half), up + [0]))
+        streams.append(pieces(z, pl.ds(half, half), up[::-1] + [0]))
+    for s in streams:
+        next(s)
+    gain_sends = [links.copy(gain_hbm, gains_ref.at[me], "head", z) for z in others]
+    for item in gain_sends:
+        item.start()
+
+    project(1 - hi, lo)
+    for item in onward:
+        item.wait()
+    project(1 - hi, 1 - lo)
+
+    rate = -jnp.exp(alog_ref[...])
+    lower = lower_mask((SPAN, SPAN))
+    lower_f = lower.astype(F32)
+    left = lax.broadcasted_iota(jnp.int32, (SPAN, 128), 1) < 64
+
+    def block(at, carry):
+        first = pl.multiple_of(at * SPAN, SPAN)
+        rows = pl.ds(first, SPAN)
+        delta = softplus(step_s[rows, :] + dtb_ref[...])
+        cum = mm_exact(lower_f, delta * rate)
+        cum_t = cum.T
+        b_val = bc_s[rows, :n].astype(BF16)
+        c_val = bc_s[rows, n:].astype(BF16)
+        inner = jnp.where(lower, mm_nt(c_val, b_val), 0.0)
+        before = state[...].astype(BF16)
+        prev_s[at] = before
+        across = mm(c_val, before)
+        quarter = at // (rows_num // SPAN)
+        sub = pl.ds(pl.multiple_of((at % (rows_num // SPAN)) * SPAN, SPAN), SPAN)
+        for pair in range(channels // 128):
+            cols = slice(pair * 128, pair * 128 + 128)
+            c0, c1, ce = pair_columns(cum, pair, left)
+            _, _, de = pair_columns(delta, pair, left)
+            tot = ce[SPAN - 1 : SPAN, :]
+            window = inner_s[pl.ds(first, SPAN + 8), cols]
+            conv_p = convb_ref[:, cols] + sum(
+                convw_ref[k : k + 1, cols] * window[5 + k : 5 + k + SPAN] for k in range(4)
+            )
+            conv_s[rows, cols] = conv_p
+            act = conv_p * sigmoid(conv_p)
+            u = act * de
+            tails[:, cols] = (u * jnp.exp(tot - ce)).astype(BF16)
+            u0 = jnp.where(left, u, 0.0).astype(BF16)
+            u1 = jnp.where(left, 0.0, u).astype(BF16)
+            p0 = (jnp.exp(jnp.minimum(c0 - cum_t[2 * pair : 2 * pair + 1, :], 0.0)) * inner).astype(BF16)
+            p1 = (jnp.exp(jnp.minimum(c1 - cum_t[2 * pair + 1 : 2 * pair + 2, :], 0.0)) * inner).astype(BF16)
+            within = mm(jnp.concatenate([p0, p1], axis=1), jnp.concatenate([u0, u1], axis=0))
+            y = within + across[:, cols] * jnp.exp(ce) + skip_ref[:, cols] * act
+            scan_s[rows, cols] = y
+            gate = gate_s[rows, cols]
+            gated_s[quarter, sub, cols] = (y * gate * sigmoid(gate)).astype(BF16)
+            state[:, cols] = state[:, cols] * jnp.exp(tot)
+        state[...] += mm(bc_s[rows, :n].T.astype(BF16), tails[...])
+        return carry
+
+    def leave(q):
+        return pltpu.make_async_remote_copy(
+            src_ref=gated_s.at[q], dst_ref=gated_out.at[me], send_sem=away_sem.at[q], recv_sem=here_sem.at[me],
+            device_id={"head": q}, device_id_type=pl.DeviceIdType.MESH,
+        )
+
+    def arrive(q):
+        return pltpu.make_async_remote_copy(
+            src_ref=gated_s.at[q], dst_ref=gated_out.at[q], send_sem=away_sem.at[q], recv_sem=here_sem.at[q],
+            device_id={"head": q}, device_id_type=pl.DeviceIdType.MESH,
+        )
+
+    subs = rows_num // SPAN
+
+    def stores(q):
+        rows = pl.ds(pl.multiple_of(q * rows_num, rows_num), rows_num)
+        inner_rows = pl.ds(pl.multiple_of(q * rows_num + 8, 8), rows_num)
+        pairs = (
+            (xs.at[q // 2, q % 2], x_out.at[rows]),
+            (gate_s.at[rows], gate_out.at[rows]),
+            (scan_s.at[rows], scan_out.at[rows]),
+            (conv_s.at[rows], conv_out.at[rows]),
+            (inner_s.at[inner_rows], inner_out.at[rows]),
+            (bc_s.at[rows], bc_out.at[rows]),
+            (step_s.at[rows], step_out.at[rows]),
+            (prev_s.at[pl.ds(q * subs, subs)], prev_out.at[pl.ds(q * subs, subs)]),
+        )
+        return [pltpu.make_async_copy(src, dst, store_sem.at[i, q]) for i, (src, dst) in enumerate(pairs)]
+
+    def quarter_step(q, carry):
+        lax.fori_loop(q * subs, (q + 1) * subs, block, 0)
+
+        @pl.when(q != me)
+        def _():
+            leave(q).start()
+
+        for item in stores(q):
+            item.start()
+        return carry
+
+    lax.fori_loop(0, groups, quarter_step, 0)
+    stay = pltpu.make_async_copy(gated_s.at[me], gated_out.at[me], local_sem.at[2])
+    stay.start()
     run_streams(streams)
-    for c in gain_sends:
-        c.wait()
-    own_copy.wait()
-    gain_copy.wait()
-
-
-def weights_call(out_weight, norm_gain, groups, batches):
-    channels, model = out_weight.shape
+    for item in gain_sends:
+        item.wait()
+    for item in keep:
+        item.wait()
+    stay.wait()
+
+    def finish(q, carry):
+        @pl.when(q != me)
+        def _():
+            leave(q).wait_send()
+            arrive(q).wait_recv()
+
+        for item in stores(q):
+            item.wait()
+        return carry
+
+    lax.fori_loop(0, groups, finish, 0)
+
+
+def front_call(tokens, pre_gain, zw, xw, bcw, dtw, out_weight, norm_gain, convw, convb, dtb, alog, skip, groups, batches):
+    rows_num, model = tokens.shape
+    channels = zw.shape[1]
+    n = bcw.shape[1] // 2
+    length = rows_num * groups
     count = log2(batches)
     part = channels // batches
-    copies = (groups - 1) * (1 + 2 * (1 + count))
+    copies = 3 + 2 + (groups - 1) * (1 + 2 * (1 + count))
     hbm = pl.BlockSpec(memory_space=pl.ANY)
-    w_all, gains = pl.pallas_call(
-        weights_kernel,
-        in_specs=[hbm, hbm],
-        out_specs=[hbm, hbm],
-        out_shape=[
-            jax.ShapeDtypeStruct((groups,) + (2,) * count + (part, model), BF16),
-            jax.ShapeDtypeStruct((groups, 8, channels), F32),
-        ],
+    vmem = pl.BlockSpec(memory_space=pltpu.VMEM)
+    wide = jax.ShapeDtypeStruct((length, channels), F32)
+    outs = [
+        jax.ShapeDtypeStruct((length, model), BF16), wide, wide, wide, wide,
+        jax.ShapeDtypeStruct((length, 2 * n), F32),
+        jax.ShapeDtypeStruct((length, dtw.shape[1]), F32),
+        jax.ShapeDtypeStruct((length // SPAN, n, channels), BF16),
+        jax.ShapeDtypeStruct((groups, rows_num, channels), BF16),
+        jax.ShapeDtypeStruct((groups,) + (2,) * count + (part, model), BF16),
+        jax.ShapeDtypeStruct((groups, 8, channels), F32),
+    ]
+    dma = pltpu.SemaphoreType.DMA
+    result = pl.pallas_call(
+        functools.partial(front_kernel, count),
+        in_specs=[vmem, vmem] + [hbm] * 6 + [vmem] * 5,
+        out_specs=[hbm] * len(outs),
+        out_shape=outs,
         scratch_shapes=[
-            pltpu.SemaphoreType.DMA((2,)), pltpu.SemaphoreType.DMA((copies,)), pltpu.SemaphoreType.DMA((copies,)),
+            pltpu.VMEM((2, 2, rows_num, model), BF16),
+            pltpu.VMEM(zw.shape, BF16), pltpu.VMEM(xw.shape, BF16),
+            pltpu.VMEM(bcw.shape, BF16), pltpu.VMEM(dtw.shape, BF16),
+            pltpu.VMEM((length, channels), F32), pltpu.VMEM((length, channels), F32),
+            pltpu.VMEM((length, channels), F32), pltpu.VMEM((length + 8, channels), F32),
+            pltpu.VMEM((length, 2 * n), F32), pltpu.VMEM((length, dtw.shape[1]), F32),
+            pltpu.VMEM((length // SPAN, n, channels), BF16),
+            pltpu.VMEM((groups, rows_num, channels), BF16),
+            pltpu.VMEM((n, channels), F32), pltpu.VMEM((SPAN, channels), BF16),
+            dma((4,)), dma((3,)), dma((8, groups)), dma((groups,)), dma((groups,)), dma((copies,)), dma((copies,)),
         ],
         compiler_params=pltpu.CompilerParams(
             collective_id=1, has_side_effects=True, vmem_limit_bytes=VMEM_BYTES
         ),
-        cost_estimate=pl.CostEstimate(flops=0, bytes_accessed=300 * 2**20, transcendentals=0),
-        name="gather_weights",
-    )(out_weight.reshape((2,) * count + (part, model)), jnp.broadcast_to(norm_gain[None], (8, channels)))
-    return w_all.reshape(groups, channels, model), gains[:, :1]
+        cost_estimate=pl.CostEstimate(
+            flops=4 * length * model * channels, bytes_accessed=400 * 2**20, transcendentals=0
+        ),
+        name="front",
+    )(
+        tokens, pre_gain[None], zw, xw, bcw, dtw, out_weight.reshape((2,) * count + (part, model)),
+        jnp.broadcast_to(norm_gain[None], (8, channels)), convw, convb, dtb, alog, skip,
+    )
+    x, gate, scan, conv, inner, bc, step, prev, gated, w_all, gains = result
+    return x, gate, scan, conv, inner, bc, step, prev, gated, w_all.reshape(groups, channels, model), gains[:, :1]
 
 
 def outgrad_scatter_kernel(count, gg_ref, dy_ref, out_ref, *refs):
@@ -786,19 +887,14 @@
     heads = dt_weight.shape[1]
     tokens_f = tokens.astype(F32)
     recip_in = lax.rsqrt(jnp.mean(tokens_f * tokens_f, axis=-1, keepdims=True) + EPSILON)
-    normed = (tokens_f * recip_in * pre_gain).astype(BF16)
-    x = lax.all_gather(normed, "head", axis=0, tiled=True)
-    w_all, gain_all = weights_call(out_weight, norm_gain, groups, batches)
-    x, w_all = lax.optimization_barrier((x, w_all))
-
     pad = lambda v: jnp.pad(v, ((0, 0), (0, 128 - heads)))
     dtb = pad(dt_bias[None])
     alog = pad(a_log[None])
     skip_r = skip[None]
-    gated, gate, scan, conv, inner, bc, step, prev = forward_call(
-        x, z_weight, x_weight, bc_weight, pad(dt_weight), conv_weight, conv_bias[None], dtb, alog, skip_r
-    )
-    gated = lax.all_to_all(gated.reshape(groups, own_len, channels), "head", 0, 0, tiled=True)
+    x, gate, scan, conv, inner, bc, step, prev, gated, w_all, gain_all = front_call(
+        tokens, pre_gain, z_weight, x_weight, bc_weight, pad(dt_weight), out_weight, norm_gain,
+        conv_weight, conv_bias[None], dtb, alog, skip_r, groups, batches,
+    )
     outputs, d_gated, dy, gg, gain_grad = middle_call(gated, w_all, gain_all, tokens, cot)
     d_gated = lax.all_to_all(d_gated, "head", 0, 0, tiled=True).reshape(groups * own_len, channels)
     out_part = outgrad_scatter_call(gg, dy, batches)

time: 612 us -> 572 us (0.935)
  waiting for transfers between devices: 47.3 us -> 0.04 us
  Pallas kernels: 426 us -> 444 us
  starting transfers between devices: 18 us -> 4.31 us
    all_to_all x1 -> x0, waiting for transfers between devices: 47.2 us -> none  [per_device(): lax.all_to_all(gated.reshape(groups, own_len, channels), 'head', 0, 0, ti...]
    pallas_call x2 -> x1, Pallas kernels: 166 us -> 184 us  [front_call(): pl.pallas_call(functools.partial(front_kernel, count), in_specs=[vmem, vm...]
    all_to_all x1 -> x0, starting transfers between devices: 13.9 us -> none  [per_device(): lax.all_to_all(gated.reshape(groups, own_len, channels), 'head', 0, 0, ti...]
  transfers between devices with their start and end apart: 5 -> 3, of which waited for: 1 -> 0; matrix products, arithmetic and copies ran while one was open for 14% -> 15% of each run, Pallas kernels for 61% -> 42%
where the time goes in v2:
time: 572 us; the launch traced here: 562 us
  Pallas kernels  444 us (78%)
  matrix products  47 us (8%)
  other arithmetic  30.7 us (5%)
  local copies, waits for them, and re-layouts  21 us (4%)
  between operations  14.6 us (3%)
    pallas_call x1, Pallas kernels, front_call(): pl.pallas_call(functools.partial(front_kernel, count), in_specs=[vmem, vm...  184 us
    pallas_call x1, Pallas kernels, tail_call(): pl.pallas_call(functools.partial(tail_kernel, count, group_bits), in_spec...  115 us
    pallas_call x1, Pallas kernels, outgrad_scatter_call(): pl.pallas_call(functools.partial(outgrad_scatter_kernel, count), in_specs...  84.2 us
    pallas_call x1, Pallas kernels, backward_call(): pl.pallas_call(backward_kernel, grid=(steps,), in_specs=[rows(a.shape[1])...  35.2 us
    pallas_call x1, Pallas kernels, middle_call(): pl.pallas_call(middle_kernel, out_shape=[jax.ShapeDtypeStruct((4, rows_nu...  25.4 us
    dot_general x3, matrix products, mm_nt(): lax.dot_general(a, b, (((1,), (1,)), ((), ())), preferred_element_type=F32)  23.8 us
    convert_element_type x3, other arithmetic, per_device(): v.astype(F32)  21.2 us
    dot_general x3, matrix products, mm_tn(): lax.dot_general(a, b, (((0,), (0,)), ((), ())), preferred_element_type=F32)  17.4 us
  transfers between devices with their start and end apart: 3, of which 0 were waited for; matrix products, arithmetic and copies ran while one was open for 15% of the time, Pallas kernels for 42%

profile of v2, /device:TPU:0, one launch (start us, length us, event | category | flops | bytes accessed | tf_op | source)
XLA Modules:
  0.0 562.0 jit_solution(4940083122547517703)
XLA Ops:
  7.2 1.2 pad.20.dtb_ref
  8.4 1.2 pad.21.alog_ref
  9.5 1.1 copy.31
  11.5 1.3 broadcast_in_dim.34.gain_hbm
  12.8 184.2 %front.1 = (bf16[1024,2048]{1,0:T(8,128)(2,1)}, f32[1024,1024]{1,0:T(8,128)}, f32[1024,1024]{1,0:T(8,128)}, f32[1024,1024]{1,0:T(8,128)}, f32[1024,1024]{1,0:T(8...) custom-call(bf16[256,2048]{1,0:T(8,128)(2,1)} %bitcast.65, ...), custom_call_target="tpu_custom_call" | custom-call | flops 8589934592 | bytes 419430400 | tf_op jit(solution)/shard_map/front/pallas_call | solution.py:660
  197.0 1.5 slice.43.gain_ref
  198.5 25.4 %nested_norm.1 = (bf16[4,256,2048]{2,1,0:T(8,128)(2,1)}, bf16[4,256,1024]{2,1,0:T(8,128)(2,1)}, bf16[4,256,2048]{2,1,0:T(8,128)(2,1)}, bf16[4,256,1024]{2,1,0:T(8,128)(2,1)}, f32[4,1,1024]{2,1,0:T(1,128)}) custom-call(bf16[4,256,1024]{2,1,0:T(8,128)(2,1)} %get-tuple-element.43.g_ref, bf16[4,1024,2048]{2,1,0:T(8,128)(2,1)} %bitcast.84, ...), custom_call_target="tpu_custom_call" | custom-call | flops 8589934592 | bytes 37748736 | tf_op jit(solution)/shard_map/nested_norm/pallas_call | solution.py:292
  224.0 3.6 all-to-all-start
  227.9 84.2 %out_weight_grad.1 = bf16[4,128,2048]{2,1,0:T(8,128)(2,1)} custom-call(bf16[4,256,1024]{2,1,0:T(8,128)(2,1)} %get-tuple-element.48.gg_ref, bf16[4,256,2048]{2,1,0:T(8,128)(2,1)} %get-tuple-element.49.dy_ref), custom_call_target="tpu_custom_call" | custom-call | flops 4294967296 | bytes 209715200 | tf_op jit(solution)/shard_map/out_weight_grad/pallas_call | solution.py:727
  313.4 35.2 %scan_backward.1 = (bf16[1024,1024]{1,0:T(8,128)(2,1)}, bf16[1024,1024]{1,0:T(8,128)(2,1)}, f32[1024,256]{1,0:T(8,128)}, f32[16,1024]{1,0:T(8,128)}, f32[8,1024]{1,0:T(8,128)}, /*index=5*/f32[32,128]{1,0:T(8,128)}) custom-call(bf16[1024,1024]{1,0:T(8,128)(2,1)} %bitcast.68, f32[1024,1024]{1,0:T(8,128)} %get-tuple-element.51.gate_ref, ...), custom_call_target="tpu_custom_call" | custom-call | flops 2147483648 | bytes 31457280 | tf_op jit(solution)/shard_map/scan_backward/pallas_call | solution.py:195
  348.7 2.3 fusion.12
  351.6 6.8 %fusion.18 = f32[1024,2048]{1,0:T(8,128)} fusion(bf16[1024,1024]{1,0:T(8,128)(2,1)S(1)} %copy-done.12, bf16[2048,1024]{1,0:T(8,128)(2,1)S(1)} %copy-done.10), kind=kOutput, calls=%fused_computation.49 | convolution fusion | flops 4294967296 | bytes 14680064 | tf_op jit(solution)/shard_map/dot_general | solution.py:25
  358.4 6.8 %fusion.19 = f32[1024,2048]{1,0:T(8,128)} fusion(bf16[1024,1024]{1,0:T(8,128)(2,1)S(1)} %copy-done.14, bf16[2048,1024]{1,0:T(8,128)(2,1)S(1)} %copy-done.11), kind=kOutput, calls=%fused_computation.50 | convolution fusion | flops 4294967296 | bytes 14680064 | tf_op jit(solution)/shard_map/dot_general | solution.py:25
  365.2 10.2 %multiply_reduce_fusion = (f32[2048]{0:T(1024)S(1)}, bf16[1024,2048]{1,0:T(8,128)(2,1)}) fusion(bf16[1024,2048]{1,0:T(8,128)(2,1)} %get-tuple-element.62, bf16[2048,256]{1,0:T(8,128)(2,1)S(1)} %copy-done.3, f32[1024,256]{1,0:T(8,128)} %get-tuple-element.61, f32[1024,2048]{1,0:T(8,128)S(1)} %fusion.12, f32[1024,2048]{1,0:T(8,128)} %fusion.18, ...), kind=kOutput, calls=%fused_computation | convolution fusion | flops 1090779136 | bytes 35659776 | tf_op jit(solution)/shard_map/dot_general | solution.py:25
  376.1 3.2 convert_reduce_fusion
  379.4 3.5 fusion.10
  384.2 5.0 convolution_convert_fusion.2
  389.2 6.2 %convolution_convert_fusion = bf16[2048,1024]{1,0:T(8,128)(2,1)} fusion(bf16[1024,2048]{1,0:T(8,128)(2,1)S(1)} %copy-done, bf16[1024,1024]{1,0:T(8,128)(2,1)S(1)} %copy-done.15), kind=kOutput, calls=%fused_computation.6 | convolution fusion | flops 4297064448 | bytes 10485760 | tf_op jit(solution)/shard_map/dot_general | solution.py:29
  395.4 6.2 %convolution_convert_fusion.1 = bf16[2048,1024]{1,0:T(8,128)(2,1)} fusion(bf16[1024,2048]{1,0:T(8,128)(2,1)S(1)} %copy-done, bf16[1024,1024]{1,0:T(8,128)(2,1)S(1)} %copy-done.13), kind=kOutput, calls=%fused_computation.7 | convolution fusion | flops 4297064448 | bytes 10485760 | tf_op jit(solution)/shard_map/dot_general | solution.py:29
  401.7 115.4 %sum_grads.1 = (bf16[2,2,2,256,1024]{4,3,2,1,0:T(8,128)(2,1)}, bf16[2,2,2,256,1024]{4,3,2,1,0:T(8,128)(2,1)}, bf16[2,2,2,128,2048]{4,3,2,1,0:T(8,128)(2,1)}, bf1...) custom-call(bf16[2,2,2,256,1024]{4,3,2,1,0:T(8,128)(2,1)} %bitcast.64, bf16[2,2,2,256,1024]{4,3,2,1,0:T(8,128)(2,1)} %bitcast.63, ...), custom_call_target="tpu_custom_call" | custom-call | bytes 314572800 | tf_op jit(solution)/shard_map/sum_grads/pallas_call | solution.py:834
  517.0 1.4 slice.48
  518.4 1.7 slice_bitcast_fusion.1
  520.1 1.4 slice.46
  521.4 1.0 slice.56
  522.5 2.2 copy.34
  524.7 0.9 copy.37
  527.6 1.4 constant_dynamic-slice_fusion
  529.0 2.7 bitcast_convert_fusion.3
  531.7 6.7 %bitcast_convert_fusion = f32[1024,2048]{1,0:T(8,128)} fusion(bf16[2,2,2,128,2048]{4,3,2,1,0:T(8,128)(2,1)} %get-tuple-element.71), kind=kLoop, calls=%fused_computation.3 | loop fusion | flops 2097152 | bytes 12582912 | tf_op jit(solution)/shard_map/convert_element_type | solution.py:935
  538.4 11.8 %bitcast_convert_fusion.1 = (f32[2048,1024]{1,0:T(8,128)}, f32[2048,1024]{1,0:T(8,128)}) fusion(bf16[2,2,2,256,1024]{4,3,2,1,0:T(8,128)(2,1)} %get-tuple-element.68, bf16[2,2,2,256,1024]{4,3,2,1,0:T(8,128)(2,1)} %get-tuple-element.67), kind=kLoop, calls=%fused_computation.4 | loop fusion | flops 4194304 | bytes 25165824 | tf_op jit(solution)/shard_map/convert_element_type | solution.py:935
  550.2 1.8 fusion.4
  552.0 2.9 fusion.6
  (58 shorter events, 7.1 us)
Async XLA Ops:
  224.0 88.1 %all-to-all-start = ((bf16[4,256,1024]{2,1,0:T(8,128)(2,1)}), bf16[4,256,1024]{2,1,0:T(8,128)(2,1)S(1)}, u32[]{:S(2)}, u32[]{:S(2)}) async-start(bf16[4,256,1024]{2,1,0:T(8,128)(2,1)} %get-tuple-element.47), calls=%async_computation | async-start | bytes 4194304 | tf_op jit(solution)/shard_map/all_to_all | solution.py:899
  227.6 174.1 %reduce-scatter.5.cloned.1.call-start = ((), (), s32[]{:S(2)}) async-start(), calls=%async_computation.4 | async-start | bytes 2621440 | tf_op jit(solution)/shard_map/reduce_scatter | solution.py:902
  312.1 1.3 copy-start.2
  312.1 238.1 %reduce-scatter.3.cloned.1.call-start = ((), (), s32[]{:S(2)}) async-start(), calls=%async_computation.3 | async-start | bytes 5242880 | tf_op jit(solution)/shard_map/reduce_scatter | solution.py:916
  313.4 35.3 %copy-start.5 = (bf16[2048,16]{0,1:T(8,128)(2,1)S(1)}, bf16[2048,16]{0,1:T(8,128)(2,1)}, u32[]{:S(2)}) copy-start(bf16[2048,16]{0,1:T(8,128)(2,1)} %param.18) | copy-start | bytes 196612
  348.7 2.3 copy-start.10
  348.7 2.9 copy-start.12
  351.6 6.8 %copy-start.11 = (bf16[2048,1024]{1,0:T(8,128)(2,1)S(1)}, bf16[2048,1024]{1,0:T(8,128)(2,1)}, u32[]{:S(2)}) copy-start(bf16[2048,1024]{1,0:T(8,128)(2,1)} %xw_hbm.1) | copy-start | bytes 12582916
  351.6 6.8 %copy-start.14 = (bf16[1024,1024]{1,0:T(8,128)(2,1)S(1)}, bf16[1024,1024]{1,0:T(8,128)(2,1)}, u32[]{:S(2)}) copy-start(bf16[1024,1024]{1,0:T(8,128)(2,1)} %get-tuple-element.59) | copy-start | bytes 6291460
  358.4 6.8 %copy-start.3 = (bf16[2048,256]{1,0:T(8,128)(2,1)S(1)}, bf16[2048,256]{1,0:T(8,128)(2,1)}, u32[]{:S(2)}) copy-start(bf16[2048,256]{1,0:T(8,128)(2,1)} %bcw_hbm.1) | copy-start | bytes 3145732
  375.4 0.7 copy-start.8
  375.4 3.9 copy-start.6
  375.5 3.9 copy-start.4
  379.3 3.9 copy-start.7
  379.3 3.9 copy-start.9
  384.2 5.0 copy-start
  384.2 5.0 copy-start.15
  389.2 6.2 %copy-start.13 = (bf16[1024,1024]{1,0:T(8,128)(2,1)S(1)}, bf16[1024,1024]{1,0:T(8,128)(2,1)}, u32[]{:S(2)}) copy-start(bf16[1024,1024]{1,0:T(8,128)(2,1)} %get-tuple-element.58) | copy-start | bytes 6291460
  538.3 11.9 %copy-start.1 = (bf16[1,256,2048]{2,1,0:T(8,128)(2,1)S(1)}, bf16[1,256,2048]{2,1,0:T(8,128)(2,1)}, u32[]{:S(2)}) copy-start(bf16[1,256,2048]{2,1,0:T(8,128)(2,1)} %param.14) | copy-start | bytes 3145732
Sparse Core Ops, SparseCore 0:
  312.2 45.2 reduce-scatter.4
  375.6 78.1 reduce-scatter.2

commit v3 on v2

v3 whole, which is shorter than its diff:
```python
import functools
import itertools

import jax
import jax.numpy as jnp
from jax import lax
from jax.experimental import pallas as pl
from jax.experimental.pallas import tpu as pltpu
from jax.sharding import PartitionSpec as P

SPAN = 128
ROWS = 256
EPSILON = 1e-05
BF16 = jnp.bfloat16
F32 = jnp.float32
HIGHEST = lax.Precision.HIGHEST
VMEM_BYTES = 60 * 1024 * 1024
BACK_VMEM_BYTES = 63 * 1024 * 1024


def mm(a, b):
    return lax.dot_general(a, b, (((1,), (0,)), ((), ())), preferred_element_type=F32)


def mm_nt(a, b):
    return lax.dot_general(a, b, (((1,), (1,)), ((), ())), preferred_element_type=F32)


def mm_tn(a, b):
    return lax.dot_general(a, b, (((0,), (0,)), ((), ())), preferred_element_type=F32)


def mm_exact(a, b):
    return lax.dot_general(
        a, b, (((1,), (0,)), ((), ())), preferred_element_type=F32, precision=HIGHEST
    )


def lower_mask(shape):
    return lax.broadcasted_iota(jnp.int32, shape, 0) >= lax.broadcasted_iota(jnp.int32, shape, 1)


def softplus(v):
    return jnp.maximum(v, 0.0) + jnp.log1p(jnp.exp(-jnp.abs(v)))


def sigmoid(v):
    return 1.0 / (1.0 + jnp.exp(-v))


def pair_columns(values, pair, left):
    shape = (SPAN, 128)
    one = jnp.broadcast_to(values[:, 2 * pair : 2 * pair + 1], shape)
    two = jnp.broadcast_to(values[:, 2 * pair + 1 : 2 * pair + 2], shape)
    return one, two, jnp.where(left, one, two)


def segments(channels):
    ends = [channels * 2**w // 8 for w in range(4)]
    return list(zip([0] + ends[:-1], ends))


def middle_kernel(g_ref, w_ref, gain_ref, tok_ref, cot_ref, out_ref, dg_ref, dy_ref, gg_ref, ggrad_ref):
    groups, rows_num, channels = g_ref.shape
    model = tok_ref.shape[1]
    segs = segments(channels)
    sums = [jnp.zeros((rows_num, 1), F32) for _ in segs]
    for j in range(groups):
        g = g_ref[j].astype(F32)
        gg_ref[j] = (g * gain_ref[j]).astype(BF16)
        for w, (lo, hi) in enumerate(segs):
            sums[w] += jnp.sum(g[:, lo:hi] * g[:, lo:hi], axis=1, keepdims=True)
    recips = []
    total = jnp.zeros((rows_num, 1), F32)
    for w, (lo, hi) in enumerate(segs):
        total = total + sums[w]
        recips.append(lax.rsqrt(total / (hi * groups) + EPSILON))
    tile = 512

    def forward(at, dots):
        cols = pl.ds(pl.multiple_of(at * tile, tile), tile)
        acc = jnp.zeros((rows_num, tile), F32)
        tok = tok_ref[:, cols].astype(F32)
        new = []
        for w, (lo, hi) in enumerate(segs):
            acc += mm(
                jnp.concatenate([gg_ref[j, :, lo:hi] for j in range(groups)], axis=1),
                jnp.concatenate([w_ref[j, lo:hi, cols] for j in range(groups)], axis=0),
            )
            out_ref[w, :, cols] = (tok + recips[w] * acc).astype(BF16)
            new.append(dots[w] + jnp.sum(cot_ref[w, :, cols].astype(F32) * acc, axis=1, keepdims=True))
        combined = jnp.zeros((rows_num, tile), F32)
        for w in reversed(range(4)):
            combined += recips[w] * cot_ref[w, :, cols].astype(F32)
            dy_ref[w, :, cols] = combined.astype(BF16)
        return tuple(new)

    dots = lax.fori_loop(
        0, model // tile, forward, tuple(jnp.zeros((rows_num, 1), F32) for _ in segs)
    )
    scales = [None] * 4
    scale = jnp.zeros((rows_num, 1), F32)
    for w in reversed(range(4)):
        scale = scale + recips[w] ** 3 * dots[w] / (segs[w][1] * groups)
        scales[w] = scale

    def back(j, carry):
        for w, (lo, hi) in enumerate(segs):
            dn = mm_nt(dy_ref[w], w_ref[j, lo:hi, :])
            g = g_ref[j, :, lo:hi].astype(F32)
            ggrad_ref[j, :, lo:hi] = jnp.sum(g * dn, axis=0, keepdims=True)
            dg_ref[j, :, lo:hi] = (gain_ref[j, :, lo:hi] * dn - g * scales[w]).astype(BF16)
        return carry

    lax.fori_loop(0, groups, back, 0)


def middle_call(g, w_all, gain, tok, cot):
    groups, rows_num, channels = g.shape
    model = tok.shape[1]
    return pl.pallas_call(
        middle_kernel,
        out_shape=[
            jax.ShapeDtypeStruct((4, rows_num, model), BF16),
            jax.ShapeDtypeStruct(g.shape, BF16),
            jax.ShapeDtypeStruct((4, rows_num, model), BF16),
            jax.ShapeDtypeStruct(g.shape, BF16),
            jax.ShapeDtypeStruct((groups, 1, channels), F32),
        ],
        compiler_params=pltpu.CompilerParams(vmem_limit_bytes=VMEM_BYTES),
        cost_estimate=pl.CostEstimate(
            flops=4 * groups * rows_num * channels * model, bytes_accessed=36 * 2**20, transcendentals=0
        ),
        name="nested_norm",
    )(g, w_all, gain, tok, cot)


def partner(axis, bit):
    me = lax.axis_index(axis)
    return me + (1 - 2 * ((me // 2**bit) % 2)) * 2**bit


def bits_of(axis, count):
    me = lax.axis_index(axis)
    return [(me // 2**b) % 2 for b in range(count)]


def log2(value):
    return value.bit_length() - 1


def place(count, fixed):
    return tuple(fixed[b] if b in fixed else slice(None) for b in reversed(range(count)))


class Links:
    def __init__(self, send, recv):
        self.send, self.recv, self.used = send, recv, 0

    def copy(self, src, dst, axis, to):
        at = self.used
        self.used += 1
        return pltpu.make_async_remote_copy(
            src_ref=src, dst_ref=dst, send_sem=self.send.at[at], recv_sem=self.recv.at[at],
            device_id={axis: to}, device_id_type=pl.DeviceIdType.MESH,
        )


def meet(peers):
    barrier = pltpu.get_barrier_semaphore()
    for axis, to in peers:
        pl.semaphore_signal(barrier, inc=1, device_id={axis: to}, device_id_type=pl.DeviceIdType.MESH)
    pl.semaphore_wait(barrier, len(peers))


def add_block(buf, index, slot, at):
    rows = slot.shape[-2]
    step = min(rows, 32)
    index = index + (slice(None),) * (len(buf.shape) - len(index))
    free = [i for i, v in enumerate(index[:-2]) if isinstance(v, slice)]
    full = list(index[:-2])
    for i, v in zip(free, at):
        full[i] = v
    full = tuple(full)

    def piece(r, carry):
        rs = pl.ds(pl.multiple_of(r * step, step), step)
        total = buf[full + (rs, index[-1])].astype(F32) + slot[tuple(at) + (rs, slice(None))].astype(F32)
        buf[full + (rs, index[-1])] = total.astype(buf.dtype)
        return carry

    lax.fori_loop(0, rows // step, piece, 0)


def scatter(links, buf, slots, order, lead=()):
    count = len(order)
    mine = bits_of("batch", count)
    fixed = {}
    for i, b in enumerate(order):
        keep = {**fixed, b: mine[b]}
        copy = links.copy(buf.at[place(count, {**fixed, b: 1 - mine[b]})], slots[i], "batch", partner("batch", b))
        copy.start()
        yield
        copy.wait()
        dims = slots[i].shape[:-2]
        for at in itertools.product(*(range(d) for d in dims)):
            add_block(buf, place(count, keep), slots[i], at)
        fixed = keep


def gather(links, buf, order):
    count = len(order)
    fixed = dict(enumerate(bits_of("batch", count)))
    for b in order:
        at = buf.at[place(count, fixed)]
        copy = links.copy(at, at, "batch", partner("batch", b))
        copy.start()
        yield
        copy.wait()
        fixed = {k: v for k, v in fixed.items() if k != b}


def doubling(links, buf, slots, axis, bits):
    for i, b in enumerate(bits):
        copy = links.copy(buf, slots[i], axis, partner(axis, b))
        copy.start()
        yield
        copy.wait()
        buf[...] = (buf[...].astype(F32) + slots[i][...].astype(F32)).astype(buf.dtype)


def chain(*parts):
    for part in parts:
        yield from part


def run_streams(streams):
    live = list(streams)
    while live:
        live = [s for s in live if next(s, live) is not live]


def halving_slots(count, block, dtype):
    return [pltpu.VMEM((2,) * (count - 1 - i) + tuple(block), dtype) for i in range(count)]


def front_kernel(
    count, tok_ref, pre_ref, zw_hbm, xw_hbm, bcw_hbm, dtw_hbm, w_hbm, gain_hbm,
    convw_ref, convb_ref, dtb_ref, alog_ref, skip_ref,
    x_out, a_out, s_out, act_out, dsc_out, inn_out, bc_out, step_out, prev_out, gated_out, all_ref, gains_ref,
    xs, zw, xw, bcw, dtw, gate_s, a_s, s_s, act_s, dsc_s, inn_s, inner_s, bc_s, bcb_s, step_s, prev_s, gated_s, state, tails,
    load_sem, local_sem, store_sem, away_sem, here_sem, send, recv,
):
    rows_num, channels = gated_s.shape[1:]
    groups = gated_s.shape[0]
    length = groups * rows_num
    n = state.shape[0]
    model = tok_ref.shape[1]
    chunks = 2
    chunk = rows_num // chunks
    me = lax.axis_index("head")
    hi, lo = me // 2, me % 2
    near = partner("head", 0)
    far = partner("head", 1)
    others = [near, far, near + far - me]
    links = Links(send, recv)

    loads = [
        pltpu.make_async_copy(src, dst, load_sem.at[i])
        for i, (src, dst) in enumerate(((zw_hbm, zw), (xw_hbm, xw), (bcw_hbm, bcw), (dtw_hbm, dtw)))
    ]
    for load in loads:
        load.start()
    tok = tok_ref[...].astype(F32)
    recip = lax.rsqrt(jnp.mean(tok * tok, axis=-1, keepdims=True) + EPSILON)
    xs[hi, lo] = (tok * recip * pre_ref[...]).astype(BF16)
    meet([("head", z) for z in others] + [("batch", partner("batch", b)) for b in range(count)])

    own_rows = xs.at[hi, lo]
    to_far = []
    for c in range(chunks):
        part = xs.at[hi, lo, pl.ds(c * chunk, chunk)]
        to_far.append(links.copy(part, part, "head", far))
        to_far[-1].start()
    to_near = links.copy(own_rows, own_rows, "head", near)
    to_near.start()
    mine = bits_of("batch", count)
    own = place(count, dict(enumerate(mine)))
    keep = [pltpu.make_async_copy(w_hbm, all_ref.at[me], local_sem.at[0])]
    keep.append(pltpu.make_async_copy(gain_hbm, gains_ref.at[me], local_sem.at[1]))
    for item in keep:
        item.start()
    inner_s[0:8, :] = jnp.zeros((8, channels), F32)
    state[...] = jnp.zeros_like(state)
    for load in loads:
        load.wait()

    def project(at_hi, at_lo):
        first = pl.multiple_of((2 * at_hi + at_lo) * rows_num, rows_num)
        rows = pl.ds(first, rows_num)
        inner_rows = pl.ds(pl.multiple_of(first + 8, 8), rows_num)
        tile = 256

        def columns(t, carry):
            cols = pl.ds(pl.multiple_of(t * tile, tile), tile)
            x = xs[at_hi, at_lo]
            gate_s[rows, cols] = mm(x, zw[:, cols])
            inner_s[inner_rows, cols] = mm(x, xw[:, cols])
            return carry

        lax.fori_loop(0, channels // tile, columns, 0)
        x = xs[at_hi, at_lo]
        bc_s[rows, :] = mm(x, bcw[...])
        step_s[rows, :] = mm(x, dtw[...])

    project(hi, lo)
    to_near.wait()
    project(hi, 1 - lo)
    onward = []
    for c in range(chunks):
        to_far[c].wait()
        part = xs.at[1 - hi, lo, pl.ds(c * chunk, chunk)]
        onward.append(links.copy(part, part, "head", near))
        onward[-1].start()

    half = w_hbm.shape[-1] // 2

    def pieces(z, cols, order):
        copy = links.copy(
            w_hbm.at[own + (slice(None), cols)], all_ref.at[(me,) + own + (slice(None), cols)], "head", z
        )
        copy.start()
        yield
        copy.wait()
        fixed = dict(enumerate(mine))
        for b in order:
            at = all_ref.at[(z,) + place(count, fixed) + (slice(None), cols)]
            step = links.copy(at, at, "batch", partner("batch", b))
            step.start()
            yield
            step.wait()
            fixed = {k: v for k, v in fixed.items() if k != b}

    up = list(range(1, count))
    streams = []
    for z in others:
        streams.append(pieces(z, pl.ds(0, half), up + [0]))
        streams.append(pieces(z, pl.ds(half, half), up[::-1] + [0]))
    for s in streams:
        next(s)
    gain_sends = [links.copy(gain_hbm, gains_ref.at[me], "head", z) for z in others]
    for item in gain_sends:
        item.start()

    project(1 - hi, lo)
    for item in onward:
        item.wait()
    project(1 - hi, 1 - lo)

    rate = -jnp.exp(alog_ref[...])
    lower = lower_mask((SPAN, SPAN))
    lower_f = lower.astype(F32)
    left = lax.broadcasted_iota(jnp.int32, (SPAN, 128), 1) < 64

    def block(at, carry):
        first = pl.multiple_of(at * SPAN, SPAN)
        rows = pl.ds(first, SPAN)
        delta = softplus(step_s[rows, :] + dtb_ref[...])
        cum = mm_exact(lower_f, delta * rate)
        cum_t = cum.T
        bcb_s[rows, :] = bc_s[rows, :].astype(BF16)
        b_val = bcb_s[rows, :n]
        c_val = bcb_s[rows, n:]
        inner = jnp.where(lower, mm_nt(c_val, b_val), 0.0)
        before = state[...].astype(BF16)
        prev_s[at] = before
        across = mm(c_val, before)
        quarter = at // (rows_num // SPAN)
        sub = pl.ds(pl.multiple_of((at % (rows_num // SPAN)) * SPAN, SPAN), SPAN)
        for pair in range(channels // 128):
            cols = slice(pair * 128, pair * 128 + 128)
            c0, c1, ce = pair_columns(cum, pair, left)
            _, _, de = pair_columns(delta, pair, left)
            tot = ce[SPAN - 1 : SPAN, :]
            window = inner_s[pl.ds(first, SPAN + 8), cols]
            conv_p = convb_ref[:, cols] + sum(
                convw_ref[k : k + 1, cols] * window[5 + k : 5 + k + SPAN] for k in range(4)
            )
            inn_s[rows, cols] = window[8:].astype(BF16)
            sc = sigmoid(conv_p)
            act = conv_p * sc
            act_s[rows, cols] = act.astype(BF16)
            dsc_s[rows, cols] = (sc + act * (1.0 - sc)).astype(BF16)
            u = act * de
            tails[:, cols] = (u * jnp.exp(tot - ce)).astype(BF16)
            u0 = jnp.where(left, u, 0.0).astype(BF16)
            u1 = jnp.where(left, 0.0, u).astype(BF16)
            p0 = (jnp.exp(jnp.minimum(c0 - cum_t[2 * pair : 2 * pair + 1, :], 0.0)) * inner).astype(BF16)
            p1 = (jnp.exp(jnp.minimum(c1 - cum_t[2 * pair + 1 : 2 * pair + 2, :], 0.0)) * inner).astype(BF16)
            within = mm(jnp.concatenate([p0, p1], axis=1), jnp.concatenate([u0, u1], axis=0))
            y = within + across[:, cols] * jnp.exp(ce) + skip_ref[:, cols] * act
            gate = gate_s[rows, cols]
            sg = sigmoid(gate)
            sl = gate * sg
            s_s[rows, cols] = sl.astype(BF16)
            a_s[rows, cols] = (y * (sg + sl * (1.0 - sg))).astype(BF16)
            gated_s[quarter, sub, cols] = (y * sl).astype(BF16)
            state[:, cols] = state[:, cols] * jnp.exp(tot)
        state[...] += mm(bc_s[rows, :n].T.astype(BF16), tails[...])
        return carry

    def leave(q):
        return pltpu.make_async_remote_copy(
            src_ref=gated_s.at[q], dst_ref=gated_out.at[me], send_sem=away_sem.at[q], recv_sem=here_sem.at[me],
            device_id={"head": q}, device_id_type=pl.DeviceIdType.MESH,
        )

    def arrive(q):
        return pltpu.make_async_remote_copy(
            src_ref=gated_s.at[q], dst_ref=gated_out.at[q], send_sem=away_sem.at[q], recv_sem=here_sem.at[q],
            device_id={"head": q}, device_id_type=pl.DeviceIdType.MESH,
        )

    subs = rows_num // SPAN

    def stores(q):
        rows = pl.ds(pl.multiple_of(q * rows_num, rows_num), rows_num)
        pairs = (
            (xs.at[q // 2, q % 2], x_out.at[rows]),
            (a_s.at[rows], a_out.at[rows]),
            (s_s.at[rows], s_out.at[rows]),
            (act_s.at[rows], act_out.at[rows]),
            (dsc_s.at[rows], dsc_out.at[rows]),
            (inn_s.at[rows], inn_out.at[rows]),
            (bcb_s.at[rows], bc_out.at[rows]),
            (step_s.at[rows], step_out.at[rows]),
            (prev_s.at[pl.ds(q * subs, subs)], prev_out.at[pl.ds(q * subs, subs)]),
        )
        return [pltpu.make_async_copy(src, dst, store_sem.at[i, q]) for i, (src, dst) in enumerate(pairs)]

    def quarter_step(q, carry):
        lax.fori_loop(q * subs, (q + 1) * subs, block, 0)

        @pl.when(q != me)
        def _():
            leave(q).start()

        for item in stores(q):
            item.start()
        return carry

    lax.fori_loop(0, groups, quarter_step, 0)
    stay = pltpu.make_async_copy(gated_s.at[me], gated_out.at[me], local_sem.at[2])
    stay.start()
    run_streams(streams)
    for item in gain_sends:
        item.wait()
    for item in keep:
        item.wait()
    stay.wait()

    def finish(q, carry):
        @pl.when(q != me)
        def _():
            leave(q).wait_send()
            arrive(q).wait_recv()

        for item in stores(q):
            item.wait()
        return carry

    lax.fori_loop(0, groups, finish, 0)


def front_call(tokens, pre_gain, zw, xw, bcw, dtw, out_weight, norm_gain, convw, convb, dtb, alog, skip, groups, batches):
    rows_num, model = tokens.shape
    channels = zw.shape[1]
    n = bcw.shape[1] // 2
    length = rows_num * groups
    count = log2(batches)
    part = channels // batches
    copies = 3 + 2 + (groups - 1) * (1 + 2 * (1 + count))
    hbm = pl.BlockSpec(memory_space=pl.ANY)
    vmem = pl.BlockSpec(memory_space=pltpu.VMEM)
    wide = jax.ShapeDtypeStruct((length, channels), BF16)
    outs = [
        jax.ShapeDtypeStruct((length, model), BF16), wide, wide, wide, wide, wide,
        jax.ShapeDtypeStruct((length, 2 * n), BF16),
        jax.ShapeDtypeStruct((length, dtw.shape[1]), F32),
        jax.ShapeDtypeStruct((length // SPAN, n, channels), BF16),
        jax.ShapeDtypeStruct((groups, rows_num, channels), BF16),
        jax.ShapeDtypeStruct((groups,) + (2,) * count + (part, model), BF16),
        jax.ShapeDtypeStruct((groups, 8, channels), F32),
    ]
    dma = pltpu.SemaphoreType.DMA
    result = pl.pallas_call(
        functools.partial(front_kernel, count),
        in_specs=[vmem, vmem] + [hbm] * 6 + [vmem] * 5,
        out_specs=[hbm] * len(outs),
        out_shape=outs,
        scratch_shapes=[
            pltpu.VMEM((2, 2, rows_num, model), BF16),
            pltpu.VMEM(zw.shape, BF16), pltpu.VMEM(xw.shape, BF16),
            pltpu.VMEM(bcw.shape, BF16), pltpu.VMEM(dtw.shape, BF16),
            pltpu.VMEM((length, channels), F32),
            pltpu.VMEM((length, channels), BF16), pltpu.VMEM((length, channels), BF16),
            pltpu.VMEM((length, channels), BF16), pltpu.VMEM((length, channels), BF16),
            pltpu.VMEM((length, channels), BF16), pltpu.VMEM((length + 8, channels), F32),
            pltpu.VMEM((length, 2 * n), F32), pltpu.VMEM((length, 2 * n), BF16),
            pltpu.VMEM((length, dtw.shape[1]), F32), pltpu.VMEM((length // SPAN, n, channels), BF16),
            pltpu.VMEM((groups, rows_num, channels), BF16),
            pltpu.VMEM((n, channels), F32), pltpu.VMEM((SPAN, channels), BF16),
            dma((4,)), dma((3,)), dma((9, groups)), dma((groups,)), dma((groups,)), dma((copies,)), dma((copies,)),
        ],
        compiler_params=pltpu.CompilerParams(
            collective_id=1, has_side_effects=True, vmem_limit_bytes=VMEM_BYTES
        ),
        cost_estimate=pl.CostEstimate(
            flops=4 * length * model * channels, bytes_accessed=400 * 2**20, transcendentals=0
        ),
        name="front",
    )(
        tokens, pre_gain[None], zw, xw, bcw, dtw, out_weight.reshape((2,) * count + (part, model)),
        jnp.broadcast_to(norm_gain[None], (8, channels)), convw, convb, dtb, alog, skip,
    )
    x, a, s, act, dsc, inn, bc, step, prev, gated, w_all, gains = result
    return x, (a, s, act, dsc, inn), bc, step, prev, gated, w_all.reshape(groups, channels, model), gains[:, :1]


def outgrad_scatter_kernel(count, gg_ref, dy_ref, out_ref, *refs):
    buf, send, recv = refs[0], refs[-2], refs[-1]
    streams_num = 4
    slots = [refs[1 + s * count : 1 + (s + 1) * count] for s in range(streams_num)]
    groups, _, channels = gg_ref.shape
    part, cols = buf.shape[-2:]
    model = dy_ref.shape[2]
    links = Links(send, recv)
    meet([("batch", partner("batch", b)) for b in range(count)])
    up = list(range(1, count))

    def stream(s):
        g0, c0 = (s // 2) * (groups // 2), (s % 2) * cols
        for j in range(groups // 2):
            for w, (lo, hi) in enumerate(segments(channels)):
                term = mm_tn(gg_ref[g0 + j, :, lo:hi], dy_ref[w, :, c0 : c0 + cols]).astype(BF16)
                for p in range(lo // part, hi // part):
                    index = tuple((p >> b) & 1 for b in reversed(range(count)))
                    buf[(s,) + index + (j,)] = term[p * part - lo : (p + 1) * part - lo]
        order = [0] + (up if s % 2 == 0 else up[::-1])
        yield from scatter(links, buf.at[s], slots[s], order)
        mine = place(count, dict(enumerate(bits_of("batch", count))))
        for j in range(groups // 2):
            out_ref[g0 + j, :, c0 : c0 + cols] = buf[(s,) + mine + (j,)]

    run_streams([stream(s) for s in range(streams_num)])


def outgrad_scatter_call(gg, dy, batches):
    groups, _, channels = gg.shape
    model = dy.shape[2]
    count = log2(batches)
    part = channels // batches
    block = (groups // 2, part, model // 2)
    vmem = pl.BlockSpec(memory_space=pltpu.VMEM)
    return pl.pallas_call(
        functools.partial(outgrad_scatter_kernel, count),
        in_specs=[vmem, vmem],
        out_specs=vmem,
        out_shape=jax.ShapeDtypeStruct((groups, part, model), BF16),
        scratch_shapes=[pltpu.VMEM((4,) + (2,) * count + block, BF16)]
        + [s for _ in range(4) for s in halving_slots(count, block, BF16)]
        + [pltpu.SemaphoreType.DMA((4 * count,)), pltpu.SemaphoreType.DMA((4 * count,))],
        compiler_params=pltpu.CompilerParams(
            collective_id=2, has_side_effects=True, vmem_limit_bytes=VMEM_BYTES
        ),
        cost_estimate=pl.CostEstimate(
            flops=2 * groups * gg.shape[1] * channels * model, bytes_accessed=200 * 2**20, transcendentals=0
        ),
        name="out_weight_grad",
    )(gg, dy)


class Stream:
    def __init__(self, *parts):
        self.steps = []
        for part in parts:
            if self.steps and part:
                last, first = self.steps.pop(), part[0]
                self.steps.append(lambda last=last, first=first: (last(), first()))
                part = part[1:]
            self.steps.extend(part)

    def advance(self):
        if self.steps:
            self.steps.pop(0)()


def advance_all(streams):
    for s in streams:
        s.advance()


def drain(streams):
    while any(s.steps for s in streams):
        advance_all(streams)


class Ports:
    def __init__(self, send, recv):
        self.send, self.recv, self.used = send, recv, 0

    def make(self, src, dst, axis, to):
        at = self.used
        self.used += 1

        def describe():
            return pltpu.make_async_remote_copy(
                src_ref=src(), dst_ref=dst(), send_sem=self.send.at[at], recv_sem=self.recv.at[at],
                device_id={axis: to()}, device_id_type=pl.DeviceIdType.MESH,
            )

        return describe


def linked(copies, work):
    steps = []
    for i in range(len(copies) + 1):
        def step(i=i):
            if i:
                copies[i - 1]().wait()
                work(i - 1)
            if i < len(copies):
                copies[i]().start()

        steps.append(step)
    return steps


def halving(ports, axis, buf, slots, order):
    count = len(order)

    def fixed(i, give):
        mine = bits_of(axis, count)
        out = {b: mine[b] for b in order[: i + 1]}
        if give:
            out[order[i]] = 1 - out[order[i]]
        return out

    copies = [
        ports.make(
            lambda i=i: buf().at[place(count, fixed(i, True))], lambda i=i: slots[i],
            axis, lambda i=i: partner(axis, order[i]),
        )
        for i in range(count)
    ]

    def work(i):
        for at in itertools.product(*(range(d) for d in slots[i].shape[:-2])):
            add_block(buf(), place(count, fixed(i, False)), slots[i], at)

    return linked(copies, work)


def spreading(ports, axis, buf, order):
    count = len(order)

    def at(i):
        mine = bits_of(axis, count)
        return buf().at[place(count, {b: mine[b] for b in order[i:]})]

    copies = [
        ports.make(lambda i=i: at(i), lambda i=i: at(i), axis, lambda i=i: partner(axis, order[i]))
        for i in range(count)
    ]
    return linked(copies, lambda i: None)


def exchanging(ports, axis, buf, slots, order):
    copies = [
        ports.make(buf, lambda i=i: slots[i], axis, lambda i=i: partner(axis, order[i])) for i in range(len(order))
    ]

    def work(i):
        ref = buf()
        ref[...] = (ref[...].astype(F32) + slots[i][...].astype(F32)).astype(ref.dtype)

    return linked(copies, work)


def back_kernel(
    count, group_bits,
    dg_hbm, a_hbm, s_hbm, act_hbm, dsc_hbm, inn_hbm, x_hbm, bc_hbm, step_hbm, prev_hbm,
    zw_hbm, xw_hbm, bcw_hbm, dtw_hbm, o_hbm, gain_ref, convw_ref, dtb_ref, alog_ref, skip_ref, hot_ref,
    z_out, x_out, o_out, bc_out, small_out, own_out,
    dg, a, s, act, dsc, inn, x, bc, step, prev, zw, xw, bdw, obuf,
    lam, dconv, dyc_s, vt_s, q_s, v_s, w_s, da_s, etot_s, draw_s, head_s, vec_s, pre_s, dbs,
    rows_s, far_s, zg, bcbuf, small, *refs,
):
    zx_slots = [refs[i * count : (i + 1) * count] for i in range(4)]
    refs = refs[4 * count :]
    bc_slots, refs = (refs[:count], refs[count : 2 * count]), refs[2 * count :]
    bc_head, refs = (refs[:group_bits], refs[group_bits : 2 * group_bits]), refs[2 * group_bits :]
    small_slots, refs = refs[:count], refs[count:]
    small_head, refs = refs[:group_bits], refs[group_bits:]
    o_slots, refs = refs[:group_bits], refs[group_bits:]
    load_sem, store_sem, rsend, rrecv, send, recv = refs
    length, channels = a.shape
    model = x.shape[1]
    n = lam.shape[0]
    heads = hot_ref.shape[0]
    groups = rows_s.shape[0] * rows_s.shape[1]
    rows_num = length // groups
    subs = rows_num // SPAN
    wide = bcbuf.shape[-1]
    me = lax.axis_index("head")
    my_hi, my_lo = me // 2, me % 2

    pairs = [
        (dg_hbm, dg), (a_hbm, a), (s_hbm, s), (x_hbm, x), (o_hbm, obuf), (step_hbm, step), (bc_hbm, bc),
        (prev_hbm, prev), (act_hbm, act), (dsc_hbm, dsc), (inn_hbm, inn), (zw_hbm, zw), (xw_hbm, xw),
        (bcw_hbm, bdw.at[:, pl.ds(0, 2 * n)]), (dtw_hbm, bdw.at[:, pl.ds(2 * n, 128)]),
    ]
    loads = [pltpu.make_async_copy(src, dst, load_sem.at[i]) for i, (src, dst) in enumerate(pairs)]
    for load in loads:
        load.start()
    for load in loads[:3]:
        load.wait()

    def gates(i, carry):
        per = rows_num // 64
        rows = pl.ds(pl.multiple_of(i * 64, 64), 64)
        d = dg[i // per, pl.ds(pl.multiple_of((i % per) * 64, 64), 64), :].astype(F32)
        a[rows, :] = (d * a[rows, :].astype(F32)).astype(BF16)
        s[rows, :] = (d * s[rows, :].astype(F32)).astype(BF16)
        return carry

    lax.fori_loop(0, length // 64, gates, 0)
    meet(
        [("batch", partner("batch", b)) for b in range(count)]
        + [("head", partner("head", b)) for b in range(group_bits)]
    )

    ports = Ports(send, recv)
    up = list(range(1, count))
    orders = [up, up[::-1]]
    cols_num = channels // 2

    def own_at():
        return place(count, dict(enumerate(bits_of("batch", count))))

    def keep(src, dst, sem):
        def step():
            copy = pltpu.make_async_copy(src(), dst(), store_sem.at[sem])
            copy.start()
            copy.wait()

        return [step]

    def grads(i):
        part = (slice(None),) * (count + 1) + (pl.ds((i % 2) * cols_num, cols_num),)
        view = lambda: (z_out, x_out)[i // 2].at[part]
        buf = lambda: (zg, zw)[i // 2].at[part]
        order = orders[i % 2]
        return Stream(
            halving(ports, "batch", buf, zx_slots[i], [0] + order),
            keep(lambda: buf().at[own_at()], lambda: view().at[own_at()], i),
            spreading(ports, "batch", view, order[::-1] + [0]),
        )

    streams = [grads(i) for i in range(4)]
    def state_part(i):
        part = (slice(None),) * (count + 1) + ((pl.ds(n, n + 128), pl.ds(0, n))[i],)
        buf = lambda: bcbuf.at[part]
        view = lambda: bc_out.at[part]
        return Stream(
            halving(ports, "batch", buf, bc_slots[i], [0] + orders[i]),
            exchanging(
                ports, "head", lambda: bcbuf.at[own_at() + (slice(None), pl.ds((n, 0)[i], n))], bc_head[i],
                range(group_bits),
            ),
            keep(lambda: buf().at[own_at()], lambda: view().at[own_at()], (4, 6)[i]),
            spreading(ports, "batch", view, orders[i][::-1] + [0]),
        )

    state = [state_part(i) for i in range(2)]
    vectors = Stream(
        exchanging(ports, "batch", lambda: small, small_slots, range(count)),
        exchanging(ports, "head", lambda: small.at[pl.ds(0, 8)], small_head, range(group_bits)),
    )
    half = model // 2

    def head_own():
        return place(group_bits, dict(enumerate(bits_of("head", group_bits))))

    def o_view(i):
        return o_out.at[(slice(None),) * (count + 1) + (pl.ds(i * half, half),)]

    outs = Stream(
        halving(ports, "head", lambda: obuf, o_slots, list(range(group_bits))),
        keep(lambda: obuf.at[head_own()], lambda: o_out.at[own_at()], 5),
    )
    spread = [Stream(spreading(ports, "batch", lambda i=i: o_view(i), orders[i] + [0])) for i in range(2)]

    for load in loads[3:5]:
        load.wait()
    outs.advance()
    tile = 256
    block_rows = model >> count

    def put(target, t, value):
        for k in range(tile // min(block_rows, tile)):
            p = (t * tile) // block_rows + k
            index = tuple((p // 2**b) % 2 for b in reversed(range(count)))
            if block_rows <= tile:
                target[index] = value[k * block_rows : (k + 1) * block_rows].astype(BF16)
            else:
                first = pl.multiple_of((t * tile) % block_rows, tile)
                target[index + (pl.ds(first, tile), slice(None))] = value.astype(BF16)

    def take(source, t):
        if block_rows >= tile:
            p = (t * tile) // block_rows
            index = tuple((p // 2**b) % 2 for b in reversed(range(count)))
            return source[index + (pl.ds(pl.multiple_of((t * tile) % block_rows, tile), tile), slice(None))]
        found = []
        for k in range(tile // block_rows):
            p = (t * tile) // block_rows + k
            found.append(source[tuple((p // 2**b) % 2 for b in reversed(range(count)))])
        return jnp.concatenate(found, axis=0)

    def weight_grad(right, target):
        def one(t, carry):
            put(target, t, mm_tn(x[:, pl.ds(pl.multiple_of(t * tile, tile), tile)], right[...]))
            return carry

        lax.fori_loop(0, model // tile, one, 0)

    weight_grad(a, zg)
    advance_all(streams[:2])
    for load in loads[5:]:
        load.wait()

    lam[...] = jnp.zeros_like(lam)
    dconv[rows_num:, :] = jnp.zeros((8, channels), F32)
    vec_s[...] = jnp.zeros_like(vec_s)
    head_s[...] = jnp.zeros_like(head_s)
    draw_s[...] = jnp.zeros_like(draw_s)
    pre_s[...] = jnp.zeros_like(pre_s)
    rate = -jnp.exp(alog_ref[...])
    lower = lower_mask((SPAN, SPAN))
    lower_f = lower.astype(F32)
    lower_b = lower.astype(BF16)
    row_at = lax.broadcasted_iota(jnp.int32, (SPAN, SPAN), 0)
    col_at = lax.broadcasted_iota(jnp.int32, (SPAN, SPAN), 1)
    upper = row_at <= col_at
    strict = row_at < col_at
    strict_f = strict.astype(F32)
    left = lax.broadcasted_iota(jnp.int32, (SPAN, 128), 1) < 64

    def block(at, local):
        rows = pl.ds(pl.multiple_of(at * SPAN, SPAN), SPAN)
        local_rows = pl.ds(pl.multiple_of(local * SPAN, SPAN), SPAN)
        raw = step[rows, :] + dtb_ref[...]
        delta = softplus(raw)
        cum = mm_exact(lower_f, delta * rate)
        cum_t = cum.T
        delta_t = delta.T
        slope_t = sigmoid(raw).T
        rate_t = jnp.broadcast_to(rate, (SPAN, 128)).T
        b_val = bc[rows, :n]
        c_val = bc[rows, n:]
        inner = jnp.where(upper, mm_nt(b_val, c_val), 0.0)
        before = prev[at]
        lam_b = lam[...].astype(BF16)
        across = mm(c_val, before)
        dtail = mm(b_val, lam_b)
        d_inner_prod = jnp.zeros((SPAN, SPAN), F32)
        for pair in range(channels // 128):
            cols = slice(pair * 128, pair * 128 + 128)
            c0, c1, ce = pair_columns(cum, pair, left)
            _, _, de = pair_columns(delta, pair, left)
            tot = ce[SPAN - 1 : SPAN, :]
            e_cum = jnp.exp(ce)
            e_tail = jnp.exp(tot - ce)
            dy_b = s[rows, cols]
            dy = dy_b.astype(F32)
            act_p = act[rows, cols].astype(F32)
            vec_s[5:6, cols] += jnp.sum(dy * act_p, axis=0, keepdims=True)
            u = act_p * de
            u_b = u.astype(BF16)
            zero = jnp.zeros_like(dy_b)
            dy01 = jnp.concatenate([jnp.where(left, dy_b, zero), jnp.where(left, zero, dy_b)], axis=0)
            m0 = jnp.exp(jnp.minimum(cum_t[2 * pair : 2 * pair + 1, :] - c0, 0.0))
            m1 = jnp.exp(jnp.minimum(cum_t[2 * pair + 1 : 2 * pair + 2, :] - c1, 0.0))
            p0 = m0 * inner
            p1 = m1 * inner
            du = mm(jnp.concatenate([p0.astype(BF16), p1.astype(BF16)], axis=1), dy01)
            dp = mm_nt(u_b, dy01)
            dp0, dp1 = dp[:, :SPAN], dp[:, SPAN:]
            d_inner_prod += dp0 * m0 + dp1 * m1
            e01 = jnp.concatenate([(dp0 * p0).astype(BF16), (dp1 * p1).astype(BF16)], axis=0)
            spans = mm(e01, lower_b)
            da_s[2 * pair : 2 * pair + 1, :] = jnp.sum(
                jnp.where(strict, spans[:SPAN], 0.0), axis=0, keepdims=True
            )
            da_s[2 * pair + 1 : 2 * pair + 2, :] = jnp.sum(
                jnp.where(strict, spans[SPAN:], 0.0), axis=0, keepdims=True
            )
            dut = dtail[:, cols] * e_tail
            du = du + dut
            dye = dy * e_cum
            dyc_s[:, cols] = dye.astype(BF16)
            vt_s[:, cols] = (u * e_tail).astype(BF16)
            q_s[:, cols] = (dye * across[:, cols]).astype(BF16)
            v_s[:, cols] = (u * dut).astype(BF16)
            w_s[:, cols] = (act_p * du).astype(BF16)
            etot_s[:, cols] = jnp.exp(tot)
            d_act = de * du + skip_ref[:, cols] * dy
            dconv[local_rows, cols] = d_act * dsc[rows, cols].astype(F32)
        hot = hot_ref[...]
        over = jnp.sum(lam[...] * before.astype(F32), axis=0, keepdims=True) * etot_s[...]
        over = jnp.broadcast_to(over, (128, channels))
        over = lax.dot_general(
            hot.astype(F32), over, (((1,), (1,)), ((), ())), preferred_element_type=F32, precision=HIGHEST
        )
        da = (
            da_s[...]
            + mm_exact(mm_nt(hot, q_s[...]), lower_f)
            + mm_exact(mm_nt(hot, v_s[...]), strict_f)
            + over
        )
        d_step = mm_nt(hot, w_s[...]) + rate_t[:heads] * da
        d_raw = d_step * slope_t[:heads]
        head_s[0:heads, :] += d_raw
        head_s[heads : 2 * heads, :] += delta_t[:heads] * da * rate_t[:heads]
        draw_s[0:heads, :] = d_raw
        dg_b = jnp.where(upper, d_inner_prod, 0.0)
        dbs[rows, :n] = (mm(dg_b.astype(BF16), c_val) + mm_nt(vt_s[...], lam_b)).astype(BF16)
        dbs[rows, n : 2 * n] = (mm(dg_b.T.astype(BF16), b_val) + mm_nt(dyc_s[...], before)).astype(BF16)
        dbs[rows, 2 * n :] = draw_s[...].T.astype(BF16)
        lam[...] = lam[...] * etot_s[...] + mm(bc[rows, n:].astype(F32).T.astype(BF16), dyc_s[...])

    def near_copy(hi, h):
        at = 2 * hi + h
        return pltpu.make_async_remote_copy(
            src_ref=rows_s.at[hi, 1 - my_lo, h], dst_ref=dg.at[at], send_sem=rsend.at[at], recv_sem=rrecv.at[at],
            device_id={"head": partner("head", 0)}, device_id_type=pl.DeviceIdType.MESH,
        )

    def far_copy(h):
        return pltpu.make_async_remote_copy(
            src_ref=rows_s.at[1 - my_hi, my_lo, h], dst_ref=far_s.at[h], send_sem=rsend.at[4 + h],
            recv_sem=rrecv.at[4 + h],
            device_id={"head": partner("head", 1)}, device_id_type=pl.DeviceIdType.MESH,
        )

    def join_near(hi, h):
        near_copy(hi, h).wait()
        add_block(rows_s, (hi, my_lo, h), dg.at[2 * hi + h], ())

        @pl.when(my_hi != hi)
        def _():
            far_copy(h).start()

    def quarter_step(i, carry):
        q = groups - 1 - i
        rows = pl.ds(pl.multiple_of(q * rows_num, rows_num), rows_num)

        def one(j, inner_carry):
            block(q * subs + subs - 1 - j, subs - 1 - j)
            return inner_carry

        lax.fori_loop(0, subs, one, 0)
        for k in range(groups):
            @pl.when(i == k)
            def _():
                for action in plan[k, "a"]:
                    action()

        for c in range(0, channels, 128):
            cols = slice(c, c + 128)
            inner_v = inn[rows, cols].astype(F32)
            d_in = jnp.zeros((rows_num, 128), F32)
            for k in range(4):
                shifted = dconv[3 - k : 3 - k + rows_num, cols]
                d_in += convw_ref[k : k + 1, cols] * shifted
                vec_s[k : k + 1, cols] += jnp.sum(inner_v * shifted, axis=0, keepdims=True)
            vec_s[4:5, cols] += jnp.sum(dconv[0:rows_num, cols], axis=0, keepdims=True)
            inn[rows, cols] = d_in.astype(BF16)
        dconv[rows_num:, :] = dconv[0:8, :]

        def columns(t, inner_carry):
            cols = pl.ds(pl.multiple_of(t * tile, tile), tile)
            value = mm_nt(a[rows, :], take(zw, t)) + mm_nt(inn[rows, :], xw[cols, :]) + mm_nt(dbs[rows, :], bdw[cols, :])
            pre_s[:, cols] += jnp.sum(value * x[rows, cols].astype(F32), axis=0, keepdims=True)
            per = model // 2 // tile
            rows_s[q // 2, q % 2, t // per, :, pl.ds(pl.multiple_of((t % per) * tile, tile), tile)] = value.astype(BF16)
            return inner_carry

        lax.fori_loop(0, model // tile, columns, 0)

        @pl.when(q % 2 != my_lo)
        def _():
            for h in range(2):
                near_copy(q // 2, h).start()

        for k in range(groups):
            @pl.when(i == k)
            def _():
                for action in plan[k, "b"]:
                    action()

        return carry

    plan = {(k, half_at): [] for k in range(groups) for half_at in "ab"}

    def book(stream, slots):
        for slot in slots:
            if stream.steps:
                plan[slot].append(stream.steps.pop(0))

    for st in streams[:2]:
        book(st, [(0, "a"), (1, "a"), (2, "a"), (2, "b"), (3, "b")])
    book(outs, [(1, "a"), (2, "b")])
    for st in spread:
        book(st, [(2, "b"), (3, "a"), (3, "b")])
    plan[3, "b"] += [lambda h=h: join_near(1, h) for h in range(2)]
    lax.fori_loop(0, groups, quarter_step, 0)

    weight_grad(inn, zw)
    advance_all(streams[2:])

    def state_grad(t, carry):
        put(bcbuf, t, mm_tn(x[:, pl.ds(pl.multiple_of(t * tile, tile), tile)], dbs[...]))
        return carry

    lax.fori_loop(0, model // tile, state_grad, 0)
    advance_all(state)
    small[...] = jnp.zeros_like(small)
    for j in range(groups):
        small[j : j + 1, :] = gain_ref[j]
    for j in range(model // channels):
        small[groups + j : groups + j + 1, :] = pre_s[:, j * channels : (j + 1) * channels]
    small[8:14, :] = vec_s[0:6, :]
    totals = lax.dot_general(
        jnp.ones((8, SPAN), F32), head_s[...], (((1,), (1,)), ((), ())),
        preferred_element_type=F32, precision=HIGHEST,
    )
    small[14:15, 0:128] = totals[0:1]
    vectors.advance()
    advance_all(streams)
    advance_all(spread)
    join_near(0, 0)
    advance_all(state + [vectors])
    join_near(0, 1)
    drain(streams + spread + state + [vectors, outs])
    for h in range(2):
        far_copy(h).wait()
    small_out[...] = small[...]

    def total(r, carry):
        rs = pl.ds(pl.multiple_of(r * 32, 32), 32)
        for h in range(2):
            own_out[rs, h * half : (h + 1) * half] = rows_s[my_hi, my_lo, h, rs, :].astype(F32) + far_s[h, rs, :].astype(F32)
        return carry

    lax.fori_loop(0, rows_num // 32, total, 0)


def back_call(dg, res, x, bc, step, prev, zw, xw, bcw, dtw, out_part, gain_grad, convw, dtb, alog, skip, hot, groups, batches):
    length, model = x.shape
    channels = xw.shape[1]
    n = bc.shape[1] // 2
    heads = hot.shape[0]
    rows_num = length // groups
    count = log2(batches)
    group_bits = log2(groups)
    lead = (2,) * count
    part = channels // batches
    rows = model // batches
    wide = 2 * n + 128
    block = (rows, channels // 2)
    hbm = pl.BlockSpec(memory_space=pl.ANY)
    vmem = pl.BlockSpec(memory_space=pltpu.VMEM)
    dma = pltpu.SemaphoreType.DMA
    copies = 4 * 2 * count + 2 * (2 * count + group_bits) + (count + group_bits) + group_bits + 2 * count
    tall = lambda w, t: pltpu.VMEM((length, w), t)
    span = pltpu.VMEM((SPAN, channels), BF16)
    z, xg, o, bcg, small, own = pl.pallas_call(
        functools.partial(back_kernel, count, group_bits),
        in_specs=[hbm] * 15 + [vmem] * 6,
        out_specs=[hbm] * 4 + [vmem] * 2,
        out_shape=[
            jax.ShapeDtypeStruct(lead + (rows, channels), BF16),
            jax.ShapeDtypeStruct(lead + (rows, channels), BF16),
            jax.ShapeDtypeStruct(lead + (part, model), BF16),
            jax.ShapeDtypeStruct(lead + (rows, wide), BF16),
            jax.ShapeDtypeStruct((16, channels), F32),
            jax.ShapeDtypeStruct((rows_num, model), F32),
        ],
        scratch_shapes=[pltpu.VMEM((groups, rows_num, model // 2), BF16)] + [tall(channels, BF16)] * 5
        + [
            tall(model, BF16), tall(2 * n, BF16), tall(128, F32), pltpu.VMEM(prev.shape, BF16),
            pltpu.VMEM(lead + (rows, channels), BF16), pltpu.VMEM(xw.shape, BF16), pltpu.VMEM((model, wide), BF16),
            pltpu.VMEM((2,) * group_bits + (part, model), BF16),
            pltpu.VMEM((n, channels), F32), pltpu.VMEM((rows_num + 8, channels), F32),
        ]
        + [span] * 5
        + [
            pltpu.VMEM((heads, SPAN), F32), pltpu.VMEM((1, channels), F32), pltpu.VMEM((128, SPAN), F32),
            pltpu.VMEM((128, SPAN), F32), pltpu.VMEM((8, channels), F32), pltpu.VMEM((1, model), F32),
            tall(wide, BF16),
            pltpu.VMEM((2, 2, 2, rows_num, model // 2), BF16), pltpu.VMEM((2, rows_num, model // 2), BF16),
            pltpu.VMEM(lead + (rows, channels), BF16), pltpu.VMEM(lead + (rows, wide), BF16),
            pltpu.VMEM((16, channels), F32),
        ]
        + [s for _ in range(4) for s in halving_slots(count, block, BF16)]
        + halving_slots(count, (rows, n + 128), BF16)
        + halving_slots(count, (rows, n), BF16)
        + [pltpu.VMEM((rows, n), BF16)] * (2 * group_bits)
        + [pltpu.VMEM((16, channels), F32)] * count
        + [pltpu.VMEM((8, channels), F32)] * group_bits
        + halving_slots(group_bits, (part, model), BF16)
        + [dma((15,)), dma((7,)), dma((6,)), dma((6,)), dma((copies,)), dma((copies,))],
        compiler_params=pltpu.CompilerParams(
            collective_id=3, has_side_effects=True, vmem_limit_bytes=BACK_VMEM_BYTES
        ),
        cost_estimate=pl.CostEstimate(
            flops=10 * length * model * channels, bytes_accessed=300 * 2**20, transcendentals=0
        ),
        name="back",
    )(
        dg, *res, x, bc, step, prev, zw.reshape(lead + (rows, channels)), xw, bcw, dtw, out_part.reshape((2,) * group_bits + (part, model)),
        gain_grad, convw, dtb, alog, skip, hot,
    )
    return (
        z.reshape(model, channels), xg.reshape(model, channels), o.reshape(channels, model),
        bcg.reshape(model, wide), small, own,
    )


def finish_kernel(
    z_ref, x_ref, o_ref, bc_ref, small_ref, own_ref, tok_ref, cot_ref, pre_ref,
    zf_ref, xf_ref, of_ref, bcf_ref, dt_ref, grad_ref, convw_ref, convb_ref, skip_ref, gain_ref, pre_out, dtb_ref, alog_ref,
):
    zf_ref[...] = z_ref[...].astype(F32)
    xf_ref[...] = x_ref[...].astype(F32)
    of_ref[...] = o_ref[...].astype(F32)
    width = bcf_ref.shape[1]
    heads = dt_ref.shape[1]
    bcf_ref[...] = bc_ref[:, :width].astype(F32)
    dt_ref[...] = bc_ref[:, width : width + 128].astype(F32)[:, :heads]
    tok = tok_ref[...].astype(F32)
    recip = lax.rsqrt(jnp.mean(tok * tok, axis=-1, keepdims=True) + EPSILON)
    scaled = pre_ref[...] * own_ref[...]
    mean = jnp.mean(tok * scaled, axis=-1, keepdims=True)
    passed = sum(cot_ref[w].astype(F32) for w in range(4))
    grad_ref[...] = (passed + recip * scaled - tok * recip**3 * mean).astype(BF16)

    @pl.when(pl.program_id(0) == 0)
    def _():
        groups = small_ref.shape[0] // 4
        channels = small_ref.shape[1]
        convw_ref[...] = small_ref[8:12, :]
        convb_ref[...] = small_ref[12:13, :]
        skip_ref[...] = small_ref[13:14, :]
        me = lax.axis_index("head")
        gain = small_ref[0:1, :]
        for j in range(1, groups):
            gain = jnp.where(me == j, small_ref[j : j + 1, :], gain)
        gain_ref[...] = gain
        for j in range(pre_out.shape[1] // channels):
            cols = slice(j * channels, (j + 1) * channels)
            pre_out[:, cols] = small_ref[groups + j : groups + j + 1, :] / pre_ref[:, cols]
        dtb_ref[...] = small_ref[14:15, 0:heads]
        alog_ref[...] = small_ref[14:15, heads : 2 * heads]


def finish_call(z, x, o, bc, small, own, tok, cot, pre_gain, heads):
    model, channels = z.shape
    rows_num = tok.shape[0]
    steps = 8
    wide = bc.shape[1]
    rows = lambda r, w: pl.BlockSpec((r // steps, w), lambda i: (i, 0))
    fixed = lambda shape: pl.BlockSpec(shape, lambda i: (0, 0))
    shapes = [
        ((model, channels), F32), ((model, channels), F32), ((channels, model), F32), ((model, wide - 128), F32),
        ((model, heads), F32), ((rows_num, model), BF16),
    ]
    flat = [(4, channels), (1, channels), (1, channels), (1, channels), (1, model), (1, heads), (1, heads)]
    return pl.pallas_call(
        finish_kernel,
        grid=(steps,),
        in_specs=[
            rows(model, channels), rows(model, channels), rows(channels, model), rows(model, wide),
            fixed(small.shape), rows(rows_num, model), rows(rows_num, model),
            pl.BlockSpec((4, rows_num // steps, model), lambda i: (0, i, 0)), fixed((1, model)),
        ],
        out_specs=[rows(*shape) for shape, _ in shapes] + [fixed(shape) for shape in flat],
        out_shape=[jax.ShapeDtypeStruct(shape, t) for shape, t in shapes]
        + [jax.ShapeDtypeStruct(shape, F32) for shape in flat],
        compiler_params=pltpu.CompilerParams(vmem_limit_bytes=VMEM_BYTES),
        cost_estimate=pl.CostEstimate(flops=0, bytes_accessed=46 * 2**20, transcendentals=0),
        name="finish",
    )(z, x, o, bc, small, own, tok, cot, pre_gain[None])


def per_device(
    tokens, z_weight, x_weight, bc_weight, dt_weight, conv_weight, conv_bias, dt_bias,
    a_log, skip, norm_gain, pre_gain, out_weight, cotangent,
):
    groups = lax.axis_size("head")
    batches = lax.axis_size("batch")
    _, own_len, model = tokens.shape
    tokens = tokens[0]
    cot = cotangent[:, 0]
    channels = z_weight.shape[1]
    heads = dt_weight.shape[1]
    pad = lambda v: jnp.pad(v, ((0, 0), (0, 128 - heads)))
    dtb = pad(dt_bias[None])
    alog = pad(a_log[None])
    skip_r = skip[None]
    dtw = pad(dt_weight)
    x, res, bc, step, prev, gated, w_all, gain_all = front_call(
        tokens, pre_gain, z_weight, x_weight, bc_weight, dtw, out_weight, norm_gain,
        conv_weight, conv_bias[None], dtb, alog, skip_r, groups, batches,
    )
    outputs, d_gated, dy, gg, gain_grad = middle_call(gated, w_all, gain_all, tokens, cot)
    d_gated = lax.all_to_all(d_gated, "head", 0, 0, tiled=True)
    out_part = outgrad_scatter_call(gg, dy, batches)
    hot = (jnp.arange(channels)[None] // (channels // heads) == jnp.arange(heads)[:, None]).astype(BF16)
    z_grad, x_grad, out_grad, bcdt_grad, small, d_own = back_call(
        d_gated, res, x, bc, step, prev, z_weight, x_weight, bc_weight, dtw, out_part, gain_grad,
        conv_weight, dtb, alog, skip_r, hot, groups, batches,
    )
    z_grad, x_grad, out_grad, bc_grad, dt_grad, tokens_grad, convw, convb, skip_g, gain_g, pre_g, dtb_g, alog_g = finish_call(
        z_grad, x_grad, out_grad, bcdt_grad, small, d_own, tokens, cot, pre_gain, heads
    )
    flat = lambda v: v.reshape(-1)
    return (
        outputs[:, None], tokens_grad[None], z_grad, x_grad, bc_grad, dt_grad, convw, flat(convb), flat(dtb_g),
        flat(alog_g), flat(skip_g), flat(gain_g), flat(pre_g), out_grad,
    )


def solution(mesh):
    head_cols = P(None, "head")
    rows4 = P(None, "batch", "head", None)
    return jax.shard_map(
        per_device,
        mesh=mesh,
        in_specs=(
            P("batch", "head", None), head_cols, head_cols, P(), head_cols, head_cols, P("head"),
            P("head"), P("head"), P("head"), P("head"), P(), P("head", None), rows4,
        ),
        out_specs=(
            rows4, P("batch", "head", None), head_cols, head_cols, P(), head_cols, head_cols,
            P("head"), P("head"), P("head"), P("head"), P("head"), P(), P("head", None),
        ),
        check_vma=False,
    )
```

time: 572 us -> 495 us (0.87); the launches traced: 562 us -> 494 us
  matrix products: 47 us -> 0 us
  Pallas kernels: 444 us -> 479 us
  other arithmetic: 30.7 us -> 0.63 us
  between operations: 14.6 us -> 0.71 us
  local copies, waits for them, and re-layouts: 21 us -> 9.36 us
    dot_general x8 -> x0, matrix products: 47 us -> none  [the longest x3 23.8 us: mm_nt(): lax.dot_general(a, b, (((1,), (1,)), ((), ())), preferred_element_type=F32)]
    pallas_call x2, Pallas kernels: 151 us -> 185 us  [the longest x1 167 us: back_call(): pl.pallas_call(functools.partial(back_kernel, count, group_bits), in_spec...]
    convert_element_type x3 -> x0, other arithmetic: 21.2 us -> none  [per_device(): v.astype(F32)]
  transfers between devices with their start and end apart: 3 -> 1, of which waited for: 0 -> 0; matrix products, arithmetic and copies ran while one was open for 15% -> 0% of each run, Pallas kernels for 42% -> 17%
where the time goes in v3:
time: 495 us; the launch traced here: 494 us
  Pallas kernels  479 us (97%)
  local copies, waits for them, and re-layouts  9.36 us (2%)
    pallas_call x1, Pallas kernels, front_call(): pl.pallas_call(functools.partial(front_kernel, count), in_specs=[vmem, vm...  184 us
    pallas_call x1, Pallas kernels, back_call(): pl.pallas_call(functools.partial(back_kernel, count, group_bits), in_spec...  167 us
    pallas_call x1, Pallas kernels, outgrad_scatter_call(): pl.pallas_call(functools.partial(outgrad_scatter_kernel, count), in_specs...  84.2 us
    pallas_call x1, Pallas kernels, middle_call(): pl.pallas_call(middle_kernel, out_shape=[jax.ShapeDtypeStruct((4, rows_nu...  25.4 us
    pallas_call x1, Pallas kernels, finish_call(): pl.pallas_call(finish_kernel, grid=(steps,), in_specs=[rows(model, channe...  18.2 us
  transfers between devices with their start and end apart: 1, of which 0 were waited for; matrix products, arithmetic and copies ran while one was open for 0% of the time, Pallas kernels for 17%

profile of v3, /device:TPU:0, one launch (start us, length us, event | category | flops | bytes accessed | tf_op | source)
XLA Modules:
  0.0 494.4 jit_solution(2447172323292623196)
XLA Ops:
  0.6 1.2 pad.12.dtb_ref
  1.8 1.2 pad.13.alog_ref
  3.0 1.1 copy.28
  4.1 0.9 pad.11.dtw_hbm
  5.0 1.3 broadcast_in_dim.31.gain_hbm
  6.3 184.2 %front.1 = (bf16[1024,2048]{1,0:T(8,128)(2,1)}, bf16[1024,1024]{1,0:T(8,128)(2,1)}, bf16[1024,1024]{1,0:T(8,128)(2,1)}, bf16[1024,1024]{1,0:T(8,128)(2,1)}, bf16...) custom-call(bf16[256,2048]{1,0:T(8,128)(2,1)} %bitcast.31, ...), custom_call_target="tpu_custom_call" | custom-call | flops 8589934592 | bytes 419430400 | tf_op jit(solution)/shard_map/front/pallas_call | solution.py:496
  190.6 1.5 slice.3.gain_ref
  192.1 25.4 %nested_norm.1 = (bf16[4,256,2048]{2,1,0:T(8,128)(2,1)}, bf16[4,256,1024]{2,1,0:T(8,128)(2,1)}, bf16[4,256,2048]{2,1,0:T(8,128)(2,1)}, bf16[4,256,1024]{2,1,0:T(8,128)(2,1)}, f32[4,1,1024]{2,1,0:T(1,128)}) custom-call(bf16[4,256,1024]{2,1,0:T(8,128)(2,1)} %get-tuple-element.50.g_ref, bf16[4,1024,2048]{2,1,0:T(8,128)(2,1)} %bitcast.50, ...), custom_call_target="tpu_custom_call" | custom-call | flops 8589934592 | bytes 37748736 | tf_op jit(solution)/shard_map/nested_norm/pallas_call | solution.py:121
  217.5 4.6 all-to-all-start
  222.2 0.6 fusion.hot_ref
  222.8 84.2 %out_weight_grad.1 = bf16[4,128,2048]{2,1,0:T(8,128)(2,1)} custom-call(bf16[4,256,1024]{2,1,0:T(8,128)(2,1)} %get-tuple-element.64.gg_ref, bf16[4,256,2048]{2,1,0:T(8,128)(2,1)} %get-tuple-element.65.dy_ref), custom_call_target="tpu_custom_call" | custom-call | flops 4294967296 | bytes 209715200 | tf_op jit(solution)/shard_map/out_weight_grad/pallas_call | solution.py:565
  307.0 0.0 all-to-all-done.dg_hbm
  307.0 167.0 %back.1 = (bf16[2,2,2,256,1024]{4,3,2,1,0:T(8,128)(2,1)}, bf16[2,2,2,256,1024]{4,3,2,1,0:T(8,128)(2,1)}, bf16[2,2,2,128,2048]{4,3,2,1,0:T(8,128)(2,1)}, bf16[2,2...) custom-call(bf16[4,256,1024]{2,1,0:T(8,128)(2,1)} %all-to-all-done.dg_hbm, ...), custom_call_target="tpu_custom_call" | custom-call | flops 21474836480 | bytes 314572800 | tf_op jit(solution)/shard_map/back/pallas_call | solution.py:1089
  474.0 18.2 %finish.1 = (f32[2048,1024]{1,0:T(8,128)}, f32[2048,1024]{1,0:T(8,128)}, f32[1024,2048]{1,0:T(8,128)}, f32[2048,256]{1,0:T(8,128)}, f32[2048,16]{1,0:T(8,128)}, ...) custom-call(bf16[2048,1024]{1,0:T(8,128)(2,1)} %bitcast.27, ...), custom_call_target="tpu_custom_call" | custom-call | bytes 48234496 | tf_op jit(solution)/shard_map/finish/pallas_call | solution.py:1191
  492.2 2.2 copy.30
  (1 shorter events, 0.0 us)
Async XLA Ops:
  217.5 89.5 %all-to-all-start = ((bf16[4,256,1024]{2,1,0:T(8,128)(2,1)}), bf16[4,256,1024]{2,1,0:T(8,128)(2,1)}, u32[]{:S(2)}, u32[]{:S(2)}) async-start(bf16[4,256,1024]{2,1,0:T(8,128)(2,1)} %get-tuple-element.54), calls=%async_computation | async-start | bytes 4194304 | tf_op jit(solution)/shard_map/all_to_all | solution.py:1229

commit v4 on v3

--- a/solution.py
+++ b/solution.py
@@ -60,81 +60,6 @@
     return list(zip([0] + ends[:-1], ends))
 
 
-def middle_kernel(g_ref, w_ref, gain_ref, tok_ref, cot_ref, out_ref, dg_ref, dy_ref, gg_ref, ggrad_ref):
-    groups, rows_num, channels = g_ref.shape
-    model = tok_ref.shape[1]
-    segs = segments(channels)
-    sums = [jnp.zeros((rows_num, 1), F32) for _ in segs]
-    for j in range(groups):
-        g = g_ref[j].astype(F32)
-        gg_ref[j] = (g * gain_ref[j]).astype(BF16)
-        for w, (lo, hi) in enumerate(segs):
-            sums[w] += jnp.sum(g[:, lo:hi] * g[:, lo:hi], axis=1, keepdims=True)
-    recips = []
-    total = jnp.zeros((rows_num, 1), F32)
-    for w, (lo, hi) in enumerate(segs):
-        total = total + sums[w]
-        recips.append(lax.rsqrt(total / (hi * groups) + EPSILON))
-    tile = 512
-
-    def forward(at, dots):
-        cols = pl.ds(pl.multiple_of(at * tile, tile), tile)
-        acc = jnp.zeros((rows_num, tile), F32)
-        tok = tok_ref[:, cols].astype(F32)
-        new = []
-        for w, (lo, hi) in enumerate(segs):
-            acc += mm(
-                jnp.concatenate([gg_ref[j, :, lo:hi] for j in range(groups)], axis=1),
-                jnp.concatenate([w_ref[j, lo:hi, cols] for j in range(groups)], axis=0),
-            )
-            out_ref[w, :, cols] = (tok + recips[w] * acc).astype(BF16)
-            new.append(dots[w] + jnp.sum(cot_ref[w, :, cols].astype(F32) * acc, axis=1, keepdims=True))
-        combined = jnp.zeros((rows_num, tile), F32)
-        for w in reversed(range(4)):
-            combined += recips[w] * cot_ref[w, :, cols].astype(F32)
-            dy_ref[w, :, cols] = combined.astype(BF16)
-        return tuple(new)
-
-    dots = lax.fori_loop(
-        0, model // tile, forward, tuple(jnp.zeros((rows_num, 1), F32) for _ in segs)
-    )
-    scales = [None] * 4
-    scale = jnp.zeros((rows_num, 1), F32)
-    for w in reversed(range(4)):
-        scale = scale + recips[w] ** 3 * dots[w] / (segs[w][1] * groups)
-        scales[w] = scale
-
-    def back(j, carry):
-        for w, (lo, hi) in enumerate(segs):
-            dn = mm_nt(dy_ref[w], w_ref[j, lo:hi, :])
-            g = g_ref[j, :, lo:hi].astype(F32)
-            ggrad_ref[j, :, lo:hi] = jnp.sum(g * dn, axis=0, keepdims=True)
-            dg_ref[j, :, lo:hi] = (gain_ref[j, :, lo:hi] * dn - g * scales[w]).astype(BF16)
-        return carry
-
-    lax.fori_loop(0, groups, back, 0)
-
-
-def middle_call(g, w_all, gain, tok, cot):
-    groups, rows_num, channels = g.shape
-    model = tok.shape[1]
-    return pl.pallas_call(
-        middle_kernel,
-        out_shape=[
-            jax.ShapeDtypeStruct((4, rows_num, model), BF16),
-            jax.ShapeDtypeStruct(g.shape, BF16),
-            jax.ShapeDtypeStruct((4, rows_num, model), BF16),
-            jax.ShapeDtypeStruct(g.shape, BF16),
-            jax.ShapeDtypeStruct((groups, 1, channels), F32),
-        ],
-        compiler_params=pltpu.CompilerParams(vmem_limit_bytes=VMEM_BYTES),
-        cost_estimate=pl.CostEstimate(
-            flops=4 * groups * rows_num * channels * model, bytes_accessed=36 * 2**20, transcendentals=0
-        ),
-        name="nested_norm",
-    )(g, w_all, gain, tok, cot)
-
-
 def partner(axis, bit):
     me = lax.axis_index(axis)
     return me + (1 - 2 * ((me // 2**bit) % 2)) * 2**bit
@@ -149,8 +74,9 @@
     return value.bit_length() - 1
 
 
-def place(count, fixed):
-    return tuple(fixed[b] if b in fixed else slice(None) for b in reversed(range(count)))
+def place(bits, fixed):
+    bits = range(bits) if isinstance(bits, int) else sorted(bits)
+    return tuple(fixed[b] if b in fixed else slice(None) for b in reversed(bits))
 
 
 class Links:
@@ -192,64 +118,128 @@
     lax.fori_loop(0, rows // step, piece, 0)
 
 
-def scatter(links, buf, slots, order, lead=()):
-    count = len(order)
-    mine = bits_of("batch", count)
-    fixed = {}
-    for i, b in enumerate(order):
-        keep = {**fixed, b: mine[b]}
-        copy = links.copy(buf.at[place(count, {**fixed, b: 1 - mine[b]})], slots[i], "batch", partner("batch", b))
-        copy.start()
-        yield
-        copy.wait()
-        dims = slots[i].shape[:-2]
-        for at in itertools.product(*(range(d) for d in dims)):
-            add_block(buf, place(count, keep), slots[i], at)
-        fixed = keep
-
-
-def gather(links, buf, order):
-    count = len(order)
-    fixed = dict(enumerate(bits_of("batch", count)))
-    for b in order:
-        at = buf.at[place(count, fixed)]
-        copy = links.copy(at, at, "batch", partner("batch", b))
-        copy.start()
-        yield
-        copy.wait()
-        fixed = {k: v for k, v in fixed.items() if k != b}
-
-
-def doubling(links, buf, slots, axis, bits):
-    for i, b in enumerate(bits):
-        copy = links.copy(buf, slots[i], axis, partner(axis, b))
-        copy.start()
-        yield
-        copy.wait()
-        buf[...] = (buf[...].astype(F32) + slots[i][...].astype(F32)).astype(buf.dtype)
-
-
-def chain(*parts):
-    for part in parts:
-        yield from part
-
-
-def run_streams(streams):
-    live = list(streams)
-    while live:
-        live = [s for s in live if next(s, live) is not live]
-
-
 def halving_slots(count, block, dtype):
     return [pltpu.VMEM((2,) * (count - 1 - i) + tuple(block), dtype) for i in range(count)]
+
+
+class Stream:
+    def __init__(self, *parts):
+        self.steps = []
+        for part in parts:
+            if self.steps and part:
+                last, first = self.steps.pop(), part[0]
+                self.steps.append(lambda last=last, first=first: (last(), first()))
+                part = part[1:]
+            self.steps.extend(part)
+
+    def advance(self):
+        if self.steps:
+            self.steps.pop(0)()
+
+
+def advance_all(streams):
+    for s in streams:
+        s.advance()
+
+
+def drain(streams):
+    while any(s.steps for s in streams):
+        advance_all(streams)
+
+
+class Ports:
+    def __init__(self, send, recv):
+        self.send, self.recv, self.used = send, recv, 0
+
+    def make(self, src, dst, axis, to):
+        at = self.used
+        self.used += 1
+
+        def describe():
+            return pltpu.make_async_remote_copy(
+                src_ref=src(), dst_ref=dst(), send_sem=self.send.at[at], recv_sem=self.recv.at[at],
+                device_id={axis: to()}, device_id_type=pl.DeviceIdType.MESH,
+            )
+
+        return describe
+
+
+def linked(copies, work):
+    steps = []
+    for i in range(len(copies) + 1):
+        def step(i=i):
+            if i:
+                copies[i - 1]().wait()
+                work(i - 1)
+            if i < len(copies):
+                copies[i]().start()
+
+        steps.append(step)
+    return steps
+
+
+def halving(ports, axis, buf, slots, order):
+    count = len(order)
+
+    def fixed(i, give):
+        mine = bits_of(axis, max(order) + 1)
+        out = {b: mine[b] for b in order[: i + 1]}
+        if give:
+            out[order[i]] = 1 - out[order[i]]
+        return out
+
+    copies = [
+        ports.make(
+            lambda i=i: buf().at[place(order, fixed(i, True))], lambda i=i: slots[i],
+            axis, lambda i=i: partner(axis, order[i]),
+        )
+        for i in range(count)
+    ]
+
+    def work(i):
+        for at in itertools.product(*(range(d) for d in slots[i].shape[:-2])):
+            add_block(buf(), place(order, fixed(i, False)), slots[i], at)
+
+    return linked(copies, work)
+
+
+def spreading(ports, axis, buf, order):
+    count = len(order)
+
+    def at(i):
+        mine = bits_of(axis, count)
+        return buf().at[place(count, {b: mine[b] for b in order[i:]})]
+
+    copies = [
+        ports.make(lambda i=i: at(i), lambda i=i: at(i), axis, lambda i=i: partner(axis, order[i]))
+        for i in range(count)
+    ]
+    return linked(copies, lambda i: None)
+
+
+def exchanging(ports, axis, buf, slots, order):
+    copies = [
+        ports.make(buf, lambda i=i: slots[i], axis, lambda i=i: partner(axis, order[i])) for i in range(len(order))
+    ]
+
+    def work(i):
+        ref = buf()
+        ref[...] = (ref[...].astype(F32) + slots[i][...].astype(F32)).astype(ref.dtype)
+
+    return linked(copies, work)
+
+
+PIECE_POLLS = (
+    ("a", 0), ("a", 1), ("a", 2), ("c", 0), ("d", 1), ("e", 2), ("e", 0), (0, 1), (1, 2), (1, 0), (2, 1), (3, 2),
+)
 
 
 def front_kernel(
     count, tok_ref, pre_ref, zw_hbm, xw_hbm, bcw_hbm, dtw_hbm, w_hbm, gain_hbm,
     convw_ref, convb_ref, dtb_ref, alog_ref, skip_ref,
     x_out, a_out, s_out, act_out, dsc_out, inn_out, bc_out, step_out, prev_out, gated_out, all_ref, gains_ref,
-    xs, zw, xw, bcw, dtw, gate_s, a_s, s_s, act_s, dsc_s, inn_s, inner_s, bc_s, bcb_s, step_s, prev_s, gated_s, state, tails,
-    load_sem, local_sem, store_sem, away_sem, here_sem, send, recv,
+    xs, zw, xw, bcw, dtw, wv, gate_s, a_s, s_s, act_s, dsc_s, inn_s, inner_s, bc_s, bcb_s, step_s, prev_s, gated_s, state, tails,
+    load_sem, local_sem, store_sem, away_sem, here_sem, send, recv, send2, recv2,
 ):
     rows_num, channels = gated_s.shape[1:]
     groups = gated_s.shape[0]
@@ -267,7 +257,7 @@
 
     loads = [
         pltpu.make_async_copy(src, dst, load_sem.at[i])
-        for i, (src, dst) in enumerate(((zw_hbm, zw), (xw_hbm, xw), (bcw_hbm, bcw), (dtw_hbm, dtw)))
+        for i, (src, dst) in enumerate(((zw_hbm, zw), (xw_hbm, xw), (bcw_hbm, bcw), (dtw_hbm, dtw), (w_hbm, wv)))
     ]
     for load in loads:
         load.start()
@@ -284,16 +274,54 @@
         to_far[-1].start()
     to_near = links.copy(own_rows, own_rows, "head", near)
     to_near.start()
-    mine = bits_of("batch", count)
-    own = place(count, dict(enumerate(mine)))
-    keep = [pltpu.make_async_copy(w_hbm, all_ref.at[me], local_sem.at[0])]
-    keep.append(pltpu.make_async_copy(gain_hbm, gains_ref.at[me], local_sem.at[1]))
-    for item in keep:
-        item.start()
+    half = w_hbm.shape[-1] // 2
+
+    def pieces(z, cols, order):
+        def own_piece(ref):
+            return ref.at[place(count, dict(enumerate(bits_of("batch", count)))) + (slice(None), cols)]
+
+        first = ports.make(
+            lambda: own_piece(w_hbm), lambda: own_piece(all_ref.at[lax.axis_index("head")]), "head", z
+        )
+
+        def at(i):
+            bits = bits_of("batch", count)
+            return all_ref.at[(z(),) + place(count, {b: bits[b] for b in order[i:]}) + (slice(None), cols)]
+
+        rest = [
+            ports.make(lambda i=i: at(i), lambda i=i: at(i), "batch", lambda i=i: partner("batch", order[i]))
+            for i in range(count)
+        ]
+        return Stream(linked([first] + rest, lambda i: None))
+
+    up = list(range(1, count))
+    ports = Ports(send2, recv2)
+    near_at = lambda: partner("head", 0)
+    far_at = lambda: partner("head", 1)
+    streams = []
+    for z in (near_at, far_at, lambda: near_at() + far_at() - lax.axis_index("head")):
+        streams.append(pieces(z, pl.ds(0, half), up + [0]))
+        streams.append(pieces(z, pl.ds(half, half), up[::-1] + [0]))
+    plan = [[] for _ in range(groups)]
+    early = {spot: [] for spot in "abcde"}
+    for spot, group in PIECE_POLLS:
+        for st in streams[2 * group : 2 * group + 2]:
+            if st.steps:
+                (early[spot] if spot in early else plan[spot]).append(st.steps.pop(0))
+
+    def poll(spot):
+        for action in early[spot]:
+            action()
+
+    poll("a")
+    keep = [pltpu.make_async_copy(gain_hbm, gains_ref.at[me], local_sem.at[1])]
+    keep[0].start()
     inner_s[0:8, :] = jnp.zeros((8, channels), F32)
     state[...] = jnp.zeros_like(state)
     for load in loads:
         load.wait()
+    keep.append(pltpu.make_async_copy(wv, all_ref.at[me], local_sem.at[0]))
+    keep[-1].start()
 
     def project(at_hi, at_lo):
         first = pl.multiple_of((2 * at_hi + at_lo) * rows_num, rows_num)
@@ -316,6 +344,7 @@
     project(hi, lo)
     to_near.wait()
     project(hi, 1 - lo)
+    poll("b")
     onward = []
     for c in range(chunks):
         to_far[c].wait()
@@ -323,39 +352,17 @@
         onward.append(links.copy(part, part, "head", near))
         onward[-1].start()
 
-    half = w_hbm.shape[-1] // 2
-
-    def pieces(z, cols, order):
-        copy = links.copy(
-            w_hbm.at[own + (slice(None), cols)], all_ref.at[(me,) + own + (slice(None), cols)], "head", z
-        )
-        copy.start()
-        yield
-        copy.wait()
-        fixed = dict(enumerate(mine))
-        for b in order:
-            at = all_ref.at[(z,) + place(count, fixed) + (slice(None), cols)]
-            step = links.copy(at, at, "batch", partner("batch", b))
-            step.start()
-            yield
-            step.wait()
-            fixed = {k: v for k, v in fixed.items() if k != b}
-
-    up = list(range(1, count))
-    streams = []
-    for z in others:
-        streams.append(pieces(z, pl.ds(0, half), up + [0]))
-        streams.append(pieces(z, pl.ds(half, half), up[::-1] + [0]))
-    for s in streams:
-        next(s)
+    poll("c")
     gain_sends = [links.copy(gain_hbm, gains_ref.at[me], "head", z) for z in others]
     for item in gain_sends:
         item.start()
 
     project(1 - hi, lo)
+    poll("d")
     for item in onward:
         item.wait()
     project(1 - hi, 1 - lo)
+    poll("e")
 
     rate = -jnp.exp(alog_ref[...])
     lower = lower_mask((SPAN, SPAN))
@@ -447,12 +454,17 @@
 
         for item in stores(q):
             item.start()
+        for k in range(groups):
+            @pl.when(q == k)
+            def _():
+                for action in plan[k]:
+                    action()
         return carry
 
     lax.fori_loop(0, groups, quarter_step, 0)
     stay = pltpu.make_async_copy(gated_s.at[me], gated_out.at[me], local_sem.at[2])
     stay.start()
-    run_streams(streams)
+    drain(streams)
     for item in gain_sends:
         item.wait()
     for item in keep:
@@ -479,7 +491,8 @@
     length = rows_num * groups
     count = log2(batches)
     part = channels // batches
-    copies = 3 + 2 + (groups - 1) * (1 + 2 * (1 + count))
+    copies = 5 + groups - 1
+    piece_copies = 2 * (groups - 1) * (1 + count)
     hbm = pl.BlockSpec(memory_space=pl.ANY)
     vmem = pl.BlockSpec(memory_space=pltpu.VMEM)
     wide = jax.ShapeDtypeStruct((length, channels), BF16)
@@ -502,6 +515,7 @@
             pltpu.VMEM((2, 2, rows_num, model), BF16),
             pltpu.VMEM(zw.shape, BF16), pltpu.VMEM(xw.shape, BF16),
             pltpu.VMEM(bcw.shape, BF16), pltpu.VMEM(dtw.shape, BF16),
+            pltpu.VMEM((2,) * count + (part, model), BF16),
             pltpu.VMEM((length, channels), F32),
             pltpu.VMEM((length, channels), BF16), pltpu.VMEM((length, channels), BF16),
             pltpu.VMEM((length, channels), BF16), pltpu.VMEM((length, channels), BF16),
@@ -510,7 +524,8 @@
             pltpu.VMEM((length, dtw.shape[1]), F32), pltpu.VMEM((length // SPAN, n, channels), BF16),
             pltpu.VMEM((groups, rows_num, channels), BF16),
             pltpu.VMEM((n, channels), F32), pltpu.VMEM((SPAN, channels), BF16),
-            dma((4,)), dma((3,)), dma((9, groups)), dma((groups,)), dma((groups,)), dma((copies,)), dma((copies,)),
+            dma((5,)), dma((3,)), dma((9, groups)), dma((groups,)), dma((groups,)), dma((copies,)), dma((copies,)),
+            dma((piece_copies,)), dma((piece_copies,)),
         ],
         compiler_params=pltpu.CompilerParams(
             collective_id=1, has_side_effects=True, vmem_limit_bytes=VMEM_BYTES
@@ -524,167 +539,245 @@
         jnp.broadcast_to(norm_gain[None], (8, channels)), convw, convb, dtb, alog, skip,
     )
     x, a, s, act, dsc, inn, bc, step, prev, gated, w_all, gains = result
-    return x, (a, s, act, dsc, inn), bc, step, prev, gated, w_all.reshape(groups, channels, model), gains[:, :1]
-
-
-def outgrad_scatter_kernel(count, gg_ref, dy_ref, out_ref, *refs):
-    buf, send, recv = refs[0], refs[-2], refs[-1]
-    streams_num = 4
-    slots = [refs[1 + s * count : 1 + (s + 1) * count] for s in range(streams_num)]
-    groups, _, channels = gg_ref.shape
-    part, cols = buf.shape[-2:]
-    model = dy_ref.shape[2]
-    links = Links(send, recv)
-    meet([("batch", partner("batch", b)) for b in range(count)])
+    return x, (a, s, act, dsc, inn), bc, step, prev, gated, w_all.reshape(groups, channels, model), gains
+
+
+def middle_kernel(
+    count, g_hbm, w_hbm, cot_hbm, gain_ref, tok_ref,
+    out_hbm, dg_out, part_ref, ggrad_ref,
+    g_s, w_s, cot_s, gg_s, out_s, dg_s, give_s, kept_s, *refs,
+):
+    slots = [refs[i * (count - 1) : (i + 1) * (count - 1)] for i in range(4)]
+    load_sem, store_sem, away_sem, here_sem, send, recv = refs[4 * (count - 1) :]
+    groups, rows_num, channels = g_s.shape
+    model = tok_ref.shape[1]
+    part, half = kept_s.shape[-2:]
+    pairs_num = groups // 2
+    segs = segments(channels)
+    tile = 512
+    tiles = model // tile
+    me = lax.axis_index("head")
+
+    def w_load(t):
+        cols = pl.ds(pl.multiple_of(t * tile, tile), tile)
+        return pltpu.make_async_copy(w_hbm.at[:, :, cols], w_s.at[:, :, cols], load_sem.at[2 + t])
+
+    loads = [
+        pltpu.make_async_copy(g_hbm, g_s, load_sem.at[0]), pltpu.make_async_copy(cot_hbm, cot_s, load_sem.at[1]),
+    ]
+    loads[0].start()
+    w_load(0).start()
+    loads[1].start()
+    for t in range(1, tiles):
+        w_load(t).start()
+    loads[0].wait()
+    sums = [jnp.zeros((rows_num, 1), F32) for _ in segs]
+    for j in range(groups):
+        for w, (lo, hi) in enumerate(segs):
+            g = g_s[j, :, lo:hi].astype(F32)
+            gg_s[j, :, lo:hi] = (g * gain_ref[j, 0:1, lo:hi]).astype(BF16)
+            sums[w] += jnp.sum(g * g, axis=1, keepdims=True)
+    recips = []
+    total = jnp.zeros((rows_num, 1), F32)
+    for w, (lo, hi) in enumerate(segs):
+        total = total + sums[w]
+        recips.append(lax.rsqrt(total / (hi * groups) + EPSILON))
+    meet(
+        [("batch", partner("batch", b)) for b in range(count)]
+        + [("head", z) for z in (partner("head", 0), partner("head", 1), partner("head", 0) + partner("head", 1) - me)]
+    )
+    loads[1].wait()
+
+    def out_store(t):
+        cols = pl.ds(pl.multiple_of(t * tile, tile), tile)
+        return pltpu.make_async_copy(out_s.at[:, :, cols], out_hbm.at[:, :, cols], store_sem.at[t])
+
+    def forward(t, dots):
+        cols = pl.ds(pl.multiple_of(t * tile, tile), tile)
+        w_load(t).wait()
+        acc = jnp.zeros((rows_num, tile), F32)
+        tok = tok_ref[:, cols].astype(F32)
+        new = []
+        for w, (lo, hi) in enumerate(segs):
+            acc += mm(
+                jnp.concatenate([gg_s[j, :, lo:hi] for j in range(groups)], axis=1),
+                jnp.concatenate([w_s[j, lo:hi, cols] for j in range(groups)], axis=0),
+            )
+            out_s[w, :, cols] = (tok + recips[w] * acc).astype(BF16)
+            new.append(dots[w] + jnp.sum(cot_s[w, :, cols].astype(F32) * acc, axis=1, keepdims=True))
+        out_store(t).start()
+        combined = jnp.zeros((rows_num, tile), F32)
+        for w in reversed(range(4)):
+            combined += recips[w] * cot_s[w, :, cols].astype(F32)
+            cot_s[w, :, cols] = combined.astype(BF16)
+        return tuple(new)
+
+    dots = lax.fori_loop(0, tiles, forward, tuple(jnp.zeros((rows_num, 1), F32) for _ in segs))
+    dy_s = cot_s
+    scales = [None] * 4
+    scale = jnp.zeros((rows_num, 1), F32)
+    for w in reversed(range(4)):
+        scale = scale + recips[w] ** 3 * dots[w] / (segs[w][1] * groups)
+        scales[w] = scale
+
+    def leave(j):
+        return pltpu.make_async_remote_copy(
+            src_ref=dg_s.at[j], dst_ref=dg_out.at[me], send_sem=away_sem.at[j], recv_sem=here_sem.at[me],
+            device_id={"head": j}, device_id_type=pl.DeviceIdType.MESH,
+        )
+
+    def arrive(j):
+        return pltpu.make_async_remote_copy(
+            src_ref=dg_s.at[j], dst_ref=dg_out.at[j], send_sem=away_sem.at[j], recv_sem=here_sem.at[j],
+            device_id={"head": j}, device_id_type=pl.DeviceIdType.MESH,
+        )
+
+    def back(k, carry):
+        j = (me + 1 + k) % groups
+        for w, (lo, hi) in enumerate(segs):
+            dn = mm_nt(dy_s[w], w_s[j, lo:hi, :])
+            g = g_s[j, :, lo:hi].astype(F32)
+            ggrad_ref[j, :, lo:hi] = jnp.sum(g * dn, axis=0, keepdims=True)
+            dg_s[j, :, lo:hi] = (gain_ref[j, 0:1, lo:hi] * dn - g * scales[w]).astype(BF16)
+
+        @pl.when(j != me)
+        def _():
+            leave(j).start()
+
+        return carry
+
+    ports = Ports(send, recv)
     up = list(range(1, count))
-
-    def stream(s):
-        g0, c0 = (s // 2) * (groups // 2), (s % 2) * cols
-        for j in range(groups // 2):
-            for w, (lo, hi) in enumerate(segments(channels)):
-                term = mm_tn(gg_ref[g0 + j, :, lo:hi], dy_ref[w, :, c0 : c0 + cols]).astype(BF16)
+    core = bits_of("batch", 1)[0]
+
+    def upper_index(p):
+        return tuple((p >> b) & 1 for b in reversed(range(1, count)))
+
+    def terms(s, bit, use):
+        g0, c0 = (s // 2) * pairs_num, (s % 2) * half
+        if part % 128 == 0:
+            for q in range(2 ** (count - 1)):
+                at = pl.ds(pl.multiple_of((2 * q + bit) * part, part), part)
+                left = jnp.concatenate([gg_s[g0 + j, :, at] for j in range(pairs_num)], axis=1)
+                owners = [[w for w, (lo, hi) in enumerate(segs) if lo <= (2 * q + c) * part < hi][0] for c in range(2)]
+                w = owners[0] + (owners[1] - owners[0]) * bit
+                term = mm_tn(left, dy_s[w, :, c0 : c0 + half])
+                for j in range(pairs_num):
+                    use(upper_index(2 * q), j, term[j * part : (j + 1) * part])
+            return
+        for j in range(pairs_num):
+            for w, (lo, hi) in enumerate(segs):
+                term = mm_tn(gg_s[g0 + j, :, lo:hi], dy_s[w, :, c0 : c0 + half])
                 for p in range(lo // part, hi // part):
-                    index = tuple((p >> b) & 1 for b in reversed(range(count)))
-                    buf[(s,) + index + (j,)] = term[p * part - lo : (p + 1) * part - lo]
-        order = [0] + (up if s % 2 == 0 else up[::-1])
-        yield from scatter(links, buf.at[s], slots[s], order)
-        mine = place(count, dict(enumerate(bits_of("batch", count))))
-        for j in range(groups // 2):
-            out_ref[g0 + j, :, c0 : c0 + cols] = buf[(s,) + mine + (j,)]
-
-    run_streams([stream(s) for s in range(streams_num)])
-
-
-def outgrad_scatter_call(gg, dy, batches):
-    groups, _, channels = gg.shape
-    model = dy.shape[2]
+                    @pl.when(bit == p % 2)
+                    def _():
+                        use(upper_index(p), j, term[p * part - lo : (p + 1) * part - lo])
+
+    def to_core(s):
+        return pltpu.make_async_remote_copy(
+            src_ref=give_s.at[s], dst_ref=kept_s.at[s], send_sem=send.at[s], recv_sem=recv.at[s],
+            device_id={"batch": partner("batch", 0)}, device_id_type=pl.DeviceIdType.MESH,
+        )
+
+    def give(s):
+        def use(index, j, rows):
+            give_s[(s,) + index + (j,)] = rows.astype(BF16)
+
+        terms(s, 1 - core, use)
+        to_core(s).start()
+
+    def keep(s):
+        to_core(s).wait()
+
+        def use(index, j, rows):
+            at = (s,) + index + (j,)
+            kept_s[at] = (kept_s[at].astype(F32) + rows).astype(BF16)
+
+        terms(s, core, use)
+
+    ports.used = 4
+    streams = [
+        Stream(halving(ports, "batch", lambda s=s: kept_s.at[s], slots[s], up if s % 2 == 0 else up[::-1]))
+        for s in range(4)
+    ]
+    for s in range(2):
+        give(s)
+    for s in range(2):
+        keep(s)
+        streams[s].advance()
+    lax.fori_loop(0, groups, back, 0)
+    stay = pltpu.make_async_copy(dg_s.at[me], dg_out.at[me], load_sem.at[0])
+    stay.start()
+    for s in range(2, 4):
+        give(s)
+    advance_all(streams[:2])
+    for s in range(2, 4):
+        keep(s)
+        streams[s].advance()
+    drain(streams)
+    mine = bits_of("batch", count)
+    own = place(up, {b: mine[b] for b in up})
+    for s in range(4):
+        for j in range(pairs_num):
+            part_ref[(s // 2) * pairs_num + j, :, (s % 2) * half : (s % 2 + 1) * half] = kept_s[(s,) + own + (j,)]
+    stay.wait()
+
+    def finish(j, carry):
+        @pl.when(j != me)
+        def _():
+            leave(j).wait_send()
+            arrive(j).wait_recv()
+
+        return carry
+
+    lax.fori_loop(0, groups, finish, 0)
+
+    def stored(t, carry):
+        out_store(t).wait()
+        return carry
+
+    lax.fori_loop(0, tiles, stored, 0)
+
+
+def middle_call(g, w_all, gain, tok, cot, batches):
+    groups, rows_num, channels = g.shape
+    model = tok.shape[1]
     count = log2(batches)
     part = channels // batches
-    block = (groups // 2, part, model // 2)
+    half = model // 2
+    block = (groups // 2, part, half)
+    hbm = pl.BlockSpec(memory_space=pl.ANY)
     vmem = pl.BlockSpec(memory_space=pltpu.VMEM)
+    dma = pltpu.SemaphoreType.DMA
+    wide = pltpu.VMEM((groups, rows_num, channels), BF16)
+    tall = pltpu.VMEM((4, rows_num, model), BF16)
+    halves = pltpu.VMEM((4,) + (2,) * (count - 1) + block, BF16)
     return pl.pallas_call(
-        functools.partial(outgrad_scatter_kernel, count),
-        in_specs=[vmem, vmem],
-        out_specs=vmem,
-        out_shape=jax.ShapeDtypeStruct((groups, part, model), BF16),
-        scratch_shapes=[pltpu.VMEM((4,) + (2,) * count + block, BF16)]
-        + [s for _ in range(4) for s in halving_slots(count, block, BF16)]
-        + [pltpu.SemaphoreType.DMA((4 * count,)), pltpu.SemaphoreType.DMA((4 * count,))],
+        functools.partial(middle_kernel, count),
+        in_specs=[hbm] * 3 + [vmem] * 2,
+        out_specs=[hbm, hbm, vmem, vmem],
+        out_shape=[
+            jax.ShapeDtypeStruct((4, rows_num, model), BF16),
+            jax.ShapeDtypeStruct(g.shape, BF16),
+            jax.ShapeDtypeStruct((groups, part, model), BF16),
+            jax.ShapeDtypeStruct((groups, 1, channels), F32),
+        ],
+        scratch_shapes=[
+            wide, pltpu.VMEM((groups, channels, model), BF16), tall, wide, tall, wide, halves, halves,
+        ]
+        + [s for _ in range(4) for s in halving_slots(count - 1, block, BF16)]
+        + [
+            dma((2 + model // 512,)), dma((model // 512,)), dma((groups,)), dma((groups,)),
+            dma((4 * count,)), dma((4 * count,)),
+        ],
         compiler_params=pltpu.CompilerParams(
             collective_id=2, has_side_effects=True, vmem_limit_bytes=VMEM_BYTES
         ),
         cost_estimate=pl.CostEstimate(
-            flops=2 * groups * gg.shape[1] * channels * model, bytes_accessed=200 * 2**20, transcendentals=0
+            flops=6 * groups * rows_num * channels * model, bytes_accessed=200 * 2**20, transcendentals=0
         ),
-        name="out_weight_grad",
-    )(gg, dy)
-
-
-class Stream:
-    def __init__(self, *parts):
-        self.steps = []
-        for part in parts:
-            if self.steps and part:
-                last, first = self.steps.pop(), part[0]
-                self.steps.append(lambda last=last, first=first: (last(), first()))
-                part = part[1:]
-            self.steps.extend(part)
-
-    def advance(self):
-        if self.steps:
-            self.steps.pop(0)()
-
-
-def advance_all(streams):
-    for s in streams:
-        s.advance()
-
-
-def drain(streams):
-    while any(s.steps for s in streams):
-        advance_all(streams)
-
-
-class Ports:
-    def __init__(self, send, recv):
-        self.send, self.recv, self.used = send, recv, 0
-
-    def make(self, src, dst, axis, to):
-        at = self.used
-        self.used += 1
-
-        def describe():
-            return pltpu.make_async_remote_copy(
-                src_ref=src(), dst_ref=dst(), send_sem=self.send.at[at], recv_sem=self.recv.at[at],
-                device_id={axis: to()}, device_id_type=pl.DeviceIdType.MESH,
-            )
-
-        return describe
-
-
-def linked(copies, work):
-    steps = []
-    for i in range(len(copies) + 1):
-        def step(i=i):
-            if i:
-                copies[i - 1]().wait()
-                work(i - 1)
-            if i < len(copies):
-                copies[i]().start()
-
-        steps.append(step)
-    return steps
-
-
-def halving(ports, axis, buf, slots, order):
-    count = len(order)
-
-    def fixed(i, give):
-        mine = bits_of(axis, count)
-        out = {b: mine[b] for b in order[: i + 1]}
-        if give:
-            out[order[i]] = 1 - out[order[i]]
-        return out
-
-    copies = [
-        ports.make(
-            lambda i=i: buf().at[place(count, fixed(i, True))], lambda i=i: slots[i],
-            axis, lambda i=i: partner(axis, order[i]),
-        )
-        for i in range(count)
-    ]
-
-    def work(i):
-        for at in itertools.product(*(range(d) for d in slots[i].shape[:-2])):
-            add_block(buf(), place(count, fixed(i, False)), slots[i], at)
-
-    return linked(copies, work)
-
-
-def spreading(ports, axis, buf, order):
-    count = len(order)
-
-    def at(i):
-        mine = bits_of(axis, count)
-        return buf().at[place(count, {b: mine[b] for b in order[i:]})]
-
-    copies = [
-        ports.make(lambda i=i: at(i), lambda i=i: at(i), axis, lambda i=i: partner(axis, order[i]))
-        for i in range(count)
-    ]
-    return linked(copies, lambda i: None)
-
-
-def exchanging(ports, axis, buf, slots, order):
-    copies = [
-        ports.make(buf, lambda i=i: slots[i], axis, lambda i=i: partner(axis, order[i])) for i in range(len(order))
-    ]
-
-    def work(i):
-        ref = buf()
-        ref[...] = (ref[...].astype(F32) + slots[i][...].astype(F32)).astype(ref.dtype)
-
-    return linked(copies, work)
+        name="nested_norm",
+    )(g, w_all, cot, gain, tok)
 
 
 def back_kernel(
@@ -1225,9 +1318,7 @@
         tokens, pre_gain, z_weight, x_weight, bc_weight, dtw, out_weight, norm_gain,
         conv_weight, conv_bias[None], dtb, alog, skip_r, groups, batches,
     )
-    outputs, d_gated, dy, gg, gain_grad = middle_call(gated, w_all, gain_all, tokens, cot)
-    d_gated = lax.all_to_all(d_gated, "head", 0, 0, tiled=True)
-    out_part = outgrad_scatter_call(gg, dy, batches)
+    outputs, d_gated, out_part, gain_grad = middle_call(gated, w_all, gain_all, tokens, cot, batches)
     hot = (jnp.arange(channels)[None] // (channels // heads) == jnp.arange(heads)[:, None]).astype(BF16)
     z_grad, x_grad, out_grad, bcdt_grad, small, d_own = back_call(
         d_gated, res, x, bc, step, prev, z_weight, x_weight, bc_weight, dtw, out_part, gain_grad,

time: 495 us -> 475 us (0.960)
  Pallas kernels: 479 us -> 460 us
    pallas_call x1, Pallas kernels: 184 us -> 161 us  [front_call(): pl.pallas_call(functools.partial(front_kernel, count), in_specs=[vmem, vm...]
    pallas_call x2 -> x1, Pallas kernels: 110 us -> 119 us  [middle_call(): pl.pallas_call(functools.partial(middle_kernel, count), in_specs=[hbm] *...]
  transfers between devices with their start and end apart: 1 -> 0, of which waited for: 0 -> 0; matrix products, arithmetic and copies ran while one was open for 0% -> 0% of each run, Pallas kernels for 17% -> 0%
where the time goes in v4:
time: 475 us; the launch traced here: 474 us
  Pallas kernels  460 us (97%)
  local copies, waits for them, and re-layouts  12.6 us (3%)
    pallas_call x1, Pallas kernels, back_call(): pl.pallas_call(functools.partial(back_kernel, count, group_bits), in_spec...  163 us
    pallas_call x1, Pallas kernels, front_call(): pl.pallas_call(functools.partial(front_kernel, count), in_specs=[vmem, vm...  161 us
    pallas_call x1, Pallas kernels, middle_call(): pl.pallas_call(functools.partial(middle_kernel, count), in_specs=[hbm] *...  119 us
    pallas_call x1, Pallas kernels, finish_call(): pl.pallas_call(finish_kernel, grid=(steps,), in_specs=[rows(model, channe...  18.2 us

profile of v4, /device:TPU:0, one launch (start us, length us, event | category | flops | bytes accessed | tf_op | source)
XLA Modules:
  0.0 474.4 jit_solution(14250822316041667253)
XLA Ops:
  0.6 1.2 pad.12.dtb_ref
  1.8 1.2 pad.13.alog_ref
  3.0 0.6 fusion.hot_ref
  3.6 1.3 broadcast_in_dim.31.gain_hbm
  4.9 1.1 copy.28
  6.0 0.9 pad.11.dtw_hbm
  6.9 160.7 %front.1 = (bf16[1024,2048]{1,0:T(8,128)(2,1)}, bf16[1024,1024]{1,0:T(8,128)(2,1)}, bf16[1024,1024]{1,0:T(8,128)(2,1)}, bf16[1024,1024]{1,0:T(8,128)(2,1)}, bf16...) custom-call(bf16[256,2048]{1,0:T(8,128)(2,1)} %bitcast.32, ...), custom_call_target="tpu_custom_call" | custom-call | flops 8589934592 | bytes 419430400 | tf_op jit(solution)/shard_map/front/pallas_call | solution.py:509
  167.7 118.6 %nested_norm.1 = (bf16[4,256,2048]{2,1,0:T(8,128)(2,1)}, bf16[4,256,1024]{2,1,0:T(8,128)(2,1)}, bf16[4,128,2048]{2,1,0:T(8,128)(2,1)}, f32[4,1,1024]{2,1,0:T(1,128)}) custom-call(bf16[4,256,1024]{2,1,0:T(8,128)(2,1)} %get-tuple-element.49.g_hbm, bf16[4,1024,2048]{2,1,0:T(8,128)(2,1)} %bitcast.51, bf16[4,256,2048]{2,1,0:T(8,128)(2,1)} %bitcast.25, ...), custom_call_target="tpu_custom_call" | custom-call | flops 12884901888 | bytes 209715200 | tf_op jit(solution)/shard_map/nested_norm/pallas_call | solution.py:755
  286.3 163.0 %back.1 = (bf16[2,2,2,256,1024]{4,3,2,1,0:T(8,128)(2,1)}, bf16[2,2,2,256,1024]{4,3,2,1,0:T(8,128)(2,1)}, bf16[2,2,2,128,2048]{4,3,2,1,0:T(8,128)(2,1)}, bf16[2,2...) custom-call(bf16[4,256,1024]{2,1,0:T(8,128)(2,1)} %get-tuple-element.53.dg_hbm, ...), custom_call_target="tpu_custom_call" | custom-call | flops 21474836480 | bytes 314572800 | tf_op jit(solution)/shard_map/back/pallas_call | solution.py:1182
  449.3 18.2 %finish.1 = (f32[2048,1024]{1,0:T(8,128)}, f32[2048,1024]{1,0:T(8,128)}, f32[1024,2048]{1,0:T(8,128)}, f32[2048,256]{1,0:T(8,128)}, f32[2048,16]{1,0:T(8,128)}, ...) custom-call(bf16[2048,1024]{1,0:T(8,128)(2,1)} %bitcast.27, ...), custom_call_target="tpu_custom_call" | custom-call | bytes 48234496 | tf_op jit(solution)/shard_map/finish/pallas_call | solution.py:1284
  467.4 2.2 copy.30
  469.6 4.8 %copy.32 = bf16[4,1,256,2048]{3,2,1,0:T(8,128)(2,1)} copy(bf16[4,1,256,2048]{3,2,1,0:T(8,128)(2,1)} %bitcast.30) | data formatting | bytes 8388608
  (1 shorter events, 0.0 us)

commit v5 on v4

--- a/solution.py
+++ b/solution.py
@@ -9,7 +9,10 @@
 from jax.sharding import PartitionSpec as P
 
 SPAN = 128
-ROWS = 256
+HEAD_PARTS = 2
+ROW_CHUNKS = 4
+BACK_PARTS = 1
+X_STREAMS = 4
 EPSILON = 1e-05
 BF16 = jnp.bfloat16
 F32 = jnp.float32
@@ -203,18 +206,31 @@
     return linked(copies, work)
 
 
-def spreading(ports, axis, buf, order):
+def spreading(ports, axis, view, order, own, sem):
     count = len(order)
 
     def at(i):
         mine = bits_of(axis, count)
-        return buf().at[place(count, {b: mine[b] for b in order[i:]})]
+        return view().at[place(count, {b: mine[b] for b in order[i:]})]
 
     copies = [
-        ports.make(lambda i=i: at(i), lambda i=i: at(i), axis, lambda i=i: partner(axis, order[i]))
+        ports.make(
+            (lambda i=i: at(i)) if i else own, lambda i=i: at(i), axis, lambda i=i: partner(axis, order[i])
+        )
         for i in range(count)
     ]
-    return linked(copies, lambda i: None)
+
+    def kept():
+        return pltpu.make_async_copy(own(), at(0), sem)
+
+    def work(i):
+        if i == 0:
+            kept().wait()
+
+    steps = linked(copies, work)
+    first = steps[0]
+    steps[0] = lambda: (kept().start(), first())
+    return steps
 
 
 def exchanging(ports, axis, buf, slots, order):
@@ -230,7 +246,7 @@
 
 
 PIECE_POLLS = (
-    ("a", 0), ("a", 1), ("a", 2), ("c", 0), ("d", 1), ("e", 2), ("e", 0), (0, 1), (1, 2), (1, 0), (2, 1), (3, 2),
+    ("a", 0), ("a", 1), ("a", 2), ("c", 0), ("d", 1), ("e", 2), ("e", 0), (1, 1), (3, 2), (3, 0), (5, 1), (7, 2),
 )
 
 
@@ -239,7 +255,7 @@
     convw_ref, convb_ref, dtb_ref, alog_ref, skip_ref,
     x_out, a_out, s_out, act_out, dsc_out, inn_out, bc_out, step_out, prev_out, gated_out, all_ref, gains_ref,
     xs, zw, xw, bcw, dtw, wv, gate_s, a_s, s_s, act_s, dsc_s, inn_s, inner_s, bc_s, bcb_s, step_s, prev_s, gated_s, state, tails,
-    load_sem, local_sem, store_sem, away_sem, here_sem, send, recv, send2, recv2,
+    cum_s, cum_t_s, inner_prod_s, b_t_s, pad_s, load_sem, local_sem, store_sem, away_sem, here_sem, send, recv, send2, recv2,
 ):
     rows_num, channels = gated_s.shape[1:]
     groups = gated_s.shape[0]
@@ -302,7 +318,7 @@
     for z in (near_at, far_at, lambda: near_at() + far_at() - lax.axis_index("head")):
         streams.append(pieces(z, pl.ds(0, half), up + [0]))
         streams.append(pieces(z, pl.ds(half, half), up[::-1] + [0]))
-    plan = [[] for _ in range(groups)]
+    plan = [[] for _ in range(HEAD_PARTS * groups)]
     early = {spot: [] for spot in "abcde"}
     for spot, group in PIECE_POLLS:
         for st in streams[2 * group : 2 * group + 2]:
@@ -318,6 +334,10 @@
     keep[0].start()
     inner_s[0:8, :] = jnp.zeros((8, channels), F32)
     state[...] = jnp.zeros_like(state)
+    step_s[...] = jnp.zeros_like(step_s)
+    pad_s[...] = jnp.zeros_like(pad_s)
+    pad_s[0:1, 0 : dtw.shape[0]] = dtb_ref[...]
+    pad_s[1:2, 0 : dtw.shape[0]] = alog_ref[...]
     for load in loads:
         load.wait()
     keep.append(pltpu.make_async_copy(wv, all_ref.at[me], local_sem.at[0]))
@@ -339,7 +359,7 @@
         lax.fori_loop(0, channels // tile, columns, 0)
         x = xs[at_hi, at_lo]
         bc_s[rows, :] = mm(x, bcw[...])
-        step_s[rows, :] = mm(x, dtw[...])
+        step_s[rows, 0 : dtw.shape[0]] = mm_nt(x, dtw[...])
 
     project(hi, lo)
     to_near.wait()
@@ -364,28 +384,37 @@
     project(1 - hi, 1 - lo)
     poll("e")
 
-    rate = -jnp.exp(alog_ref[...])
+    rate = -jnp.exp(pad_s[1:2, :])
     lower = lower_mask((SPAN, SPAN))
     lower_f = lower.astype(F32)
     left = lax.broadcasted_iota(jnp.int32, (SPAN, 128), 1) < 64
 
-    def block(at, carry):
+    span_num = channels // HEAD_PARTS
+
+    def block(at, part):
         first = pl.multiple_of(at * SPAN, SPAN)
         rows = pl.ds(first, SPAN)
-        delta = softplus(step_s[rows, :] + dtb_ref[...])
-        cum = mm_exact(lower_f, delta * rate)
-        cum_t = cum.T
-        bcb_s[rows, :] = bc_s[rows, :].astype(BF16)
-        b_val = bcb_s[rows, :n]
-        c_val = bcb_s[rows, n:]
-        inner = jnp.where(lower, mm_nt(c_val, b_val), 0.0)
-        before = state[...].astype(BF16)
-        prev_s[at] = before
-        across = mm(c_val, before)
+        if part == 0:
+            delta = softplus(step_s[rows, :] + pad_s[0:1, :])
+            cum = mm_exact(lower_f, delta * rate)
+            cum_t = cum.T
+            bcb_s[rows, :] = bc_s[rows, :].astype(BF16)
+            inner = jnp.where(lower, mm_nt(bcb_s[rows, n:], bcb_s[rows, :n]), 0.0)
+            b_t = bc_s[rows, :n].T.astype(BF16)
+            step_s[rows, :] = delta
+            cum_s[at], cum_t_s[at], inner_prod_s[at], b_t_s[at] = cum, cum_t, inner, b_t
+        else:
+            delta = step_s[rows, :]
+            cum, cum_t, inner, b_t = cum_s[at], cum_t_s[at], inner_prod_s[at], b_t_s[at]
+        span_cols = pl.ds(part * span_num, span_num)
+        before = state[:, span_cols].astype(BF16)
+        prev_s[at, :, span_cols] = before
+        across = mm(bcb_s[rows, n:], before)
         quarter = at // (rows_num // SPAN)
         sub = pl.ds(pl.multiple_of((at % (rows_num // SPAN)) * SPAN, SPAN), SPAN)
-        for pair in range(channels // 128):
+        for pair in range(part * span_num // 128, (part + 1) * span_num // 128):
             cols = slice(pair * 128, pair * 128 + 128)
+            local = slice(pair * 128 - part * span_num, pair * 128 + 128 - part * span_num)
             c0, c1, ce = pair_columns(cum, pair, left)
             _, _, de = pair_columns(delta, pair, left)
             tot = ce[SPAN - 1 : SPAN, :]
@@ -399,13 +428,13 @@
             act_s[rows, cols] = act.astype(BF16)
             dsc_s[rows, cols] = (sc + act * (1.0 - sc)).astype(BF16)
             u = act * de
-            tails[:, cols] = (u * jnp.exp(tot - ce)).astype(BF16)
+            tails[:, local] = (u * jnp.exp(tot - ce)).astype(BF16)
             u0 = jnp.where(left, u, 0.0).astype(BF16)
             u1 = jnp.where(left, 0.0, u).astype(BF16)
             p0 = (jnp.exp(jnp.minimum(c0 - cum_t[2 * pair : 2 * pair + 1, :], 0.0)) * inner).astype(BF16)
             p1 = (jnp.exp(jnp.minimum(c1 - cum_t[2 * pair + 1 : 2 * pair + 2, :], 0.0)) * inner).astype(BF16)
             within = mm(jnp.concatenate([p0, p1], axis=1), jnp.concatenate([u0, u1], axis=0))
-            y = within + across[:, cols] * jnp.exp(ce) + skip_ref[:, cols] * act
+            y = within + across[:, local] * jnp.exp(ce) + skip_ref[:, cols] * act
             gate = gate_s[rows, cols]
             sg = sigmoid(gate)
             sl = gate * sg
@@ -413,18 +442,21 @@
             a_s[rows, cols] = (y * (sg + sl * (1.0 - sg))).astype(BF16)
             gated_s[quarter, sub, cols] = (y * sl).astype(BF16)
             state[:, cols] = state[:, cols] * jnp.exp(tot)
-        state[...] += mm(bc_s[rows, :n].T.astype(BF16), tails[...])
-        return carry
-
-    def leave(q):
+        state[:, span_cols] += mm(b_t, tails[...])
+
+    def leave(q, part):
+        cols = pl.ds(part * span_num, span_num)
         return pltpu.make_async_remote_copy(
-            src_ref=gated_s.at[q], dst_ref=gated_out.at[me], send_sem=away_sem.at[q], recv_sem=here_sem.at[me],
+            src_ref=gated_s.at[q, :, cols], dst_ref=gated_out.at[me, :, cols],
+            send_sem=away_sem.at[part, q], recv_sem=here_sem.at[part, me],
             device_id={"head": q}, device_id_type=pl.DeviceIdType.MESH,
         )
 
-    def arrive(q):
+    def arrive(q, part):
+        cols = pl.ds(part * span_num, span_num)
         return pltpu.make_async_remote_copy(
-            src_ref=gated_s.at[q], dst_ref=gated_out.at[q], send_sem=away_sem.at[q], recv_sem=here_sem.at[q],
+            src_ref=gated_s.at[q, :, cols], dst_ref=gated_out.at[q, :, cols],
+            send_sem=away_sem.at[part, q], recv_sem=here_sem.at[part, q],
             device_id={"head": q}, device_id_type=pl.DeviceIdType.MESH,
         )
 
@@ -445,23 +477,29 @@
         )
         return [pltpu.make_async_copy(src, dst, store_sem.at[i, q]) for i, (src, dst) in enumerate(pairs)]
 
-    def quarter_step(q, carry):
-        lax.fori_loop(q * subs, (q + 1) * subs, block, 0)
-
-        @pl.when(q != me)
-        def _():
-            leave(q).start()
-
-        for item in stores(q):
-            item.start()
-        for k in range(groups):
-            @pl.when(q == k)
+    for part in range(HEAD_PARTS):
+        def quarter_step(q, carry):
+            def one(at, inner_carry):
+                block(at, part)
+                return inner_carry
+
+            lax.fori_loop(q * subs, (q + 1) * subs, one, 0)
+
+            @pl.when(q != me)
             def _():
-                for action in plan[k]:
-                    action()
-        return carry
-
-    lax.fori_loop(0, groups, quarter_step, 0)
+                leave(q, part).start()
+
+            if part == HEAD_PARTS - 1:
+                for item in stores(q):
+                    item.start()
+            for k in range(groups):
+                @pl.when(q == k)
+                def _():
+                    for action in plan[part * groups + k]:
+                        action()
+            return carry
+
+        lax.fori_loop(0, groups, quarter_step, 0)
     stay = pltpu.make_async_copy(gated_s.at[me], gated_out.at[me], local_sem.at[2])
     stay.start()
     drain(streams)
@@ -474,8 +512,9 @@
     def finish(q, carry):
         @pl.when(q != me)
         def _():
-            leave(q).wait_send()
-            arrive(q).wait_recv()
+            for part in range(HEAD_PARTS):
+                leave(q, part).wait_send()
+                arrive(q, part).wait_recv()
 
         for item in stores(q):
             item.wait()
@@ -499,11 +538,11 @@
     outs = [
         jax.ShapeDtypeStruct((length, model), BF16), wide, wide, wide, wide, wide,
         jax.ShapeDtypeStruct((length, 2 * n), BF16),
-        jax.ShapeDtypeStruct((length, dtw.shape[1]), F32),
+        jax.ShapeDtypeStruct((length, 128), F32),
         jax.ShapeDtypeStruct((length // SPAN, n, channels), BF16),
         jax.ShapeDtypeStruct((groups, rows_num, channels), BF16),
         jax.ShapeDtypeStruct((groups,) + (2,) * count + (part, model), BF16),
-        jax.ShapeDtypeStruct((groups, 8, channels), F32),
+        jax.ShapeDtypeStruct((groups, 1, channels), F32),
     ]
     dma = pltpu.SemaphoreType.DMA
     result = pl.pallas_call(
@@ -521,10 +560,13 @@
             pltpu.VMEM((length, channels), BF16), pltpu.VMEM((length, channels), BF16),
             pltpu.VMEM((length, channels), BF16), pltpu.VMEM((length + 8, channels), F32),
             pltpu.VMEM((length, 2 * n), F32), pltpu.VMEM((length, 2 * n), BF16),
-            pltpu.VMEM((length, dtw.shape[1]), F32), pltpu.VMEM((length // SPAN, n, channels), BF16),
+            pltpu.VMEM((length, 128), F32), pltpu.VMEM((length // SPAN, n, channels), BF16),
             pltpu.VMEM((groups, rows_num, channels), BF16),
-            pltpu.VMEM((n, channels), F32), pltpu.VMEM((SPAN, channels), BF16),
-            dma((5,)), dma((3,)), dma((9, groups)), dma((groups,)), dma((groups,)), dma((copies,)), dma((copies,)),
+            pltpu.VMEM((n, channels), F32), pltpu.VMEM((SPAN, channels // HEAD_PARTS), BF16),
+            pltpu.VMEM((length // SPAN, SPAN, 128), F32), pltpu.VMEM((length // SPAN, 128, SPAN), F32),
+            pltpu.VMEM((length // SPAN, SPAN, SPAN), F32), pltpu.VMEM((length // SPAN, n, SPAN), BF16),
+            pltpu.VMEM((8, 128), F32),
+            dma((5,)), dma((3,)), dma((9, groups)), dma((HEAD_PARTS, groups)), dma((HEAD_PARTS, groups)), dma((copies,)), dma((copies,)),
             dma((piece_copies,)), dma((piece_copies,)),
         ],
         compiler_params=pltpu.CompilerParams(
@@ -536,7 +578,7 @@
         name="front",
     )(
         tokens, pre_gain[None], zw, xw, bcw, dtw, out_weight.reshape((2,) * count + (part, model)),
-        jnp.broadcast_to(norm_gain[None], (8, channels)), convw, convb, dtb, alog, skip,
+        norm_gain[None], convw, convb, dtb, alog, skip,
     )
     x, a, s, act, dsc, inn, bc, step, prev, gated, w_all, gains = result
     return x, (a, s, act, dsc, inn), bc, step, prev, gated, w_all.reshape(groups, channels, model), gains
@@ -544,8 +586,8 @@
 
 def middle_kernel(
     count, g_hbm, w_hbm, cot_hbm, gain_ref, tok_ref,
-    out_hbm, dg_out, part_ref, ggrad_ref,
-    g_s, w_s, cot_s, gg_s, out_s, dg_s, give_s, kept_s, *refs,
+    out_hbm, dg_out, own_ref, part_ref, ggrad_ref,
+    g_s, w_s, cot_s, dy_s, gg_s, out_s, dg_s, give_s, kept_s, obuf, oslot0, oslot1, *refs,
 ):
     slots = [refs[i * (count - 1) : (i + 1) * (count - 1)] for i in range(4)]
     load_sem, store_sem, away_sem, here_sem, send, recv = refs[4 * (count - 1) :]
@@ -565,10 +607,9 @@
     loads = [
         pltpu.make_async_copy(g_hbm, g_s, load_sem.at[0]), pltpu.make_async_copy(cot_hbm, cot_s, load_sem.at[1]),
     ]
-    loads[0].start()
-    w_load(0).start()
-    loads[1].start()
-    for t in range(1, tiles):
+    for load in loads:
+        load.start()
+    for t in range(tiles):
         w_load(t).start()
     loads[0].wait()
     sums = [jnp.zeros((rows_num, 1), F32) for _ in segs]
@@ -606,19 +647,17 @@
             out_s[w, :, cols] = (tok + recips[w] * acc).astype(BF16)
             new.append(dots[w] + jnp.sum(cot_s[w, :, cols].astype(F32) * acc, axis=1, keepdims=True))
         out_store(t).start()
+        return tuple(new)
+
+    def combine(t, carry):
+        cols = pl.ds(pl.multiple_of(t * tile, tile), tile)
         combined = jnp.zeros((rows_num, tile), F32)
         for w in reversed(range(4)):
             combined += recips[w] * cot_s[w, :, cols].astype(F32)
-            cot_s[w, :, cols] = combined.astype(BF16)
-        return tuple(new)
-
-    dots = lax.fori_loop(0, tiles, forward, tuple(jnp.zeros((rows_num, 1), F32) for _ in segs))
-    dy_s = cot_s
-    scales = [None] * 4
-    scale = jnp.zeros((rows_num, 1), F32)
-    for w in reversed(range(4)):
-        scale = scale + recips[w] ** 3 * dots[w] / (segs[w][1] * groups)
-        scales[w] = scale
+            dy_s[w, :, cols] = combined.astype(BF16)
+        return carry
+
+    lax.fori_loop(0, tiles, combine, 0)
 
     def leave(j):
         return pltpu.make_async_remote_copy(
@@ -654,7 +693,7 @@
         return tuple((p >> b) & 1 for b in reversed(range(1, count)))
 
     def terms(s, bit, use):
-        g0, c0 = (s // 2) * pairs_num, (s % 2) * half
+        g0, c0 = (s % 2) * pairs_num, (s // 2) * half
         if part % 128 == 0:
             for q in range(2 ** (count - 1)):
                 at = pl.ds(pl.multiple_of((2 * q + bit) * part, part), part)
@@ -700,11 +739,20 @@
         Stream(halving(ports, "batch", lambda s=s: kept_s.at[s], slots[s], up if s % 2 == 0 else up[::-1]))
         for s in range(4)
     ]
+    mine = bits_of("batch", count)
+    own = place(up, {b: mine[b] for b in up})
+    head_sum = Stream(halving(ports, "head", lambda: obuf, (oslot0, oslot1), [0, 1]))
     for s in range(2):
         give(s)
     for s in range(2):
         keep(s)
         streams[s].advance()
+    dots = lax.fori_loop(0, tiles, forward, tuple(jnp.zeros((rows_num, 1), F32) for _ in segs))
+    scales = [None] * 4
+    scale = jnp.zeros((rows_num, 1), F32)
+    for w in reversed(range(4)):
+        scale = scale + recips[w] ** 3 * dots[w] / (segs[w][1] * groups)
+        scales[w] = scale
     lax.fori_loop(0, groups, back, 0)
     stay = pltpu.make_async_copy(dg_s.at[me], dg_out.at[me], load_sem.at[0])
     stay.start()
@@ -714,12 +762,19 @@
     for s in range(2, 4):
         keep(s)
         streams[s].advance()
+    drain(streams[:2])
+    for s in range(2):
+        for j in range(pairs_num):
+            obuf[s, j] = kept_s[(s,) + own + (j,)]
+    head_sum.advance()
+    advance_all(streams[2:])
+    head_sum.advance()
     drain(streams)
-    mine = bits_of("batch", count)
-    own = place(up, {b: mine[b] for b in up})
-    for s in range(4):
+    drain([head_sum])
+    own_ref[...] = obuf[place(2, dict(enumerate(bits_of("head", 2))))]
+    for s in range(2, 4):
         for j in range(pairs_num):
-            part_ref[(s // 2) * pairs_num + j, :, (s % 2) * half : (s % 2 + 1) * half] = kept_s[(s,) + own + (j,)]
+            part_ref[s - 2, j] = kept_s[(s,) + own + (j,)]
     stay.wait()
 
     def finish(j, carry):
@@ -755,23 +810,25 @@
     return pl.pallas_call(
         functools.partial(middle_kernel, count),
         in_specs=[hbm] * 3 + [vmem] * 2,
-        out_specs=[hbm, hbm, vmem, vmem],
+        out_specs=[hbm, hbm, vmem, vmem, vmem],
         out_shape=[
             jax.ShapeDtypeStruct((4, rows_num, model), BF16),
             jax.ShapeDtypeStruct(g.shape, BF16),
-            jax.ShapeDtypeStruct((groups, part, model), BF16),
+            jax.ShapeDtypeStruct((part, half), BF16),
+            jax.ShapeDtypeStruct((2, 2, part, half), BF16),
             jax.ShapeDtypeStruct((groups, 1, channels), F32),
         ],
         scratch_shapes=[
-            wide, pltpu.VMEM((groups, channels, model), BF16), tall, wide, tall, wide, halves, halves,
+            wide, pltpu.VMEM((groups, channels, model), BF16), tall, tall, wide, tall, wide, halves, halves,
+            pltpu.VMEM((2, 2, part, half), BF16), pltpu.VMEM((2, part, half), BF16), pltpu.VMEM((part, half), BF16),
         ]
         + [s for _ in range(4) for s in halving_slots(count - 1, block, BF16)]
         + [
             dma((2 + model // 512,)), dma((model // 512,)), dma((groups,)), dma((groups,)),
-            dma((4 * count,)), dma((4 * count,)),
+            dma((4 * count + 2,)), dma((4 * count + 2,)),
         ],
         compiler_params=pltpu.CompilerParams(
-            collective_id=2, has_side_effects=True, vmem_limit_bytes=VMEM_BYTES
+            collective_id=2, has_side_effects=True, vmem_limit_bytes=BACK_VMEM_BYTES
         ),
         cost_estimate=pl.CostEstimate(
             flops=6 * groups * rows_num * channels * model, bytes_accessed=200 * 2**20, transcendentals=0
@@ -780,23 +837,38 @@
     )(g, w_all, cot, gain, tok)
 
 
+BACK_POLLS = {
+    "z": ((0, 0, "a"), (0, 1, "a"), (0, 1, "b"), (0, 2, "a"), (0, 3, "a"), (0, 3, "b")),
+    "out": ((0, 0, "a"), (0, 1, "a")),
+    "spread": (((0, 0, "a"), (0, 1, "a"), (0, 1, "b")), ((0, 1, "b"), (0, 2, "a"), (0, 2, "b"), (0, 3, "a"))),
+    "relay": (
+        ((0, 1, "a"), 3, 0, 1), ((0, 1, "b"), 3, 1, 1), ((0, 2, "a"), 3, 2, 1), ((0, 2, "a"), 3, 3, 1),
+        ((0, 1, "b"), 3, 0, 2), ((0, 2, "a"), 3, 1, 2), ((0, 2, "b"), 3, 2, 2), ((0, 3, "a"), 3, 3, 2),
+        ((0, 2, "b"), 2, 0, 1), ((0, 3, "a"), 2, 1, 1), ((0, 3, "b"), 2, 2, 1),
+    ),
+    "tail": (1, 1, 2, 2),
+}
+RELAY_ORDER = [(2, c, 1) for c in range(4)] + [(1, c, 1) for c in range(4)]
+RELAY_ORDER += [(0, 0, 1), (0, 1, 1), (0, 0, 2), (0, 2, 1), (0, 1, 2), (0, 3, 1), (0, 2, 2), (0, 3, 2)]
+
+
 def back_kernel(
     count, group_bits,
     dg_hbm, a_hbm, s_hbm, act_hbm, dsc_hbm, inn_hbm, x_hbm, bc_hbm, step_hbm, prev_hbm,
-    zw_hbm, xw_hbm, bcw_hbm, dtw_hbm, o_hbm, gain_ref, convw_ref, dtb_ref, alog_ref, skip_ref, hot_ref,
+    zw_hbm, xw_hbm, bcw_hbm, dtw_hbm, o_hbm, own_hbm, gain_ref, convw_ref, alog_ref, skip_ref,
     z_out, x_out, o_out, bc_out, small_out, own_out,
-    dg, a, s, act, dsc, inn, x, bc, step, prev, zw, xw, bdw, obuf,
+    dg, a, s, act, dsc, inn, x, bc, step, prev, zw, xw, bdw, dtw, obuf, o_first, hot_ref, pad_s,
     lam, dconv, dyc_s, vt_s, q_s, v_s, w_s, da_s, etot_s, draw_s, head_s, vec_s, pre_s, dbs,
-    rows_s, far_s, zg, bcbuf, small, *refs,
+    rows_s, line_s, last_s, zg, bcbuf, small, *refs,
 ):
-    zx_slots = [refs[i * count : (i + 1) * count] for i in range(4)]
-    refs = refs[4 * count :]
+    zx_slots = [refs[i * count : (i + 1) * count] for i in range(2)]
+    refs = refs[2 * count :]
     bc_slots, refs = (refs[:count], refs[count : 2 * count]), refs[2 * count :]
     bc_head, refs = (refs[:group_bits], refs[group_bits : 2 * group_bits]), refs[2 * group_bits :]
     small_slots, refs = refs[:count], refs[count:]
     small_head, refs = refs[:group_bits], refs[group_bits:]
     o_slots, refs = refs[:group_bits], refs[group_bits:]
-    load_sem, store_sem, rsend, rrecv, send, recv = refs
+    load_sem, store_sem, rsend, rrecv, rrecv_own, send, recv = refs
     length, channels = a.shape
     model = x.shape[1]
     n = lam.shape[0]
@@ -806,25 +878,28 @@
     subs = rows_num // SPAN
     wide = bcbuf.shape[-1]
     me = lax.axis_index("head")
-    my_hi, my_lo = me // 2, me % 2
 
     pairs = [
-        (dg_hbm, dg), (a_hbm, a), (s_hbm, s), (x_hbm, x), (o_hbm, obuf), (step_hbm, step), (bc_hbm, bc),
+        (dg_hbm.at[:, :, pl.ds(0, channels // 2)], dg.at[0]),
+        (dg_hbm.at[:, :, pl.ds(channels // 2, channels // 2)], dg.at[1]), (a_hbm, a), (s_hbm, s), (x_hbm, x), (o_hbm, obuf), (own_hbm, o_first), (step_hbm, step), (bc_hbm, bc),
         (prev_hbm, prev), (act_hbm, act), (dsc_hbm, dsc), (inn_hbm, inn), (zw_hbm, zw), (xw_hbm, xw),
-        (bcw_hbm, bdw.at[:, pl.ds(0, 2 * n)]), (dtw_hbm, bdw.at[:, pl.ds(2 * n, 128)]),
+        (bcw_hbm, bdw.at[:, pl.ds(0, 2 * n)]), (dtw_hbm, dtw),
     ]
     loads = [pltpu.make_async_copy(src, dst, load_sem.at[i]) for i, (src, dst) in enumerate(pairs)]
     for load in loads:
         load.start()
-    for load in loads[:3]:
+    for load in loads[:4]:
         load.wait()
 
     def gates(i, carry):
         per = rows_num // 64
         rows = pl.ds(pl.multiple_of(i * 64, 64), 64)
-        d = dg[i // per, pl.ds(pl.multiple_of((i % per) * 64, 64), 64), :].astype(F32)
-        a[rows, :] = (d * a[rows, :].astype(F32)).astype(BF16)
-        s[rows, :] = (d * s[rows, :].astype(F32)).astype(BF16)
+        piece = dg.shape[-1]
+        for h in range(dg.shape[0]):
+            cols = slice(h * piece, (h + 1) * piece)
+            d = dg[h, i // per, pl.ds(pl.multiple_of((i % per) * 64, 64), 64), :].astype(F32)
+            a[rows, cols] = (d * a[rows, cols].astype(F32)).astype(BF16)
+            s[rows, cols] = (d * s[rows, cols].astype(F32)).astype(BF16)
         return carry
 
     lax.fori_loop(0, length // 64, gates, 0)
@@ -836,31 +911,30 @@
     ports = Ports(send, recv)
     up = list(range(1, count))
     orders = [up, up[::-1]]
-    cols_num = channels // 2
 
     def own_at():
         return place(count, dict(enumerate(bits_of("batch", count))))
 
-    def keep(src, dst, sem):
-        def step():
-            copy = pltpu.make_async_copy(src(), dst(), store_sem.at[sem])
-            copy.start()
-            copy.wait()
-
-        return [step]
-
-    def grads(i):
-        part = (slice(None),) * (count + 1) + (pl.ds((i % 2) * cols_num, cols_num),)
-        view = lambda: (z_out, x_out)[i // 2].at[part]
-        buf = lambda: (zg, zw)[i // 2].at[part]
+    def grads(i, out, slots, first, width):
+        part = (slice(None),) * (count + 1) + (pl.ds(first, width),)
+        view = lambda: out.at[part]
+        buf = lambda: zg.at[part]
         order = orders[i % 2]
         return Stream(
-            halving(ports, "batch", buf, zx_slots[i], [0] + order),
-            keep(lambda: buf().at[own_at()], lambda: view().at[own_at()], i),
-            spreading(ports, "batch", view, order[::-1] + [0]),
+            halving(ports, "batch", buf, slots, [0] + order),
+            spreading(
+                ports, "batch", view, order[::-1] + [0], lambda: buf().at[own_at()], store_sem.at[2 + i]
+            ),
         )
 
-    streams = [grads(i) for i in range(4)]
+    z_width, x_width = channels // 2, channels // X_STREAMS
+    streams = [grads(i, z_out, zx_slots[i], i * z_width, z_width) for i in range(2)]
+    per = z_width // x_width
+    for i in range(X_STREAMS):
+        cols = pl.ds((i % per) * x_width, x_width)
+        slots = [ref.at[(slice(None),) * (len(ref.shape) - 1) + (cols,)] for ref in zx_slots[i // per]]
+        streams.append(grads(2 + i, x_out, slots, i * x_width, x_width))
+
     def state_part(i):
         part = (slice(None),) * (count + 1) + ((pl.ds(n, n + 128), pl.ds(0, n))[i],)
         buf = lambda: bcbuf.at[part]
@@ -871,8 +945,9 @@
                 ports, "head", lambda: bcbuf.at[own_at() + (slice(None), pl.ds((n, 0)[i], n))], bc_head[i],
                 range(group_bits),
             ),
-            keep(lambda: buf().at[own_at()], lambda: view().at[own_at()], (4, 6)[i]),
-            spreading(ports, "batch", view, orders[i][::-1] + [0]),
+            spreading(
+                ports, "batch", view, orders[i][::-1] + [0], lambda: buf().at[own_at()], store_sem.at[i]
+            ),
         )
 
     state = [state_part(i) for i in range(2)]
@@ -888,15 +963,23 @@
     def o_view(i):
         return o_out.at[(slice(None),) * (count + 1) + (pl.ds(i * half, half),)]
 
-    outs = Stream(
-        halving(ports, "head", lambda: obuf, o_slots, list(range(group_bits))),
-        keep(lambda: obuf.at[head_own()], lambda: o_out.at[own_at()], 5),
-    )
-    spread = [Stream(spreading(ports, "batch", lambda i=i: o_view(i), orders[i] + [0])) for i in range(2)]
-
-    for load in loads[3:5]:
+    outs = Stream(halving(ports, "head", lambda: obuf, o_slots, list(range(group_bits))))
+
+    def o_own(i):
+        return obuf.at[head_own()] if i else o_first
+
+    spread = [
+        Stream(spreading(
+            ports, "batch", lambda i=i: o_view(i), orders[i] + [0], lambda i=i: o_own(i),
+            store_sem.at[2 + 2 + X_STREAMS + i],
+        ))
+        for i in range(2)
+    ]
+
+    for load in loads[4:7]:
         load.wait()
     outs.advance()
+    spread[0].advance()
     tile = 256
     block_rows = model >> count
 
@@ -910,17 +993,6 @@
                 first = pl.multiple_of((t * tile) % block_rows, tile)
                 target[index + (pl.ds(first, tile), slice(None))] = value.astype(BF16)
 
-    def take(source, t):
-        if block_rows >= tile:
-            p = (t * tile) // block_rows
-            index = tuple((p // 2**b) % 2 for b in reversed(range(count)))
-            return source[index + (pl.ds(pl.multiple_of((t * tile) % block_rows, tile), tile), slice(None))]
-        found = []
-        for k in range(tile // block_rows):
-            p = (t * tile) // block_rows + k
-            found.append(source[tuple((p // 2**b) % 2 for b in reversed(range(count)))])
-        return jnp.concatenate(found, axis=0)
-
     def weight_grad(right, target):
         def one(t, carry):
             put(target, t, mm_tn(x[:, pl.ds(pl.multiple_of(t * tile, tile), tile)], right[...]))
@@ -930,8 +1002,15 @@
 
     weight_grad(a, zg)
     advance_all(streams[:2])
-    for load in loads[5:]:
+    for load in loads[7:]:
         load.wait()
+    bdw[:, 2 * n :] = jnp.concatenate([dtw[...], jnp.zeros((128 - heads, model), BF16)], axis=0).T
+    pad_s[...] = jnp.zeros_like(pad_s)
+    pad_s[0:1, 0:heads] = alog_ref[...]
+    hot_ref[...] = (
+        lax.broadcasted_iota(jnp.int32, hot_ref.shape, 1) // (channels // heads)
+        == lax.broadcasted_iota(jnp.int32, hot_ref.shape, 0)
+    ).astype(F32).astype(BF16)
 
     lam[...] = jnp.zeros_like(lam)
     dconv[rows_num:, :] = jnp.zeros((8, channels), F32)
@@ -939,7 +1018,7 @@
     head_s[...] = jnp.zeros_like(head_s)
     draw_s[...] = jnp.zeros_like(draw_s)
     pre_s[...] = jnp.zeros_like(pre_s)
-    rate = -jnp.exp(alog_ref[...])
+    rate = -jnp.exp(pad_s[0:1, :])
     lower = lower_mask((SPAN, SPAN))
     lower_f = lower.astype(F32)
     lower_b = lower.astype(BF16)
@@ -950,26 +1029,32 @@
     strict_f = strict.astype(F32)
     left = lax.broadcasted_iota(jnp.int32, (SPAN, 128), 1) < 64
 
-    def block(at, local):
+    span_num = channels // BACK_PARTS
+    span_heads = heads // BACK_PARTS
+
+    def block(at, local, part):
         rows = pl.ds(pl.multiple_of(at * SPAN, SPAN), SPAN)
         local_rows = pl.ds(pl.multiple_of(local * SPAN, SPAN), SPAN)
-        raw = step[rows, :] + dtb_ref[...]
-        delta = softplus(raw)
+        delta = step[rows, :]
         cum = mm_exact(lower_f, delta * rate)
         cum_t = cum.T
         delta_t = delta.T
-        slope_t = sigmoid(raw).T
+        series = delta_t * (1.0 - delta_t * (0.5 - delta_t * (1.0 / 6.0 - delta_t / 24.0)))
+        slope_t = jnp.where(delta_t < 0.04, series, 1.0 - jnp.exp(-delta_t))
         rate_t = jnp.broadcast_to(rate, (SPAN, 128)).T
         b_val = bc[rows, :n]
         c_val = bc[rows, n:]
         inner = jnp.where(upper, mm_nt(b_val, c_val), 0.0)
-        before = prev[at]
-        lam_b = lam[...].astype(BF16)
+        span_cols = pl.ds(part * span_num, span_num)
+        before = prev[at, :, span_cols]
+        lam_b = lam[:, span_cols].astype(BF16)
         across = mm(c_val, before)
         dtail = mm(b_val, lam_b)
         d_inner_prod = jnp.zeros((SPAN, SPAN), F32)
-        for pair in range(channels // 128):
+        for pair in range(part * span_num // 128, (part + 1) * span_num // 128):
             cols = slice(pair * 128, pair * 128 + 128)
+            own = pair - part * span_num // 128
+            here = slice(own * 128, own * 128 + 128)
             c0, c1, ce = pair_columns(cum, pair, left)
             _, _, de = pair_columns(delta, pair, left)
             tot = ce[SPAN - 1 : SPAN, :]
@@ -993,26 +1078,27 @@
             d_inner_prod += dp0 * m0 + dp1 * m1
             e01 = jnp.concatenate([(dp0 * p0).astype(BF16), (dp1 * p1).astype(BF16)], axis=0)
             spans = mm(e01, lower_b)
-            da_s[2 * pair : 2 * pair + 1, :] = jnp.sum(
+            da_s[2 * own : 2 * own + 1, :] = jnp.sum(
                 jnp.where(strict, spans[:SPAN], 0.0), axis=0, keepdims=True
             )
-            da_s[2 * pair + 1 : 2 * pair + 2, :] = jnp.sum(
+            da_s[2 * own + 1 : 2 * own + 2, :] = jnp.sum(
                 jnp.where(strict, spans[SPAN:], 0.0), axis=0, keepdims=True
             )
-            dut = dtail[:, cols] * e_tail
+            dut = dtail[:, here] * e_tail
             du = du + dut
             dye = dy * e_cum
-            dyc_s[:, cols] = dye.astype(BF16)
-            vt_s[:, cols] = (u * e_tail).astype(BF16)
-            q_s[:, cols] = (dye * across[:, cols]).astype(BF16)
-            v_s[:, cols] = (u * dut).astype(BF16)
-            w_s[:, cols] = (act_p * du).astype(BF16)
-            etot_s[:, cols] = jnp.exp(tot)
+            dyc_s[:, here] = dye.astype(BF16)
+            vt_s[:, here] = (u * e_tail).astype(BF16)
+            q_s[:, here] = (dye * across[:, here]).astype(BF16)
+            v_s[:, here] = (u * dut).astype(BF16)
+            w_s[:, here] = (act_p * du).astype(BF16)
+            etot_s[:, here] = jnp.exp(tot)
             d_act = de * du + skip_ref[:, cols] * dy
             dconv[local_rows, cols] = d_act * dsc[rows, cols].astype(F32)
-        hot = hot_ref[...]
-        over = jnp.sum(lam[...] * before.astype(F32), axis=0, keepdims=True) * etot_s[...]
-        over = jnp.broadcast_to(over, (128, channels))
+        hot = hot_ref[:span_heads, :span_num]
+        these = slice(part * span_heads, (part + 1) * span_heads)
+        over = jnp.sum(lam[:, span_cols] * before.astype(F32), axis=0, keepdims=True) * etot_s[...]
+        over = jnp.broadcast_to(over, (128, span_num))
         over = lax.dot_general(
             hot.astype(F32), over, (((1,), (1,)), ((), ())), preferred_element_type=F32, precision=HIGHEST
         )
@@ -1022,55 +1108,80 @@
             + mm_exact(mm_nt(hot, v_s[...]), strict_f)
             + over
         )
-        d_step = mm_nt(hot, w_s[...]) + rate_t[:heads] * da
-        d_raw = d_step * slope_t[:heads]
-        head_s[0:heads, :] += d_raw
-        head_s[heads : 2 * heads, :] += delta_t[:heads] * da * rate_t[:heads]
-        draw_s[0:heads, :] = d_raw
+        d_step = mm_nt(hot, w_s[...]) + rate_t[these] * da
+        d_raw = d_step * slope_t[these]
+        head_s[these, :] += d_raw
+        head_s[heads + part * span_heads : heads + (part + 1) * span_heads, :] += delta_t[these] * da * rate_t[these]
+        draw_s[these, :] = d_raw
         dg_b = jnp.where(upper, d_inner_prod, 0.0)
-        dbs[rows, :n] = (mm(dg_b.astype(BF16), c_val) + mm_nt(vt_s[...], lam_b)).astype(BF16)
-        dbs[rows, n : 2 * n] = (mm(dg_b.T.astype(BF16), b_val) + mm_nt(dyc_s[...], before)).astype(BF16)
-        dbs[rows, 2 * n :] = draw_s[...].T.astype(BF16)
-        lam[...] = lam[...] * etot_s[...] + mm(bc[rows, n:].astype(F32).T.astype(BF16), dyc_s[...])
-
-    def near_copy(hi, h):
-        at = 2 * hi + h
+        d_b = mm(dg_b.astype(BF16), c_val) + mm_nt(vt_s[...], lam_b)
+        d_c = mm(dg_b.T.astype(BF16), b_val) + mm_nt(dyc_s[...], before)
+        d_t = draw_s[...].T
+        if part:
+            d_b += dbs[rows, :n].astype(F32)
+            d_c += dbs[rows, n : 2 * n].astype(F32)
+            d_t += dbs[rows, 2 * n :].astype(F32)
+        dbs[rows, :n] = d_b.astype(BF16)
+        dbs[rows, n : 2 * n] = d_c.astype(BF16)
+        dbs[rows, 2 * n :] = d_t.astype(BF16)
+        lam[:, span_cols] = lam[:, span_cols] * etot_s[...] + mm(bc[rows, n:].astype(F32).T.astype(BF16), dyc_s[...])
+
+    top = groups - 1
+
+    def slot(q, c):
+        return dg.at[q, c] if q < 2 else line_s.at[q - 2, c]
+
+    def hop(q, c, dst, sem, to):
         return pltpu.make_async_remote_copy(
-            src_ref=rows_s.at[hi, 1 - my_lo, h], dst_ref=dg.at[at], send_sem=rsend.at[at], recv_sem=rrecv.at[at],
-            device_id={"head": partner("head", 0)}, device_id_type=pl.DeviceIdType.MESH,
+            src_ref=rows_s.at[q // 2, q % 2, c], dst_ref=dst, send_sem=rsend.at[q, c], recv_sem=sem,
+            device_id={"head": to}, device_id_type=pl.DeviceIdType.MESH,
         )
 
-    def far_copy(h):
-        return pltpu.make_async_remote_copy(
-            src_ref=rows_s.at[1 - my_hi, my_lo, h], dst_ref=far_s.at[h], send_sem=rsend.at[4 + h],
-            recv_sem=rrecv.at[4 + h],
-            device_id={"head": partner("head", 1)}, device_id_type=pl.DeviceIdType.MESH,
-        )
-
-    def join_near(hi, h):
-        near_copy(hi, h).wait()
-        add_block(rows_s, (hi, my_lo, h), dg.at[2 * hi + h], ())
-
-        @pl.when(my_hi != hi)
+    def send_up(q, c):
+        @pl.when(me + 1 < q)
         def _():
-            far_copy(h).start()
-
-    def quarter_step(i, carry):
-        q = groups - 1 - i
-        rows = pl.ds(pl.multiple_of(q * rows_num, rows_num), rows_num)
-
-        def one(j, inner_carry):
-            block(q * subs + subs - 1 - j, subs - 1 - j)
-            return inner_carry
-
-        lax.fori_loop(0, subs, one, 0)
-        for k in range(groups):
-            @pl.when(i == k)
+            hop(q, c, slot(q, c), rrecv.at[q, c], me + 1).start()
+
+        @pl.when(me + 1 == q)
+        def _():
+            hop(q, c, last_s.at[c], rrecv_own.at[c], me + 1).start()
+
+    def send_down(q, c):
+        hop(q, c, slot(q, c), rrecv.at[q, c], me - 1).start()
+
+    def arrived(q, c):
+        hop(q, c, slot(q, c), rrecv.at[q, c], me).wait_recv()
+
+    def arrived_last(q, c):
+        hop(q, c, last_s.at[c], rrecv_own.at[c], me).wait_recv()
+
+    def begin(q):
+        for c in range(ROW_CHUNKS):
+            if q > 0:
+                @pl.when(me == 0)
+                def _():
+                    send_up(q, c)
+            if q < top:
+                @pl.when(me == top)
+                def _():
+                    send_down(q, c)
+
+    def relay(q, c, distance):
+        if distance < q:
+            @pl.when(me == distance)
             def _():
-                for action in plan[k, "a"]:
-                    action()
-
-        for c in range(0, channels, 128):
+                arrived(q, c)
+                add_block(rows_s, (q // 2, q % 2, c), slot(q, c), ())
+                send_up(q, c)
+        if top - distance > q:
+            @pl.when(me == top - distance)
+            def _():
+                arrived(q, c)
+                add_block(rows_s, (q // 2, q % 2, c), slot(q, c), ())
+                send_down(q, c)
+
+    def conv_back(rows, part):
+        for c in range(part * span_num, (part + 1) * span_num, 128):
             cols = slice(c, c + 128)
             inner_v = inn[rows, cols].astype(F32)
             d_in = jnp.zeros((rows_num, 128), F32)
@@ -1080,32 +1191,22 @@
                 vec_s[k : k + 1, cols] += jnp.sum(inner_v * shifted, axis=0, keepdims=True)
             vec_s[4:5, cols] += jnp.sum(dconv[0:rows_num, cols], axis=0, keepdims=True)
             inn[rows, cols] = d_in.astype(BF16)
-        dconv[rows_num:, :] = dconv[0:8, :]
-
-        def columns(t, inner_carry):
+        kept = pl.ds(part * span_num, span_num)
+        dconv[rows_num:, kept] = dconv[0:8, kept]
+
+    def row_grads(q, rows):
+        per = model // ROW_CHUNKS // tile
+
+        def columns(t, carry):
             cols = pl.ds(pl.multiple_of(t * tile, tile), tile)
-            value = mm_nt(a[rows, :], take(zw, t)) + mm_nt(inn[rows, :], xw[cols, :]) + mm_nt(dbs[rows, :], bdw[cols, :])
+            value = mm_nt(a[rows, :], zw[cols, :]) + mm_nt(inn[rows, :], xw[cols, :]) + mm_nt(dbs[rows, :], bdw[cols, :])
             pre_s[:, cols] += jnp.sum(value * x[rows, cols].astype(F32), axis=0, keepdims=True)
-            per = model // 2 // tile
             rows_s[q // 2, q % 2, t // per, :, pl.ds(pl.multiple_of((t % per) * tile, tile), tile)] = value.astype(BF16)
-            return inner_carry
+            return carry
 
         lax.fori_loop(0, model // tile, columns, 0)
 
-        @pl.when(q % 2 != my_lo)
-        def _():
-            for h in range(2):
-                near_copy(q // 2, h).start()
-
-        for k in range(groups):
-            @pl.when(i == k)
-            def _():
-                for action in plan[k, "b"]:
-                    action()
-
-        return carry
-
-    plan = {(k, half_at): [] for k in range(groups) for half_at in "ab"}
+    plan = {(part, k, spot): [] for part in range(BACK_PARTS) for k in range(groups) for spot in "ab"}
 
     def book(stream, slots):
         for slot in slots:
@@ -1113,15 +1214,59 @@
                 plan[slot].append(stream.steps.pop(0))
 
     for st in streams[:2]:
-        book(st, [(0, "a"), (1, "a"), (2, "a"), (2, "b"), (3, "b")])
-    book(outs, [(1, "a"), (2, "b")])
-    for st in spread:
-        book(st, [(2, "b"), (3, "a"), (3, "b")])
-    plan[3, "b"] += [lambda h=h: join_near(1, h) for h in range(2)]
-    lax.fori_loop(0, groups, quarter_step, 0)
-
-    weight_grad(inn, zw)
-    advance_all(streams[2:])
+        book(st, BACK_POLLS["z"])
+    book(outs, BACK_POLLS["out"])
+    for i, st in enumerate(spread):
+        book(st, BACK_POLLS["spread"][i])
+    last = BACK_PARTS - 1
+    for k in range(groups):
+        plan[last, k, "b"].insert(0, lambda q=top - k: begin(q))
+    for spot, q, c, distance in BACK_POLLS["relay"]:
+        plan[spot].append(lambda q=q, c=c, distance=distance: relay(q, c, distance))
+
+    for part in range(BACK_PARTS):
+        def quarter_step(i, carry):
+            q = groups - 1 - i
+            rows = pl.ds(pl.multiple_of(q * rows_num, rows_num), rows_num)
+
+            def one(j, inner_carry):
+                block(q * subs + subs - 1 - j, subs - 1 - j, part)
+                return inner_carry
+
+            lax.fori_loop(0, subs, one, 0)
+
+            def polls(spot):
+                for k in range(groups):
+                    if plan[part, k, spot]:
+                        @pl.when(i == k)
+                        def _():
+                            for action in plan[part, k, spot]:
+                                action()
+
+            polls("a")
+            conv_back(rows, part)
+            if part == last:
+                row_grads(q, rows)
+            polls("b")
+            return carry
+
+        lax.fori_loop(0, groups, quarter_step, 0)
+
+    drain(streams[:2])
+    tail = list(BACK_POLLS["tail"])
+    booked = {key[1:] for key in BACK_POLLS["relay"]}
+    relays = [r for r in RELAY_ORDER if r not in booked]
+
+    def relay_some(number):
+        for _ in range(number):
+            if relays:
+                relay(*relays.pop(0))
+
+    per = X_STREAMS // 2
+    for h in range(2):
+        weight_grad(inn.at[:, pl.ds(h * z_width, z_width)], zg.at[(slice(None),) * (count + 1) + (pl.ds(h * z_width, z_width),)])
+        advance_all(streams[2 + h * per : 2 + (h + 1) * per])
+        relay_some(tail.pop(0))
 
     def state_grad(t, carry):
         put(bcbuf, t, mm_tn(x[:, pl.ds(pl.multiple_of(t * tile, tile), tile)], dbs[...]))
@@ -1141,30 +1286,47 @@
     )
     small[14:15, 0:128] = totals[0:1]
     vectors.advance()
-    advance_all(streams)
-    advance_all(spread)
-    join_near(0, 0)
-    advance_all(state + [vectors])
-    join_near(0, 1)
+    while relays:
+        advance_all(streams[2 : 2 + per])
+        relay_some(tail.pop(0) if tail else 1)
+        advance_all(streams[2 + per :] + spread)
+        relay_some(tail.pop(0) if tail else 1)
+        advance_all(state + [vectors])
     drain(streams + spread + state + [vectors, outs])
-    for h in range(2):
-        far_copy(h).wait()
     small_out[...] = small[...]
 
-    def total(r, carry):
-        rs = pl.ds(pl.multiple_of(r * 32, 32), 32)
-        for h in range(2):
-            own_out[rs, h * half : (h + 1) * half] = rows_s[my_hi, my_lo, h, rs, :].astype(F32) + far_s[h, rs, :].astype(F32)
-        return carry
-
-    lax.fori_loop(0, rows_num // 32, total, 0)
-
-
-def back_call(dg, res, x, bc, step, prev, zw, xw, bcw, dtw, out_part, gain_grad, convw, dtb, alog, skip, hot, groups, batches):
+    piece = model // ROW_CHUNKS
+    for c in range(ROW_CHUNKS):
+        for q in range(groups):
+            @pl.when(me == q)
+            def _():
+                if q > 0:
+                    arrived_last(q, c)
+                if q < top:
+                    arrived(q, c)
+
+                def total(r, carry):
+                    rs = pl.ds(pl.multiple_of(r * 32, 32), 32)
+                    value = rows_s[q // 2, q % 2, c, rs, :].astype(F32)
+                    if q > 0:
+                        value += last_s[c, rs, :].astype(F32)
+                    if q < top:
+                        value += slot(q, c)[rs, :].astype(F32)
+                    own_out[rs, c * piece : (c + 1) * piece] = value
+                    return carry
+
+                lax.fori_loop(0, rows_num // 32, total, 0)
+
+            @pl.when(me != q)
+            def _():
+                hop(q, c, slot(q, c), rrecv.at[q, c], me).wait_send()
+
+
+def back_call(dg, res, x, bc, step, prev, zw, xw, bcw, dtw, out_part, out_own, gain_grad, convw, alog, skip, groups, batches):
     length, model = x.shape
     channels = xw.shape[1]
     n = bc.shape[1] // 2
-    heads = hot.shape[0]
+    heads = dtw.shape[0]
     rows_num = length // groups
     count = log2(batches)
     group_bits = log2(groups)
@@ -1172,16 +1334,15 @@
     part = channels // batches
     rows = model // batches
     wide = 2 * n + 128
-    block = (rows, channels // 2)
     hbm = pl.BlockSpec(memory_space=pl.ANY)
     vmem = pl.BlockSpec(memory_space=pltpu.VMEM)
     dma = pltpu.SemaphoreType.DMA
-    copies = 4 * 2 * count + 2 * (2 * count + group_bits) + (count + group_bits) + group_bits + 2 * count
+    copies = (2 + X_STREAMS) * 2 * count + 2 * (2 * count + group_bits) + (count + group_bits) + group_bits + 2 * count
     tall = lambda w, t: pltpu.VMEM((length, w), t)
-    span = pltpu.VMEM((SPAN, channels), BF16)
+    span = pltpu.VMEM((SPAN, channels // BACK_PARTS), BF16)
     z, xg, o, bcg, small, own = pl.pallas_call(
         functools.partial(back_kernel, count, group_bits),
-        in_specs=[hbm] * 15 + [vmem] * 6,
+        in_specs=[hbm] * 16 + [vmem] * 4,
         out_specs=[hbm] * 4 + [vmem] * 2,
         out_shape=[
             jax.ShapeDtypeStruct(lead + (rows, channels), BF16),
@@ -1191,30 +1352,36 @@
             jax.ShapeDtypeStruct((16, channels), F32),
             jax.ShapeDtypeStruct((rows_num, model), F32),
         ],
-        scratch_shapes=[pltpu.VMEM((groups, rows_num, model // 2), BF16)] + [tall(channels, BF16)] * 5
+        scratch_shapes=[pltpu.VMEM((2, groups, rows_num, channels // 2), BF16)] + [tall(channels, BF16)] * 5
         + [
             tall(model, BF16), tall(2 * n, BF16), tall(128, F32), pltpu.VMEM(prev.shape, BF16),
-            pltpu.VMEM(lead + (rows, channels), BF16), pltpu.VMEM(xw.shape, BF16), pltpu.VMEM((model, wide), BF16),
-            pltpu.VMEM((2,) * group_bits + (part, model), BF16),
+            pltpu.VMEM(zw.shape, BF16), pltpu.VMEM(xw.shape, BF16), pltpu.VMEM((model, wide), BF16),
+            pltpu.VMEM(dtw.shape, BF16),
+            pltpu.VMEM((2,) * group_bits + (part, model // 2), BF16), pltpu.VMEM((part, model // 2), BF16),
+            pltpu.VMEM((heads, channels), BF16), pltpu.VMEM((8, 128), F32),
             pltpu.VMEM((n, channels), F32), pltpu.VMEM((rows_num + 8, channels), F32),
         ]
         + [span] * 5
         + [
-            pltpu.VMEM((heads, SPAN), F32), pltpu.VMEM((1, channels), F32), pltpu.VMEM((128, SPAN), F32),
+            pltpu.VMEM((heads // BACK_PARTS, SPAN), F32), pltpu.VMEM((1, channels // BACK_PARTS), F32),
+            pltpu.VMEM((128, SPAN), F32),
             pltpu.VMEM((128, SPAN), F32), pltpu.VMEM((8, channels), F32), pltpu.VMEM((1, model), F32),
             tall(wide, BF16),
-            pltpu.VMEM((2, 2, 2, rows_num, model // 2), BF16), pltpu.VMEM((2, rows_num, model // 2), BF16),
+            pltpu.VMEM((2, 2, ROW_CHUNKS, rows_num, model // ROW_CHUNKS), BF16),
+            pltpu.VMEM((2, ROW_CHUNKS, rows_num, model // ROW_CHUNKS), BF16),
+            pltpu.VMEM((ROW_CHUNKS, rows_num, model // ROW_CHUNKS), BF16),
             pltpu.VMEM(lead + (rows, channels), BF16), pltpu.VMEM(lead + (rows, wide), BF16),
             pltpu.VMEM((16, channels), F32),
         ]
-        + [s for _ in range(4) for s in halving_slots(count, block, BF16)]
+        + [s for _ in range(2) for s in halving_slots(count, (rows, channels // 2), BF16)]
         + halving_slots(count, (rows, n + 128), BF16)
         + halving_slots(count, (rows, n), BF16)
         + [pltpu.VMEM((rows, n), BF16)] * (2 * group_bits)
         + [pltpu.VMEM((16, channels), F32)] * count
         + [pltpu.VMEM((8, channels), F32)] * group_bits
-        + halving_slots(group_bits, (part, model), BF16)
-        + [dma((15,)), dma((7,)), dma((6,)), dma((6,)), dma((copies,)), dma((copies,))],
+        + halving_slots(group_bits, (part, model // 2), BF16)
+        + [dma((17,)), dma((6 + X_STREAMS,)),
+            dma((groups, ROW_CHUNKS)), dma((groups, ROW_CHUNKS)), dma((ROW_CHUNKS,)), dma((copies,)), dma((copies,))],
         compiler_params=pltpu.CompilerParams(
             collective_id=3, has_side_effects=True, vmem_limit_bytes=BACK_VMEM_BYTES
         ),
@@ -1223,8 +1390,8 @@
         ),
         name="back",
     )(
-        dg, *res, x, bc, step, prev, zw.reshape(lead + (rows, channels)), xw, bcw, dtw, out_part.reshape((2,) * group_bits + (part, model)),
-        gain_grad, convw, dtb, alog, skip, hot,
+        dg, *res, x, bc, step, prev, zw, xw, bcw, dtw, out_part, out_own,
+        gain_grad, convw, alog, skip,
     )
     return (
         z.reshape(model, channels), xg.reshape(model, channels), o.reshape(channels, model),
@@ -1233,16 +1400,17 @@
 
 
 def finish_kernel(
-    z_ref, x_ref, o_ref, bc_ref, small_ref, own_ref, tok_ref, cot_ref, pre_ref,
-    zf_ref, xf_ref, of_ref, bcf_ref, dt_ref, grad_ref, convw_ref, convb_ref, skip_ref, gain_ref, pre_out, dtb_ref, alog_ref,
+    z_ref, x_ref, o_ref, bc_ref, small_ref, own_ref, tok_ref, cot_ref, pre_ref, out_ref,
+    zf_ref, xf_ref, of_ref, bcf_ref, dt_ref, grad_ref, outf_ref, convw_ref, convb_ref, skip_ref, gain_ref, pre_out, dtb_ref, alog_ref,
 ):
     zf_ref[...] = z_ref[...].astype(F32)
     xf_ref[...] = x_ref[...].astype(F32)
     of_ref[...] = o_ref[...].astype(F32)
     width = bcf_ref.shape[1]
-    heads = dt_ref.shape[1]
+    heads = dt_ref.shape[0]
+    outf_ref[...] = out_ref[...]
     bcf_ref[...] = bc_ref[:, :width].astype(F32)
-    dt_ref[...] = bc_ref[:, width : width + 128].astype(F32)[:, :heads]
+    dt_ref[...] = bc_ref[:, width : width + 128].astype(F32).T[:heads]
     tok = tok_ref[...].astype(F32)
     recip = lax.rsqrt(jnp.mean(tok * tok, axis=-1, keepdims=True) + EPSILON)
     scaled = pre_ref[...] * own_ref[...]
@@ -1269,17 +1437,17 @@
         alog_ref[...] = small_ref[14:15, heads : 2 * heads]
 
 
-def finish_call(z, x, o, bc, small, own, tok, cot, pre_gain, heads):
+def finish_call(z, x, o, bc, small, own, tok, cot, pre_gain, out, heads):
     model, channels = z.shape
     rows_num = tok.shape[0]
-    steps = 8
+    steps = 16
     wide = bc.shape[1]
     rows = lambda r, w: pl.BlockSpec((r // steps, w), lambda i: (i, 0))
     fixed = lambda shape: pl.BlockSpec(shape, lambda i: (0, 0))
     shapes = [
         ((model, channels), F32), ((model, channels), F32), ((channels, model), F32), ((model, wide - 128), F32),
-        ((model, heads), F32), ((rows_num, model), BF16),
     ]
+    wide4 = pl.BlockSpec((4, rows_num // steps, model), lambda i: (0, i, 0))
     flat = [(4, channels), (1, channels), (1, channels), (1, channels), (1, model), (1, heads), (1, heads)]
     return pl.pallas_call(
         finish_kernel,
@@ -1287,15 +1455,21 @@
         in_specs=[
             rows(model, channels), rows(model, channels), rows(channels, model), rows(model, wide),
             fixed(small.shape), rows(rows_num, model), rows(rows_num, model),
-            pl.BlockSpec((4, rows_num // steps, model), lambda i: (0, i, 0)), fixed((1, model)),
+            wide4, fixed((1, model)), wide4,
         ],
-        out_specs=[rows(*shape) for shape, _ in shapes] + [fixed(shape) for shape in flat],
+        out_specs=[rows(*shape) for shape, _ in shapes]
+        + [pl.BlockSpec((heads, model // steps), lambda i: (0, i)), rows(rows_num, model), wide4]
+        + [fixed(shape) for shape in flat],
         out_shape=[jax.ShapeDtypeStruct(shape, t) for shape, t in shapes]
+        + [
+            jax.ShapeDtypeStruct((heads, model), F32), jax.ShapeDtypeStruct((rows_num, model), BF16),
+            jax.ShapeDtypeStruct(out.shape, BF16),
+        ]
         + [jax.ShapeDtypeStruct(shape, F32) for shape in flat],
         compiler_params=pltpu.CompilerParams(vmem_limit_bytes=VMEM_BYTES),
         cost_estimate=pl.CostEstimate(flops=0, bytes_accessed=46 * 2**20, transcendentals=0),
         name="finish",
-    )(z, x, o, bc, small, own, tok, cot, pre_gain[None])
+    )(z, x, o, bc, small, own, tok, cot, pre_gain[None], out)
 
 
 def per_device(
@@ -1309,27 +1483,24 @@
     cot = cotangent[:, 0]
     channels = z_weight.shape[1]
     heads = dt_weight.shape[1]
-    pad = lambda v: jnp.pad(v, ((0, 0), (0, 128 - heads)))
-    dtb = pad(dt_bias[None])
-    alog = pad(a_log[None])
+    dtw = dt_weight.T
+    alog = a_log[None]
     skip_r = skip[None]
-    dtw = pad(dt_weight)
     x, res, bc, step, prev, gated, w_all, gain_all = front_call(
         tokens, pre_gain, z_weight, x_weight, bc_weight, dtw, out_weight, norm_gain,
-        conv_weight, conv_bias[None], dtb, alog, skip_r, groups, batches,
+        conv_weight, conv_bias[None], dt_bias[None], alog, skip_r, groups, batches,
     )
-    outputs, d_gated, out_part, gain_grad = middle_call(gated, w_all, gain_all, tokens, cot, batches)
-    hot = (jnp.arange(channels)[None] // (channels // heads) == jnp.arange(heads)[:, None]).astype(BF16)
+    outputs, d_gated, out_own, out_part, gain_grad = middle_call(gated, w_all, gain_all, tokens, cot, batches)
     z_grad, x_grad, out_grad, bcdt_grad, small, d_own = back_call(
-        d_gated, res, x, bc, step, prev, z_weight, x_weight, bc_weight, dtw, out_part, gain_grad,
-        conv_weight, dtb, alog, skip_r, hot, groups, batches,
+        d_gated, res, x, bc, step, prev, z_weight, x_weight, bc_weight, dtw, out_part, out_own, gain_grad,
+        conv_weight, alog, skip_r, groups, batches,
     )
-    z_grad, x_grad, out_grad, bc_grad, dt_grad, tokens_grad, convw, convb, skip_g, gain_g, pre_g, dtb_g, alog_g = finish_call(
-        z_grad, x_grad, out_grad, bcdt_grad, small, d_own, tokens, cot, pre_gain, heads
-    )
+    (
+        z_grad, x_grad, out_grad, bc_grad, dt_grad, tokens_grad, outputs, convw, convb, skip_g, gain_g, pre_g, dtb_g, alog_g,
+    ) = finish_call(z_grad, x_grad, out_grad, bcdt_grad, small, d_own, tokens, cot, pre_gain, outputs, heads)
     flat = lambda v: v.reshape(-1)
     return (
-        outputs[:, None], tokens_grad[None], z_grad, x_grad, bc_grad, dt_grad, convw, flat(convb), flat(dtb_g),
+        outputs[:, None], tokens_grad[None], z_grad, x_grad, bc_grad, dt_grad.T, convw, flat(convb), flat(dtb_g),
         flat(alog_g), flat(skip_g), flat(gain_g), flat(pre_g), out_grad,
     )
 

time: 475 us -> 458 us (0.964)
  local copies, waits for them, and re-layouts: 12.6 us -> 0 us
    pallas_call x1, Pallas kernels: 119 us -> 106 us  [middle_call(): pl.pallas_call(functools.partial(middle_kernel, count), in_specs=[hbm] *...]
    unnamed x3 -> x0, local copies, waits for them, and re-layouts: 8.08 us -> none
    pallas_call x1, Pallas kernels: 18.2 us -> 24.2 us  [finish_call(): pl.pallas_call(finish_kernel, grid=(steps,), in_specs=[rows(model, channe...]
where the time goes in v5:
time: 458 us
  Pallas kernels  457 us (100%)
    pallas_call x1, Pallas kernels, back_call(): pl.pallas_call(functools.partial(back_kernel, count, group_bits), in_spec...  166 us
    pallas_call x1, Pallas kernels, front_call(): pl.pallas_call(functools.partial(front_kernel, count), in_specs=[vmem, vm...  160 us
    pallas_call x1, Pallas kernels, middle_call(): pl.pallas_call(functools.partial(middle_kernel, count), in_specs=[hbm] *...  106 us
    pallas_call x1, Pallas kernels, finish_call(): pl.pallas_call(finish_kernel, grid=(steps,), in_specs=[rows(model, channe...  24.2 us

profile of v5, /device:TPU:0, one launch (start us, length us, event | category | flops | bytes accessed | tf_op | source)
XLA Modules:
  0.0 457.6 jit_solution(6965206264308118673)
XLA Ops:
  0.6 160.0 %front.1 = (bf16[1024,2048]{1,0:T(8,128)(2,1)}, bf16[1024,1024]{1,0:T(8,128)(2,1)}, bf16[1024,1024]{1,0:T(8,128)(2,1)}, bf16[1024,1024]{1,0:T(8,128)(2,1)}, bf16...) custom-call(bf16[256,2048]{1,0:T(8,128)(2,1)} %bitcast.32, ...), custom_call_target="tpu_custom_call" | custom-call | flops 8589934592 | bytes 419430400 | tf_op jit(solution)/shard_map/front/pallas_call | solution.py:548
  160.6 106.1 %nested_norm.1 = (bf16[4,256,2048]{2,1,0:T(8,128)(2,1)}, bf16[4,256,1024]{2,1,0:T(8,128)(2,1)}, bf16[128,1024]{1,0:T(8,128)(2,1)}, bf16[2,2,128,1024]{3,2,1,0:T(8,128)(2,1)}, f32[4,1,1024]{2,1,0:T(1,128)}) custom-call(bf16[4,256,1024]{2,1,0:T(8,128)(2,1)} %get-tuple-element.51.g_hbm, bf16[4,1024,2048]{2,1,0:T(8,128)(2,1)} %bitcast.56, ...), custom_call_target="tpu_custom_call" | custom-call | flops 12884901888 | bytes 209715200 | tf_op jit(solution)/shard_map/nested_norm/pallas_call | solution.py:810
  266.7 166.4 %back.1 = (bf16[2,2,2,256,1024]{4,3,2,1,0:T(8,128)(2,1)}, bf16[2,2,2,256,1024]{4,3,2,1,0:T(8,128)(2,1)}, bf16[2,2,2,128,2048]{4,3,2,1,0:T(8,128)(2,1)}, bf16[2,2...) custom-call(bf16[4,256,1024]{2,1,0:T(8,128)(2,1)} %get-tuple-element.54.dg_hbm, ...), custom_call_target="tpu_custom_call" | custom-call | flops 21474836480 | bytes 314572800 | tf_op jit(solution)/shard_map/back/pallas_call | solution.py:1343
  433.1 24.2 %finish.1 = (f32[2048,1024]{1,0:T(8,128)}, f32[2048,1024]{1,0:T(8,128)}, f32[1024,2048]{1,0:T(8,128)}, f32[2048,256]{1,0:T(8,128)}, f32[16,2048]{1,0:T(8,128)}, ...) custom-call(bf16[2048,1024]{1,0:T(8,128)(2,1)} %bitcast.28, ...), custom_call_target="tpu_custom_call" | custom-call | bytes 48234496 | tf_op jit(solution)/shard_map/finish/pallas_call | solution.py:1452

commit v6 on v5

--- a/solution.py
+++ b/solution.py
@@ -150,6 +150,29 @@
         advance_all(streams)
 
 
+def exchanging_once(ports, axis, bits, buf, slots):
+    def to(k):
+        return lax.axis_index(axis) + sum(
+            (1 - 2 * b) * 2**i for i, b in enumerate(bits_of(axis, bits)) if k & 2**i
+        )
+
+    copies = [
+        ports.make(buf, lambda k=k: slots[k - 1], axis, lambda k=k: to(k)) for k in range(1, 2**bits)
+    ]
+
+    def start():
+        for copy in copies:
+            copy().start()
+
+    def finish():
+        for copy in copies:
+            copy().wait()
+        ref = buf()
+        ref[...] = (ref[...].astype(F32) + sum(slot[...].astype(F32) for slot in slots)).astype(ref.dtype)
+
+    return [start, finish]
+
+
 class Ports:
     def __init__(self, send, recv):
         self.send, self.recv, self.used = send, recv, 0
@@ -246,7 +269,7 @@
 
 
 PIECE_POLLS = (
-    ("a", 0), ("a", 1), ("a", 2), ("c", 0), ("d", 1), ("e", 2), ("e", 0), (1, 1), (3, 2), (3, 0), (5, 1), (7, 2),
+    ("a", 0), ("a", 1), ("c", 2), ("c", 0), ("d", 1), ("e", 0), (1, 1), (2, 2), (3, 0), (4, 1), (5, 2), (7, 2),
 )
 
 
@@ -840,7 +863,7 @@
 BACK_POLLS = {
     "z": ((0, 0, "a"), (0, 1, "a"), (0, 1, "b"), (0, 2, "a"), (0, 3, "a"), (0, 3, "b")),
     "out": ((0, 0, "a"), (0, 1, "a")),
-    "spread": (((0, 0, "a"), (0, 1, "a"), (0, 1, "b")), ((0, 1, "b"), (0, 2, "a"), (0, 2, "b"), (0, 3, "a"))),
+    "spread": (((0, 2, "a"), (0, 2, "b"), (0, 3, "b")), ((0, 2, "a"), (0, 2, "b"), (0, 3, "b"))),
     "relay": (
         ((0, 1, "a"), 3, 0, 1), ((0, 1, "b"), 3, 1, 1), ((0, 2, "a"), 3, 2, 1), ((0, 2, "a"), 3, 3, 1),
         ((0, 1, "b"), 3, 0, 2), ((0, 2, "a"), 3, 1, 2), ((0, 2, "b"), 3, 2, 2), ((0, 3, "a"), 3, 3, 2),
@@ -861,10 +884,11 @@
     lam, dconv, dyc_s, vt_s, q_s, v_s, w_s, da_s, etot_s, draw_s, head_s, vec_s, pre_s, dbs,
     rows_s, line_s, last_s, zg, bcbuf, small, *refs,
 ):
+    groups = rows_s.shape[0] * rows_s.shape[1]
     zx_slots = [refs[i * count : (i + 1) * count] for i in range(2)]
     refs = refs[2 * count :]
     bc_slots, refs = (refs[:count], refs[count : 2 * count]), refs[2 * count :]
-    bc_head, refs = (refs[:group_bits], refs[group_bits : 2 * group_bits]), refs[2 * group_bits :]
+    bc_head, refs = (refs[: groups - 1], refs[groups - 1 : 2 * (groups - 1)]), refs[2 * (groups - 1) :]
     small_slots, refs = refs[:count], refs[count:]
     small_head, refs = refs[:group_bits], refs[group_bits:]
     o_slots, refs = refs[:group_bits], refs[group_bits:]
@@ -873,7 +897,6 @@
     model = x.shape[1]
     n = lam.shape[0]
     heads = hot_ref.shape[0]
-    groups = rows_s.shape[0] * rows_s.shape[1]
     rows_num = length // groups
     subs = rows_num // SPAN
     wide = bcbuf.shape[-1]
@@ -903,9 +926,10 @@
         return carry
 
     lax.fori_loop(0, length // 64, gates, 0)
+    near, far = partner("head", 0), partner("head", 1)
     meet(
         [("batch", partner("batch", b)) for b in range(count)]
-        + [("head", partner("head", b)) for b in range(group_bits)]
+        + [("head", to) for to in (near, far, near + far - me)]
     )
 
     ports = Ports(send, recv)
@@ -941,9 +965,8 @@
         view = lambda: bc_out.at[part]
         return Stream(
             halving(ports, "batch", buf, bc_slots[i], [0] + orders[i]),
-            exchanging(
-                ports, "head", lambda: bcbuf.at[own_at() + (slice(None), pl.ds((n, 0)[i], n))], bc_head[i],
-                range(group_bits),
+            exchanging_once(
+                ports, "head", group_bits, lambda: bcbuf.at[own_at() + (slice(None), pl.ds((n, 0)[i], n))], bc_head[i]
             ),
             spreading(
                 ports, "batch", view, orders[i][::-1] + [0], lambda: buf().at[own_at()], store_sem.at[i]
@@ -979,7 +1002,6 @@
     for load in loads[4:7]:
         load.wait()
     outs.advance()
-    spread[0].advance()
     tile = 256
     block_rows = model >> count
 
@@ -995,10 +1017,12 @@
 
     def weight_grad(right, target):
         def one(t, carry):
-            put(target, t, mm_tn(x[:, pl.ds(pl.multiple_of(t * tile, tile), tile)], right[...]))
+            value = mm_tn(x[:, pl.ds(pl.multiple_of(t * 2 * tile, 2 * tile), 2 * tile)], right[...])
+            for k in range(2):
+                put(target, 2 * t + k, value[k * tile : (k + 1) * tile])
             return carry
 
-        lax.fori_loop(0, model // tile, one, 0)
+        lax.fori_loop(0, model // (2 * tile), one, 0)
 
     weight_grad(a, zg)
     advance_all(streams[:2])
@@ -1195,16 +1219,17 @@
         dconv[rows_num:, kept] = dconv[0:8, kept]
 
     def row_grads(q, rows):
-        per = model // ROW_CHUNKS // tile
+        wide_tile = 2 * tile
+        per = model // ROW_CHUNKS // wide_tile
 
         def columns(t, carry):
-            cols = pl.ds(pl.multiple_of(t * tile, tile), tile)
+            cols = pl.ds(pl.multiple_of(t * wide_tile, wide_tile), wide_tile)
             value = mm_nt(a[rows, :], zw[cols, :]) + mm_nt(inn[rows, :], xw[cols, :]) + mm_nt(dbs[rows, :], bdw[cols, :])
             pre_s[:, cols] += jnp.sum(value * x[rows, cols].astype(F32), axis=0, keepdims=True)
-            rows_s[q // 2, q % 2, t // per, :, pl.ds(pl.multiple_of((t % per) * tile, tile), tile)] = value.astype(BF16)
+            rows_s[q // 2, q % 2, t // per, :, pl.ds(pl.multiple_of((t % per) * wide_tile, wide_tile), wide_tile)] = value.astype(BF16)
             return carry
 
-        lax.fori_loop(0, model // tile, columns, 0)
+        lax.fori_loop(0, model // wide_tile, columns, 0)
 
     plan = {(part, k, spot): [] for part in range(BACK_PARTS) for k in range(groups) for spot in "ab"}
 
@@ -1257,16 +1282,10 @@
     booked = {key[1:] for key in BACK_POLLS["relay"]}
     relays = [r for r in RELAY_ORDER if r not in booked]
 
-    def relay_some(number):
-        for _ in range(number):
+    def relay_some():
+        for _ in range(tail.pop(0) if tail else 1):
             if relays:
                 relay(*relays.pop(0))
-
-    per = X_STREAMS // 2
-    for h in range(2):
-        weight_grad(inn.at[:, pl.ds(h * z_width, z_width)], zg.at[(slice(None),) * (count + 1) + (pl.ds(h * z_width, z_width),)])
-        advance_all(streams[2 + h * per : 2 + (h + 1) * per])
-        relay_some(tail.pop(0))
 
     def state_grad(t, carry):
         put(bcbuf, t, mm_tn(x[:, pl.ds(pl.multiple_of(t * tile, tile), tile)], dbs[...]))
@@ -1274,6 +1293,14 @@
 
     lax.fori_loop(0, model // tile, state_grad, 0)
     advance_all(state)
+    per = X_STREAMS // 2
+    x_pairs = [streams[2 + h * per : 2 + (h + 1) * per] for h in range(2)]
+    for h in range(2):
+        cols = pl.ds(h * z_width, z_width)
+        weight_grad(inn.at[:, cols], zg.at[(slice(None),) * (count + 1) + (cols,)])
+        advance_all(x_pairs[h])
+        relay_some()
+        advance_all(state)
     small[...] = jnp.zeros_like(small)
     for j in range(groups):
         small[j : j + 1, :] = gain_ref[j]
@@ -1286,13 +1313,13 @@
     )
     small[14:15, 0:128] = totals[0:1]
     vectors.advance()
-    while relays:
-        advance_all(streams[2 : 2 + per])
-        relay_some(tail.pop(0) if tail else 1)
-        advance_all(streams[2 + per :] + spread)
-        relay_some(tail.pop(0) if tail else 1)
+    while relays or any(st.steps for st in streams + state + spread + [vectors, outs]):
+        advance_all(x_pairs[0])
+        relay_some()
         advance_all(state + [vectors])
-    drain(streams + spread + state + [vectors, outs])
+        advance_all(x_pairs[1])
+        relay_some()
+        advance_all(spread + [outs])
     small_out[...] = small[...]
 
     piece = model // ROW_CHUNKS
@@ -1337,7 +1364,7 @@
     hbm = pl.BlockSpec(memory_space=pl.ANY)
     vmem = pl.BlockSpec(memory_space=pltpu.VMEM)
     dma = pltpu.SemaphoreType.DMA
-    copies = (2 + X_STREAMS) * 2 * count + 2 * (2 * count + group_bits) + (count + group_bits) + group_bits + 2 * count
+    copies = (2 + X_STREAMS) * 2 * count + 2 * (2 * count + groups - 1) + (count + group_bits) + group_bits + 2 * count
     tall = lambda w, t: pltpu.VMEM((length, w), t)
     span = pltpu.VMEM((SPAN, channels // BACK_PARTS), BF16)
     z, xg, o, bcg, small, own = pl.pallas_call(
@@ -1376,7 +1403,7 @@
         + [s for _ in range(2) for s in halving_slots(count, (rows, channels // 2), BF16)]
         + halving_slots(count, (rows, n + 128), BF16)
         + halving_slots(count, (rows, n), BF16)
-        + [pltpu.VMEM((rows, n), BF16)] * (2 * group_bits)
+        + [pltpu.VMEM((rows, n), BF16)] * (2 * (groups - 1))
         + [pltpu.VMEM((16, channels), F32)] * count
         + [pltpu.VMEM((8, channels), F32)] * group_bits
         + halving_slots(group_bits, (part, model // 2), BF16)
@@ -1440,7 +1467,7 @@
 def finish_call(z, x, o, bc, small, own, tok, cot, pre_gain, out, heads):
     model, channels = z.shape
     rows_num = tok.shape[0]
-    steps = 16
+    steps = 8
     wide = bc.shape[1]
     rows = lambda r, w: pl.BlockSpec((r // steps, w), lambda i: (i, 0))
     fixed = lambda shape: pl.BlockSpec(shape, lambda i: (0, 0))

time: 458 us -> 429 us (0.937)
  Pallas kernels: 457 us -> 428 us
    pallas_call x1, Pallas kernels: 166 us -> 153 us  [back_call(): pl.pallas_call(functools.partial(back_kernel, count, group_bits), in_spec...]
    pallas_call x1, Pallas kernels: 160 us -> 151 us  [front_call(): pl.pallas_call(functools.partial(front_kernel, count), in_specs=[vmem, vm...]
where the time goes in v6:
time: 429 us; the launch traced here: 428 us
  Pallas kernels  428 us (100%)
    pallas_call x1, Pallas kernels, back_call(): pl.pallas_call(functools.partial(back_kernel, count, group_bits), in_spec...  153 us
    pallas_call x1, Pallas kernels, front_call(): pl.pallas_call(functools.partial(front_kernel, count), in_specs=[vmem, vm...  151 us
    pallas_call x1, Pallas kernels, middle_call(): pl.pallas_call(functools.partial(middle_kernel, count), in_specs=[hbm] *...  103 us
    pallas_call x1, Pallas kernels, finish_call(): pl.pallas_call(finish_kernel, grid=(steps,), in_specs=[rows(model, channe...  20.4 us

profile of v6, /device:TPU:0, one launch (start us, length us, event | category | flops | bytes accessed | tf_op | source)
XLA Modules:
  0.0 428.5 jit_solution(3283840964923437172)
XLA Ops:
  0.6 150.9 %front.1 = (bf16[1024,2048]{1,0:T(8,128)(2,1)}, bf16[1024,1024]{1,0:T(8,128)(2,1)}, bf16[1024,1024]{1,0:T(8,128)(2,1)}, bf16[1024,1024]{1,0:T(8,128)(2,1)}, bf16...) custom-call(bf16[256,2048]{1,0:T(8,128)(2,1)} %bitcast.32, ...), custom_call_target="tpu_custom_call" | custom-call | flops 8589934592 | bytes 419430400 | tf_op jit(solution)/shard_map/front/pallas_call | solution.py:571
  151.5 103.0 %nested_norm.1 = (bf16[4,256,2048]{2,1,0:T(8,128)(2,1)}, bf16[4,256,1024]{2,1,0:T(8,128)(2,1)}, bf16[128,1024]{1,0:T(8,128)(2,1)}, bf16[2,2,128,1024]{3,2,1,0:T(8,128)(2,1)}, f32[4,1,1024]{2,1,0:T(1,128)}) custom-call(bf16[4,256,1024]{2,1,0:T(8,128)(2,1)} %get-tuple-element.51.g_hbm, bf16[4,1024,2048]{2,1,0:T(8,128)(2,1)} %bitcast.56, ...), custom_call_target="tpu_custom_call" | custom-call | flops 12884901888 | bytes 209715200 | tf_op jit(solution)/shard_map/nested_norm/pallas_call | solution.py:833
  254.6 153.3 %back.1 = (bf16[2,2,2,256,1024]{4,3,2,1,0:T(8,128)(2,1)}, bf16[2,2,2,256,1024]{4,3,2,1,0:T(8,128)(2,1)}, bf16[2,2,2,128,2048]{4,3,2,1,0:T(8,128)(2,1)}, bf16[2,2...) custom-call(bf16[4,256,1024]{2,1,0:T(8,128)(2,1)} %get-tuple-element.54.dg_hbm, ...), custom_call_target="tpu_custom_call" | custom-call | flops 21474836480 | bytes 314572800 | tf_op jit(solution)/shard_map/back/pallas_call | solution.py:1370
  407.9 20.4 %finish.1 = (f32[2048,1024]{1,0:T(8,128)}, f32[2048,1024]{1,0:T(8,128)}, f32[1024,2048]{1,0:T(8,128)}, f32[2048,256]{1,0:T(8,128)}, f32[16,2048]{1,0:T(8,128)}, ...) custom-call(bf16[2048,1024]{1,0:T(8,128)(2,1)} %bitcast.28, ...), custom_call_target="tpu_custom_call" | custom-call | bytes 48234496 | tf_op jit(solution)/shard_map/finish/pallas_call | solution.py:1479

commit v7 on v6

--- a/solution.py
+++ b/solution.py
@@ -608,9 +608,9 @@
 
 
 def middle_kernel(
-    count, g_hbm, w_hbm, cot_hbm, gain_ref, tok_ref,
-    out_hbm, dg_out, own_ref, part_ref, ggrad_ref,
-    g_s, w_s, cot_s, dy_s, gg_s, out_s, dg_s, give_s, kept_s, obuf, oslot0, oslot1, *refs,
+    count, g_hbm, w_hbm, cot_hbm, x_hbm, a_hbm, s_hbm, gain_ref, tok_ref,
+    out_hbm, da_out, ds_out, z_out, own_ref, part_ref, ggrad_ref,
+    g_s, w_s, cot_s, dy_s, gg_s, out_s, dg_s, dg_in, give_s, kept_s, obuf, oslot0, oslot1, *refs,
 ):
     slots = [refs[i * (count - 1) : (i + 1) * (count - 1)] for i in range(4)]
     load_sem, store_sem, away_sem, here_sem, send, recv = refs[4 * (count - 1) :]
@@ -652,13 +652,21 @@
     )
     loads[1].wait()
 
-    def out_store(t):
-        cols = pl.ds(pl.multiple_of(t * tile, tile), tile)
-        return pltpu.make_async_copy(out_s.at[:, :, cols], out_hbm.at[:, :, cols], store_sem.at[t])
+    out_tile = tile // 2
+
+    def out_store(t, h):
+        cols = pl.ds(pl.multiple_of(t * tile + h * out_tile, out_tile), out_tile)
+        return pltpu.make_async_copy(out_s.at[h], out_hbm.at[:, :, cols], store_sem.at[t, h])
 
     def forward(t, dots):
         cols = pl.ds(pl.multiple_of(t * tile, tile), tile)
         w_load(t).wait()
+
+        @pl.when(t >= 1)
+        def _():
+            for h in range(2):
+                out_store(t - 1, h).wait()
+
         acc = jnp.zeros((rows_num, tile), F32)
         tok = tok_ref[:, cols].astype(F32)
         new = []
@@ -667,9 +675,12 @@
                 jnp.concatenate([gg_s[j, :, lo:hi] for j in range(groups)], axis=1),
                 jnp.concatenate([w_s[j, lo:hi, cols] for j in range(groups)], axis=0),
             )
-            out_s[w, :, cols] = (tok + recips[w] * acc).astype(BF16)
+            value = (tok + recips[w] * acc).astype(BF16)
+            for h in range(2):
+                out_s[h, w] = value[:, h * out_tile : (h + 1) * out_tile]
             new.append(dots[w] + jnp.sum(cot_s[w, :, cols].astype(F32) * acc, axis=1, keepdims=True))
-        out_store(t).start()
+        for h in range(2):
+            out_store(t, h).start()
         return tuple(new)
 
     def combine(t, carry):
@@ -684,13 +695,13 @@
 
     def leave(j):
         return pltpu.make_async_remote_copy(
-            src_ref=dg_s.at[j], dst_ref=dg_out.at[me], send_sem=away_sem.at[j], recv_sem=here_sem.at[me],
+            src_ref=dg_s.at[j], dst_ref=dg_in.at[me], send_sem=away_sem.at[j], recv_sem=here_sem.at[me],
             device_id={"head": j}, device_id_type=pl.DeviceIdType.MESH,
         )
 
     def arrive(j):
         return pltpu.make_async_remote_copy(
-            src_ref=dg_s.at[j], dst_ref=dg_out.at[j], send_sem=away_sem.at[j], recv_sem=here_sem.at[j],
+            src_ref=dg_s.at[j], dst_ref=dg_in.at[j], send_sem=away_sem.at[j], recv_sem=here_sem.at[j],
             device_id={"head": j}, device_id_type=pl.DeviceIdType.MESH,
         )
 
@@ -777,8 +788,17 @@
         scale = scale + recips[w] ** 3 * dots[w] / (segs[w][1] * groups)
         scales[w] = scale
     lax.fori_loop(0, groups, back, 0)
-    stay = pltpu.make_async_copy(dg_s.at[me], dg_out.at[me], load_sem.at[0])
+    stay = pltpu.make_async_copy(dg_s.at[me], dg_in.at[me], load_sem.at[0])
     stay.start()
+    x_s, factors, z_s = w_s.at[0], w_s.at[1], w_s.at[2]
+    wide_at = [pl.ds(h * channels, channels) for h in range(2)]
+    late = [
+        pltpu.make_async_copy(x_hbm, x_s, load_sem.at[2]),
+        pltpu.make_async_copy(a_hbm, factors.at[:, wide_at[0]], load_sem.at[3]),
+        pltpu.make_async_copy(s_hbm, factors.at[:, wide_at[1]], load_sem.at[4]),
+    ]
+    for load in late:
+        load.start()
     for s in range(2, 4):
         give(s)
     advance_all(streams[:2])
@@ -791,33 +811,74 @@
             obuf[s, j] = kept_s[(s,) + own + (j,)]
     head_sum.advance()
     advance_all(streams[2:])
+
+    def taken(j, carry):
+        @pl.when(j != me)
+        def _():
+            leave(j).wait_send()
+            arrive(j).wait_recv()
+
+        return carry
+
+    lax.fori_loop(0, groups, taken, 0)
+    stay.wait()
+    for load in late:
+        load.wait()
+    length = groups * rows_num
+    rows_at = 64
+
+    def gates(i, carry):
+        per = rows_num // rows_at
+        rows = pl.ds(pl.multiple_of(i * rows_at, rows_at), rows_at)
+        d = dg_in[i // per, pl.ds(pl.multiple_of((i % per) * rows_at, rows_at), rows_at), :].astype(F32)
+        for at in wide_at:
+            factors[rows, at] = (d * factors[rows, at].astype(F32)).astype(BF16)
+        return carry
+
+    lax.fori_loop(0, length // rows_at, gates, 0)
+    stores = [
+        pltpu.make_async_copy(factors.at[:, wide_at[0]], da_out, load_sem.at[0]),
+        pltpu.make_async_copy(factors.at[:, wide_at[1]], ds_out, load_sem.at[1]),
+    ]
+    for item in stores:
+        item.start()
     head_sum.advance()
+    per_half = model // tile // 2
+
+    def z_store(t):
+        first = pl.multiple_of((t % per_half) * tile, tile)
+        cols = pl.ds(pl.multiple_of((t // per_half) * channels, channels), channels)
+        rows = pl.ds(pl.multiple_of(t * tile, tile), tile)
+        return pltpu.make_async_copy(z_s.at[pl.ds(first, tile), cols], z_out.at[rows], load_sem.at[2 + t])
+
+    def z_grad(t, carry):
+        value = mm_tn(x_s[:, pl.ds(pl.multiple_of(t * tile, tile), tile)], factors[:, wide_at[0]])
+        first = pl.multiple_of((t % per_half) * tile, tile)
+        cols = pl.ds(pl.multiple_of((t // per_half) * channels, channels), channels)
+        z_s[pl.ds(first, tile), cols] = value.astype(BF16)
+        z_store(t).start()
+        return carry
+
+    lax.fori_loop(0, tiles, z_grad, 0)
     drain(streams)
     drain([head_sum])
+    for item in stores:
+        item.wait()
+
+    def z_stored(t, carry):
+        z_store(t).wait()
+        return carry
+
+    lax.fori_loop(0, tiles, z_stored, 0)
     own_ref[...] = obuf[place(2, dict(enumerate(bits_of("head", 2))))]
     for s in range(2, 4):
         for j in range(pairs_num):
             part_ref[s - 2, j] = kept_s[(s,) + own + (j,)]
-    stay.wait()
-
-    def finish(j, carry):
-        @pl.when(j != me)
-        def _():
-            leave(j).wait_send()
-            arrive(j).wait_recv()
-
-        return carry
-
-    lax.fori_loop(0, groups, finish, 0)
-
-    def stored(t, carry):
-        out_store(t).wait()
-        return carry
-
-    lax.fori_loop(0, tiles, stored, 0)
-
-
-def middle_call(g, w_all, gain, tok, cot, batches):
+    for h in range(2):
+        out_store(tiles - 1, h).wait()
+
+
+def middle_call(g, w_all, gain, tok, cot, x, a, s, batches):
     groups, rows_num, channels = g.shape
     model = tok.shape[1]
     count = log2(batches)
@@ -832,22 +893,25 @@
     halves = pltpu.VMEM((4,) + (2,) * (count - 1) + block, BF16)
     return pl.pallas_call(
         functools.partial(middle_kernel, count),
-        in_specs=[hbm] * 3 + [vmem] * 2,
-        out_specs=[hbm, hbm, vmem, vmem, vmem],
+        in_specs=[hbm] * 6 + [vmem] * 2,
+        out_specs=[hbm] * 4 + [vmem] * 3,
         out_shape=[
             jax.ShapeDtypeStruct((4, rows_num, model), BF16),
-            jax.ShapeDtypeStruct(g.shape, BF16),
+            jax.ShapeDtypeStruct(a.shape, BF16),
+            jax.ShapeDtypeStruct(s.shape, BF16),
+            jax.ShapeDtypeStruct((model, channels), BF16),
             jax.ShapeDtypeStruct((part, half), BF16),
             jax.ShapeDtypeStruct((2, 2, part, half), BF16),
             jax.ShapeDtypeStruct((groups, 1, channels), F32),
         ],
         scratch_shapes=[
-            wide, pltpu.VMEM((groups, channels, model), BF16), tall, tall, wide, tall, wide, halves, halves,
+            wide, pltpu.VMEM((groups, channels, model), BF16), tall, tall, wide,
+            pltpu.VMEM((2, 4, rows_num, 256), BF16), wide, wide, halves, halves,
             pltpu.VMEM((2, 2, part, half), BF16), pltpu.VMEM((2, part, half), BF16), pltpu.VMEM((part, half), BF16),
         ]
         + [s for _ in range(4) for s in halving_slots(count - 1, block, BF16)]
         + [
-            dma((2 + model // 512,)), dma((model // 512,)), dma((groups,)), dma((groups,)),
+            dma((2 + model // 512,)), dma((model // 512, 2)), dma((groups,)), dma((groups,)),
             dma((4 * count + 2,)), dma((4 * count + 2,)),
         ],
         compiler_params=pltpu.CompilerParams(
@@ -857,17 +921,18 @@
             flops=6 * groups * rows_num * channels * model, bytes_accessed=200 * 2**20, transcendentals=0
         ),
         name="nested_norm",
-    )(g, w_all, cot, gain, tok)
+    )(g, w_all, cot, x, a, s, gain, tok)
 
 
 BACK_POLLS = {
     "z": ((0, 0, "a"), (0, 1, "a"), (0, 1, "b"), (0, 2, "a"), (0, 3, "a"), (0, 3, "b")),
     "out": ((0, 0, "a"), (0, 1, "a")),
-    "spread": (((0, 2, "a"), (0, 2, "b"), (0, 3, "b")), ((0, 2, "a"), (0, 2, "b"), (0, 3, "b"))),
+    "spread": (((0, 3, "b"),), ((0, 3, "b"),)),
     "relay": (
-        ((0, 1, "a"), 3, 0, 1), ((0, 1, "b"), 3, 1, 1), ((0, 2, "a"), 3, 2, 1), ((0, 2, "a"), 3, 3, 1),
-        ((0, 1, "b"), 3, 0, 2), ((0, 2, "a"), 3, 1, 2), ((0, 2, "b"), 3, 2, 2), ((0, 3, "a"), 3, 3, 2),
-        ((0, 2, "b"), 2, 0, 1), ((0, 3, "a"), 2, 1, 1), ((0, 3, "b"), 2, 2, 1),
+        ((0, 1, "a"), 3, 0, 1), ((0, 1, "b"), 3, 1, 1), ((0, 1, "b"), 3, 2, 1), ((0, 2, "a"), 3, 3, 1),
+        ((0, 1, "b"), 3, 0, 2), ((0, 2, "a"), 3, 1, 2), ((0, 2, "a"), 3, 2, 2), ((0, 2, "b"), 3, 3, 2),
+        ((0, 2, "b"), 2, 0, 1), ((0, 2, "b"), 2, 1, 1), ((0, 3, "a"), 2, 2, 1), ((0, 3, "b"), 2, 3, 1),
+        ((0, 3, "b"), 1, 0, 1),
     ),
     "tail": (1, 1, 2, 2),
 }
@@ -877,7 +942,7 @@
 
 def back_kernel(
     count, group_bits,
-    dg_hbm, a_hbm, s_hbm, act_hbm, dsc_hbm, inn_hbm, x_hbm, bc_hbm, step_hbm, prev_hbm,
+    zg_hbm, a_hbm, s_hbm, act_hbm, dsc_hbm, inn_hbm, x_hbm, bc_hbm, step_hbm, prev_hbm,
     zw_hbm, xw_hbm, bcw_hbm, dtw_hbm, o_hbm, own_hbm, gain_ref, convw_ref, alog_ref, skip_ref,
     z_out, x_out, o_out, bc_out, small_out, own_out,
     dg, a, s, act, dsc, inn, x, bc, step, prev, zw, xw, bdw, dtw, obuf, o_first, hot_ref, pad_s,
@@ -903,29 +968,13 @@
     me = lax.axis_index("head")
 
     pairs = [
-        (dg_hbm.at[:, :, pl.ds(0, channels // 2)], dg.at[0]),
-        (dg_hbm.at[:, :, pl.ds(channels // 2, channels // 2)], dg.at[1]), (a_hbm, a), (s_hbm, s), (x_hbm, x), (o_hbm, obuf), (own_hbm, o_first), (step_hbm, step), (bc_hbm, bc),
-        (prev_hbm, prev), (act_hbm, act), (dsc_hbm, dsc), (inn_hbm, inn), (zw_hbm, zw), (xw_hbm, xw),
-        (bcw_hbm, bdw.at[:, pl.ds(0, 2 * n)]), (dtw_hbm, dtw),
+        (zg_hbm, zg), (o_hbm, obuf), (own_hbm, o_first), (step_hbm, step), (bc_hbm, bc), (prev_hbm, prev),
+        (s_hbm, s), (act_hbm, act), (dsc_hbm, dsc), (inn_hbm, inn), (a_hbm, a), (zw_hbm, zw), (xw_hbm, xw),
+        (x_hbm, x), (bcw_hbm, bdw.at[:, pl.ds(0, 2 * n)]), (dtw_hbm, dtw),
     ]
     loads = [pltpu.make_async_copy(src, dst, load_sem.at[i]) for i, (src, dst) in enumerate(pairs)]
     for load in loads:
         load.start()
-    for load in loads[:4]:
-        load.wait()
-
-    def gates(i, carry):
-        per = rows_num // 64
-        rows = pl.ds(pl.multiple_of(i * 64, 64), 64)
-        piece = dg.shape[-1]
-        for h in range(dg.shape[0]):
-            cols = slice(h * piece, (h + 1) * piece)
-            d = dg[h, i // per, pl.ds(pl.multiple_of((i % per) * 64, 64), 64), :].astype(F32)
-            a[rows, cols] = (d * a[rows, cols].astype(F32)).astype(BF16)
-            s[rows, cols] = (d * s[rows, cols].astype(F32)).astype(BF16)
-        return carry
-
-    lax.fori_loop(0, length // 64, gates, 0)
     near, far = partner("head", 0), partner("head", 1)
     meet(
         [("batch", partner("batch", b)) for b in range(count)]
@@ -999,7 +1048,9 @@
         for i in range(2)
     ]
 
-    for load in loads[4:7]:
+    loads[0].wait()
+    advance_all(streams[:2])
+    for load in loads[1:3]:
         load.wait()
     outs.advance()
     tile = 256
@@ -1024,11 +1075,14 @@
 
         lax.fori_loop(0, model // (2 * tile), one, 0)
 
-    weight_grad(a, zg)
-    advance_all(streams[:2])
-    for load in loads[7:]:
+    for load in loads[3:10]:
         load.wait()
-    bdw[:, 2 * n :] = jnp.concatenate([dtw[...], jnp.zeros((128 - heads, model), BF16)], axis=0).T
+
+    def late_loads():
+        for load in loads[10:]:
+            load.wait()
+        bdw[:, 2 * n :] = jnp.concatenate([dtw[...], jnp.zeros((128 - heads, model), BF16)], axis=0).T
+
     pad_s[...] = jnp.zeros_like(pad_s)
     pad_s[0:1, 0:heads] = alog_ref[...]
     hot_ref[...] = (
@@ -1238,6 +1292,7 @@
             if stream.steps:
                 plan[slot].append(stream.steps.pop(0))
 
+    plan[0, 0, "a"].append(late_loads)
     for st in streams[:2]:
         book(st, BACK_POLLS["z"])
     book(outs, BACK_POLLS["out"])
@@ -1349,7 +1404,7 @@
                 hop(q, c, slot(q, c), rrecv.at[q, c], me).wait_send()
 
 
-def back_call(dg, res, x, bc, step, prev, zw, xw, bcw, dtw, out_part, out_own, gain_grad, convw, alog, skip, groups, batches):
+def back_call(z_grad, res, x, bc, step, prev, zw, xw, bcw, dtw, out_part, out_own, gain_grad, convw, alog, skip, groups, batches):
     length, model = x.shape
     channels = xw.shape[1]
     n = bc.shape[1] // 2
@@ -1417,7 +1472,7 @@
         ),
         name="back",
     )(
-        dg, *res, x, bc, step, prev, zw, xw, bcw, dtw, out_part, out_own,
+        z_grad.reshape(lead + (rows, channels)), *res, x, bc, step, prev, zw, xw, bcw, dtw, out_part, out_own,
         gain_grad, convw, alog, skip,
     )
     return (
@@ -1517,9 +1572,11 @@
         tokens, pre_gain, z_weight, x_weight, bc_weight, dtw, out_weight, norm_gain,
         conv_weight, conv_bias[None], dt_bias[None], alog, skip_r, groups, batches,
     )
-    outputs, d_gated, out_own, out_part, gain_grad = middle_call(gated, w_all, gain_all, tokens, cot, batches)
+    outputs, d_gate, d_scanned, z_grad, out_own, out_part, gain_grad = middle_call(
+        gated, w_all, gain_all, tokens, cot, x, res[0], res[1], batches
+    )
     z_grad, x_grad, out_grad, bcdt_grad, small, d_own = back_call(
-        d_gated, res, x, bc, step, prev, z_weight, x_weight, bc_weight, dtw, out_part, out_own, gain_grad,
+        z_grad, (d_gate, d_scanned) + res[2:], x, bc, step, prev, z_weight, x_weight, bc_weight, dtw, out_part, out_own, gain_grad,
         conv_weight, alog, skip_r, groups, batches,
     )
     (

time: 429 us -> 430 us (level)
  no operation moved by 1% of the time
where the time goes in v7:
time: 430 us; the launch traced here: 429 us
  Pallas kernels  428 us (100%)
    pallas_call x1, Pallas kernels, back_call(): pl.pallas_call(functools.partial(back_kernel, count, group_bits), in_spec...  151 us
    pallas_call x1, Pallas kernels, front_call(): pl.pallas_call(functools.partial(front_kernel, count), in_specs=[vmem, vm...  151 us
    pallas_call x1, Pallas kernels, middle_call(): pl.pallas_call(functools.partial(middle_kernel, count), in_specs=[hbm] *...  106 us
    pallas_call x1, Pallas kernels, finish_call(): pl.pallas_call(finish_kernel, grid=(steps,), in_specs=[rows(model, channe...  20.4 us

profile of v7, /device:TPU:0, one launch (start us, length us, event | category | flops | bytes accessed | tf_op | source)
XLA Modules:
  0.0 429.3 jit_solution(16295508082846746230)
XLA Ops:
  0.6 150.9 %front.1 = (bf16[1024,2048]{1,0:T(8,128)(2,1)}, bf16[1024,1024]{1,0:T(8,128)(2,1)}, bf16[1024,1024]{1,0:T(8,128)(2,1)}, bf16[1024,1024]{1,0:T(8,128)(2,1)}, bf16...) custom-call(bf16[256,2048]{1,0:T(8,128)(2,1)} %bitcast.33, ...), custom_call_target="tpu_custom_call" | custom-call | flops 8589934592 | bytes 419430400 | tf_op jit(solution)/shard_map/front/pallas_call | solution.py:571
  151.5 105.8 %nested_norm.1 = (bf16[4,256,2048]{2,1,0:T(8,128)(2,1)}, bf16[1024,1024]{1,0:T(8,128)(2,1)}, bf16[1024,1024]{1,0:T(8,128)(2,1)}, bf16[2048,1024]{1,0:T(8,128)(2,...) custom-call(bf16[4,256,1024]{2,1,0:T(8,128)(2,1)} %get-tuple-element.53.g_hbm, ...), custom_call_target="tpu_custom_call" | custom-call | flops 12884901888 | bytes 209715200 | tf_op jit(solution)/shard_map/nested_norm/pallas_call | solution.py:894
  257.3 151.4 %back.1 = (bf16[2,2,2,256,1024]{4,3,2,1,0:T(8,128)(2,1)}, bf16[2,2,2,256,1024]{4,3,2,1,0:T(8,128)(2,1)}, bf16[2,2,2,128,2048]{4,3,2,1,0:T(8,128)(2,1)}, bf16[2,2...) custom-call(bf16[2,2,2,256,1024]{4,3,2,1,0:T(8,128)(2,1)} %bitcast.58, ...), custom_call_target="tpu_custom_call" | custom-call | flops 21474836480 | bytes 314572800 | tf_op jit(solution)/shard_map/back/pallas_call | solution.py:1425
  408.7 20.4 %finish.1 = (f32[2048,1024]{1,0:T(8,128)}, f32[2048,1024]{1,0:T(8,128)}, f32[1024,2048]{1,0:T(8,128)}, f32[2048,256]{1,0:T(8,128)}, f32[16,2048]{1,0:T(8,128)}, ...) custom-call(bf16[2048,1024]{1,0:T(8,128)(2,1)} %bitcast.29, ...), custom_call_target="tpu_custom_call" | custom-call | bytes 48234496 | tf_op jit(solution)/shard_map/finish/pallas_call | solution.py:1534

commit v8 on v6

--- a/solution.py
+++ b/solution.py
@@ -863,11 +863,12 @@
 BACK_POLLS = {
     "z": ((0, 0, "a"), (0, 1, "a"), (0, 1, "b"), (0, 2, "a"), (0, 3, "a"), (0, 3, "b")),
     "out": ((0, 0, "a"), (0, 1, "a")),
-    "spread": (((0, 2, "a"), (0, 2, "b"), (0, 3, "b")), ((0, 2, "a"), (0, 2, "b"), (0, 3, "b"))),
+    "spread": (((0, 3, "b"),), ((0, 3, "b"),)),
     "relay": (
-        ((0, 1, "a"), 3, 0, 1), ((0, 1, "b"), 3, 1, 1), ((0, 2, "a"), 3, 2, 1), ((0, 2, "a"), 3, 3, 1),
-        ((0, 1, "b"), 3, 0, 2), ((0, 2, "a"), 3, 1, 2), ((0, 2, "b"), 3, 2, 2), ((0, 3, "a"), 3, 3, 2),
-        ((0, 2, "b"), 2, 0, 1), ((0, 3, "a"), 2, 1, 1), ((0, 3, "b"), 2, 2, 1),
+        ((0, 1, "a"), 3, 0, 1), ((0, 1, "b"), 3, 1, 1), ((0, 1, "b"), 3, 2, 1), ((0, 2, "a"), 3, 3, 1),
+        ((0, 1, "b"), 3, 0, 2), ((0, 2, "a"), 3, 1, 2), ((0, 2, "a"), 3, 2, 2), ((0, 2, "b"), 3, 3, 2),
+        ((0, 2, "b"), 2, 0, 1), ((0, 2, "b"), 2, 1, 1), ((0, 3, "a"), 2, 2, 1), ((0, 3, "b"), 2, 3, 1),
+        ((0, 3, "b"), 1, 0, 1),
     ),
     "tail": (1, 1, 2, 2),
 }

time: 429 us -> 425 us (level)
  Pallas kernels: 428 us -> 421 us
    pallas_call x1, Pallas kernels: 153 us -> 147 us  [back_call(): pl.pallas_call(functools.partial(back_kernel, count, group_bits), in_spec...]
where the time goes in v8:
time: 425 us; the launch traced here: 422 us
  Pallas kernels  421 us (99%)
    pallas_call x1, Pallas kernels, front_call(): pl.pallas_call(functools.partial(front_kernel, count), in_specs=[vmem, vm...  151 us
    pallas_call x1, Pallas kernels, back_call(): pl.pallas_call(functools.partial(back_kernel, count, group_bits), in_spec...  147 us
    pallas_call x1, Pallas kernels, middle_call(): pl.pallas_call(functools.partial(middle_kernel, count), in_specs=[hbm] *...  103 us
    pallas_call x1, Pallas kernels, finish_call(): pl.pallas_call(finish_kernel, grid=(steps,), in_specs=[rows(model, channe...  20.4 us

profile of v8, /device:TPU:0, one launch (start us, length us, event | category | flops | bytes accessed | tf_op | source)
XLA Modules:
  0.0 422.2 jit_solution(10507866214453021015)
XLA Ops:
  0.6 150.9 %front.1 = (bf16[1024,2048]{1,0:T(8,128)(2,1)}, bf16[1024,1024]{1,0:T(8,128)(2,1)}, bf16[1024,1024]{1,0:T(8,128)(2,1)}, bf16[1024,1024]{1,0:T(8,128)(2,1)}, bf16...) custom-call(bf16[256,2048]{1,0:T(8,128)(2,1)} %bitcast.32, ...), custom_call_target="tpu_custom_call" | custom-call | flops 8589934592 | bytes 419430400 | tf_op jit(solution)/shard_map/front/pallas_call | solution.py:571
  151.5 103.0 %nested_norm.1 = (bf16[4,256,2048]{2,1,0:T(8,128)(2,1)}, bf16[4,256,1024]{2,1,0:T(8,128)(2,1)}, bf16[128,1024]{1,0:T(8,128)(2,1)}, bf16[2,2,128,1024]{3,2,1,0:T(8,128)(2,1)}, f32[4,1,1024]{2,1,0:T(1,128)}) custom-call(bf16[4,256,1024]{2,1,0:T(8,128)(2,1)} %get-tuple-element.51.g_hbm, bf16[4,1024,2048]{2,1,0:T(8,128)(2,1)} %bitcast.56, ...), custom_call_target="tpu_custom_call" | custom-call | flops 12884901888 | bytes 209715200 | tf_op jit(solution)/shard_map/nested_norm/pallas_call | solution.py:833
  254.6 147.1 %back.1 = (bf16[2,2,2,256,1024]{4,3,2,1,0:T(8,128)(2,1)}, bf16[2,2,2,256,1024]{4,3,2,1,0:T(8,128)(2,1)}, bf16[2,2,2,128,2048]{4,3,2,1,0:T(8,128)(2,1)}, bf16[2,2...) custom-call(bf16[4,256,1024]{2,1,0:T(8,128)(2,1)} %get-tuple-element.54.dg_hbm, ...), custom_call_target="tpu_custom_call" | custom-call | flops 21474836480 | bytes 314572800 | tf_op jit(solution)/shard_map/back/pallas_call | solution.py:1371
  401.6 20.4 %finish.1 = (f32[2048,1024]{1,0:T(8,128)}, f32[2048,1024]{1,0:T(8,128)}, f32[1024,2048]{1,0:T(8,128)}, f32[2048,256]{1,0:T(8,128)}, f32[16,2048]{1,0:T(8,128)}, ...) custom-call(bf16[2048,1024]{1,0:T(8,128)(2,1)} %bitcast.28, ...), custom_call_target="tpu_custom_call" | custom-call | bytes 48234496 | tf_op jit(solution)/shard_map/finish/pallas_call | solution.py:1480

commit v9 on v8

--- a/solution.py
+++ b/solution.py
@@ -609,7 +609,7 @@
 
 def middle_kernel(
     count, g_hbm, w_hbm, cot_hbm, gain_ref, tok_ref,
-    out_hbm, dg_out, own_ref, part_ref, ggrad_ref,
+    out_hbm, dg_out, passed_hbm, own_ref, part_ref, ggrad_ref,
     g_s, w_s, cot_s, dy_s, gg_s, out_s, dg_s, give_s, kept_s, obuf, oslot0, oslot1, *refs,
 ):
     slots = [refs[i * (count - 1) : (i + 1) * (count - 1)] for i in range(4)]
@@ -670,6 +670,7 @@
             out_s[w, :, cols] = (tok + recips[w] * acc).astype(BF16)
             new.append(dots[w] + jnp.sum(cot_s[w, :, cols].astype(F32) * acc, axis=1, keepdims=True))
         out_store(t).start()
+        cot_s[0, :, cols] = sum(cot_s[w, :, cols].astype(F32) for w in range(4)).astype(BF16)
         return tuple(new)
 
     def combine(t, carry):
@@ -779,6 +780,8 @@
     lax.fori_loop(0, groups, back, 0)
     stay = pltpu.make_async_copy(dg_s.at[me], dg_out.at[me], load_sem.at[0])
     stay.start()
+    pass_on = pltpu.make_async_copy(cot_s.at[0], passed_hbm, load_sem.at[1])
+    pass_on.start()
     for s in range(2, 4):
         give(s)
     advance_all(streams[:2])
@@ -799,6 +802,7 @@
         for j in range(pairs_num):
             part_ref[s - 2, j] = kept_s[(s,) + own + (j,)]
     stay.wait()
+    pass_on.wait()
 
     def finish(j, carry):
         @pl.when(j != me)
@@ -833,10 +837,11 @@
     return pl.pallas_call(
         functools.partial(middle_kernel, count),
         in_specs=[hbm] * 3 + [vmem] * 2,
-        out_specs=[hbm, hbm, vmem, vmem, vmem],
+        out_specs=[hbm, hbm, hbm, vmem, vmem, vmem],
         out_shape=[
             jax.ShapeDtypeStruct((4, rows_num, model), BF16),
             jax.ShapeDtypeStruct(g.shape, BF16),
+            jax.ShapeDtypeStruct((rows_num, model), BF16),
             jax.ShapeDtypeStruct((part, half), BF16),
             jax.ShapeDtypeStruct((2, 2, part, half), BF16),
             jax.ShapeDtypeStruct((groups, 1, channels), F32),
@@ -1340,7 +1345,7 @@
                         value += last_s[c, rs, :].astype(F32)
                     if q < top:
                         value += slot(q, c)[rs, :].astype(F32)
-                    own_out[rs, c * piece : (c + 1) * piece] = value
+                    own_out[rs, c * piece : (c + 1) * piece] = value.astype(BF16)
                     return carry
 
                 lax.fori_loop(0, rows_num // 32, total, 0)
@@ -1378,7 +1383,7 @@
             jax.ShapeDtypeStruct(lead + (part, model), BF16),
             jax.ShapeDtypeStruct(lead + (rows, wide), BF16),
             jax.ShapeDtypeStruct((16, channels), F32),
-            jax.ShapeDtypeStruct((rows_num, model), F32),
+            jax.ShapeDtypeStruct((rows_num, model), BF16),
         ],
         scratch_shapes=[pltpu.VMEM((2, groups, rows_num, channels // 2), BF16)] + [tall(channels, BF16)] * 5
         + [
@@ -1428,7 +1433,7 @@
 
 
 def finish_kernel(
-    z_ref, x_ref, o_ref, bc_ref, small_ref, own_ref, tok_ref, cot_ref, pre_ref, out_ref,
+    z_ref, x_ref, o_ref, bc_ref, small_ref, own_ref, tok_ref, passed_ref, pre_ref, out_ref,
     zf_ref, xf_ref, of_ref, bcf_ref, dt_ref, grad_ref, outf_ref, convw_ref, convb_ref, skip_ref, gain_ref, pre_out, dtb_ref, alog_ref,
 ):
     zf_ref[...] = z_ref[...].astype(F32)
@@ -1441,10 +1446,9 @@
     dt_ref[...] = bc_ref[:, width : width + 128].astype(F32).T[:heads]
     tok = tok_ref[...].astype(F32)
     recip = lax.rsqrt(jnp.mean(tok * tok, axis=-1, keepdims=True) + EPSILON)
-    scaled = pre_ref[...] * own_ref[...]
+    scaled = pre_ref[...] * own_ref[...].astype(F32)
     mean = jnp.mean(tok * scaled, axis=-1, keepdims=True)
-    passed = sum(cot_ref[w].astype(F32) for w in range(4))
-    grad_ref[...] = (passed + recip * scaled - tok * recip**3 * mean).astype(BF16)
+    grad_ref[...] = (passed_ref[...].astype(F32) + recip * scaled - tok * recip**3 * mean).astype(BF16)
 
     @pl.when(pl.program_id(0) == 0)
     def _():
@@ -1465,7 +1469,7 @@
         alog_ref[...] = small_ref[14:15, heads : 2 * heads]
 
 
-def finish_call(z, x, o, bc, small, own, tok, cot, pre_gain, out, heads):
+def finish_call(z, x, o, bc, small, own, tok, passed, pre_gain, out, heads):
     model, channels = z.shape
     rows_num = tok.shape[0]
     steps = 8
@@ -1483,7 +1487,7 @@
         in_specs=[
             rows(model, channels), rows(model, channels), rows(channels, model), rows(model, wide),
             fixed(small.shape), rows(rows_num, model), rows(rows_num, model),
-            wide4, fixed((1, model)), wide4,
+            rows(rows_num, model), fixed((1, model)), wide4,
         ],
         out_specs=[rows(*shape) for shape, _ in shapes]
         + [pl.BlockSpec((heads, model // steps), lambda i: (0, i)), rows(rows_num, model), wide4]
@@ -1497,7 +1501,7 @@
         compiler_params=pltpu.CompilerParams(vmem_limit_bytes=VMEM_BYTES),
         cost_estimate=pl.CostEstimate(flops=0, bytes_accessed=46 * 2**20, transcendentals=0),
         name="finish",
-    )(z, x, o, bc, small, own, tok, cot, pre_gain[None], out)
+    )(z, x, o, bc, small, own, tok, passed, pre_gain[None], out)
 
 
 def per_device(
@@ -1518,14 +1522,14 @@
         tokens, pre_gain, z_weight, x_weight, bc_weight, dtw, out_weight, norm_gain,
         conv_weight, conv_bias[None], dt_bias[None], alog, skip_r, groups, batches,
     )
-    outputs, d_gated, out_own, out_part, gain_grad = middle_call(gated, w_all, gain_all, tokens, cot, batches)
+    outputs, d_gated, passed, out_own, out_part, gain_grad = middle_call(gated, w_all, gain_all, tokens, cot, batches)
     z_grad, x_grad, out_grad, bcdt_grad, small, d_own = back_call(
         d_gated, res, x, bc, step, prev, z_weight, x_weight, bc_weight, dtw, out_part, out_own, gain_grad,
         conv_weight, alog, skip_r, groups, batches,
     )
     (
         z_grad, x_grad, out_grad, bc_grad, dt_grad, tokens_grad, outputs, convw, convb, skip_g, gain_g, pre_g, dtb_g, alog_g,
-    ) = finish_call(z_grad, x_grad, out_grad, bcdt_grad, small, d_own, tokens, cot, pre_gain, outputs, heads)
+    ) = finish_call(z_grad, x_grad, out_grad, bcdt_grad, small, d_own, tokens, passed, pre_gain, outputs, heads)
     flat = lambda v: v.reshape(-1)
     return (
         outputs[:, None], tokens_grad[None], z_grad, x_grad, bc_grad, dt_grad.T, convw, flat(convb), flat(dtb_g),

time: 425 us -> 427 us (level)
  no operation moved by 1% of the time
where the time goes in v9:
time: 427 us; the launch traced here: 423 us
  Pallas kernels  422 us (99%)
    pallas_call x1, Pallas kernels, front_call(): pl.pallas_call(functools.partial(front_kernel, count), in_specs=[vmem, vm...  151 us
    pallas_call x1, Pallas kernels, back_call(): pl.pallas_call(functools.partial(back_kernel, count, group_bits), in_spec...  148 us
    pallas_call x1, Pallas kernels, middle_call(): pl.pallas_call(functools.partial(middle_kernel, count), in_specs=[hbm] *...  103 us
    pallas_call x1, Pallas kernels, finish_call(): pl.pallas_call(finish_kernel, grid=(steps,), in_specs=[rows(model, channe...  20 us

profile of v9, /device:TPU:0, one launch (start us, length us, event | category | flops | bytes accessed | tf_op | source)
XLA Modules:
  0.0 422.8 jit_solution(16816403010285362136)
XLA Ops:
  0.6 150.9 %front.1 = (bf16[1024,2048]{1,0:T(8,128)(2,1)}, bf16[1024,1024]{1,0:T(8,128)(2,1)}, bf16[1024,1024]{1,0:T(8,128)(2,1)}, bf16[1024,1024]{1,0:T(8,128)(2,1)}, bf16...) custom-call(bf16[256,2048]{1,0:T(8,128)(2,1)} %bitcast.30, ...), custom_call_target="tpu_custom_call" | custom-call | flops 8589934592 | bytes 419430400 | tf_op jit(solution)/shard_map/front/pallas_call | solution.py:571
  151.5 103.3 %nested_norm.1 = (bf16[4,256,2048]{2,1,0:T(8,128)(2,1)}, bf16[4,256,1024]{2,1,0:T(8,128)(2,1)}, bf16[256,2048]{1,0:T(8,128)(2,1)}, bf16[128,1024]{1,0:T(8,128)(2...) custom-call(bf16[4,256,1024]{2,1,0:T(8,128)(2,1)} %get-tuple-element.52.g_hbm, ...), custom_call_target="tpu_custom_call" | custom-call | flops 12884901888 | bytes 209715200 | tf_op jit(solution)/shard_map/nested_norm/pallas_call | solution.py:837
  254.9 147.8 %back.1 = (bf16[2,2,2,256,1024]{4,3,2,1,0:T(8,128)(2,1)}, bf16[2,2,2,256,1024]{4,3,2,1,0:T(8,128)(2,1)}, bf16[2,2,2,128,2048]{4,3,2,1,0:T(8,128)(2,1)}, bf16[2,2...) custom-call(bf16[4,256,1024]{2,1,0:T(8,128)(2,1)} %get-tuple-element.55.dg_hbm, ...), custom_call_target="tpu_custom_call" | custom-call | flops 21474836480 | bytes 314572800 | tf_op jit(solution)/shard_map/back/pallas_call | solution.py:1376
  402.6 20.0 %finish.1 = (f32[2048,1024]{1,0:T(8,128)}, f32[2048,1024]{1,0:T(8,128)}, f32[1024,2048]{1,0:T(8,128)}, f32[2048,256]{1,0:T(8,128)}, f32[16,2048]{1,0:T(8,128)}, ...) custom-call(bf16[2048,1024]{1,0:T(8,128)(2,1)} %bitcast.26, ...), custom_call_target="tpu_custom_call" | custom-call | bytes 48234496 | tf_op jit(solution)/shard_map/finish/pallas_call | solution.py:1484
